TPU v7x, 32 devices: a whole 2x2x4 slice. The times are simulated.
32 devices in a mesh: dp: 8 (over z, y), seq: 4 (over x, core).
Axes of the slice: x: 2, y: 2, z: 4, core: 2. Of those that a mesh axis runs over, the one named last changes fastest.
Arguments:
- inputs: float32 [8, 1024, 2048], P('dp', 'seq'), may hold values from -6 to 6
- segments: int32 [8, 1024], P('dp', 'seq'), may hold values from 0 to 31, as said below
- valid_count: int32 [8], P('dp'), may hold values from 512 to 1024
- teacher: float32 [8, 1024, 2048], P('dp', 'seq'), may hold values from -6 to 6
- cotangent: float32 [8, 1024, 2048], P('dp', 'seq'), may hold values from -6 to 6
- w_proj: bfloat16 [2048, 8192], P('dp'), may hold values from -0.125 to 0.125
- w_decay: bfloat16 [2048, 16], P('dp'), may hold values from -0.25 to 0.25
- b_decay: float32 [16], replicated, may hold values from 1 to 5
- w_out: bfloat16 [2048, 2048], P('dp'), may hold values from -0.125 to 0.125
- gain_ret: float32 [2048], replicated, may hold values from 0.5 to 1.5
- gain_ffn: float32 [2048], replicated, may hold values from 0.5 to 1.5
- w_gu: bfloat16 [2048, 11008], P('dp'), may hold values from -0.125 to 0.125
- w_down: bfloat16 [5504, 2048], P('dp'), may hold values from -0.078125 to 0.078125
Outputs:
- output: float32 [8, 1024, 2048], P('dp', 'seq')
- grad_inputs: float32 [8, 1024, 2048], P('dp', 'seq')
- grad_w_proj: float32 [2048, 8192], P('dp')
- grad_w_decay: float32 [2048, 16], P('dp')
- grad_b_decay: float32 [16], replicated
- grad_w_out: float32 [2048, 2048], P('dp')
- grad_gain_ret: float32 [2048], replicated
- grad_gain_ffn: float32 [2048], replicated
- grad_w_gu: float32 [2048, 11008], P('dp')
- grad_w_down: float32 [5504, 2048], P('dp')
- mse: float32 [], replicated
Inputs may be any that keep to these rules, and one draw needn't show every extreme that they name: `segments`: within a row the numbers never fall and each number is one run of positions; different rows use different numbers.
All inputs are finite; a program needn't handle non-finite values.
Results may differ from a plain program's by a relative error of at most 0.018.
Values may be sent and summed in bfloat16 or wider, within the bound.
A program may use at most 448 MiB of HBM per device.

v0:
```python
import jax
import jax.numpy as jnp
from jax import lax
from jax.sharding import PartitionSpec as P

HIGHEST_PRECISION = lax.Precision.HIGHEST


def carried_in(value, axis, join, neutral):
    count, mine = (lax.axis_size(axis), lax.axis_index(axis))
    pieces = jax.tree.map(lambda part: lax.all_gather(part, axis), value)
    total = jax.tree.map(
        lambda part, zero: jnp.full_like(part, 0) + jnp.asarray(zero, part.dtype), value, neutral
    )

    def lap(position, total):
        longer = join(total, jax.tree.map(lambda part: part[position], pieces))
        return jax.tree.map(lambda new, old: jnp.where(position < mine, new, old), longer, total)

    return lax.fori_loop(0, count - 1, lap, total)


def carried_in_2(value, axis, combine, identity):
    peers, place = (lax.axis_size(axis), lax.axis_index(axis))
    everything = jax.tree.map(
        lambda part, kind: lax.all_gather(part.astype(kind), axis),
        value,
        jax.tree.map(lambda a: jnp.bfloat16 if a.dtype == jnp.float32 else a.dtype, value),
    )
    start = jax.tree.map(
        lambda part, zero: jnp.broadcast_to(jnp.asarray(zero, part.dtype), part.shape),
        value,
        identity,
    )

    def lap(k, before):
        at = peers - 1 - k
        reached = at > place
        new = combine(
            before, jax.tree.map(lambda part, own: part[at].astype(own.dtype), everything, value)
        )
        return jax.tree.map(lambda a, b: jnp.where(reached, a, b), new, before)

    return lax.fori_loop(0, peers, lap, start)


def contract(left, right, left_dim, right_dim):
    return lax.dot_general(
        left, right, (((left_dim,), (right_dim,)), ((), ())), preferred_element_type=jnp.float32
    )


def heads_first(matrix, head_count):
    return matrix.reshape(matrix.shape[0], head_count, -1).transpose(1, 0, 2)


def tokens_first(tensor):
    return tensor.transpose(1, 0, 2).reshape(tensor.shape[1], -1)


def decay_table(cumulative, allowed):
    spread = cumulative[:, :, None] - cumulative[:, None, :]
    return jnp.where(allowed[None], jnp.exp(jnp.where(allowed[None], spread, 0.0)), 0.0)


def retain(queries, key_rows, values, cumulative, entering, same_first, allowed):
    scores = jnp.einsum(
        "htd,hsd->hts", queries, key_rows, precision=HIGHEST_PRECISION
    ) * decay_table(cumulative, allowed)
    result = jnp.einsum("hts,hse->hte", scores, values, precision=HIGHEST_PRECISION)
    inflow = jnp.exp(cumulative) * same_first[None, :]
    carried = jnp.einsum("htd,hde->hte", queries, entering, precision=HIGHEST_PRECISION)
    return result + carried * inflow[:, :, None]


def tail_state(key_rows, values, cumulative, same_last):
    outflow = jnp.exp(cumulative[:, -1:] - cumulative) * same_last[None, :]
    return jnp.einsum(
        "htd,hte->hde", key_rows * outflow[:, :, None], values, precision=HIGHEST_PRECISION
    )


def finish(merged, outgate, head_count):
    count = merged.shape[0]
    per_head = merged.reshape(count, head_count, -1)
    normal = per_head * lax.rsqrt(
        jnp.maximum(jnp.mean(per_head * per_head, axis=2, keepdims=True), 1.0)
    )
    return jax.nn.silu(outgate) * normal.reshape(count, -1)


def norm_back(grad_normed, source, inverse, gain):
    grad_gain = jnp.sum(grad_normed * source * inverse, axis=0)
    scaled = grad_normed * gain
    grad_source = inverse * (
        scaled - source * inverse * inverse * jnp.mean(scaled * source, axis=1, keepdims=True)
    )
    return (grad_source, grad_gain)


def match_factor(left_last, right_first, left_live, right_live):
    both_live = left_live * right_live
    return jnp.where(left_last == right_first, 1.0, 0.0) * both_live + (1.0 - both_live)


def join_forward(earlier, later):
    live_early, first_early, last_early, pass_early, state_early = earlier
    live_late, first_late, last_late, pass_late, state_late = later
    linked = match_factor(last_early, first_late, live_early, live_late)
    return (
        jnp.maximum(live_early, live_late),
        jnp.where(live_early > 0, first_early, first_late),
        jnp.where(live_late > 0, last_late, last_early),
        pass_early * pass_late * linked,
        (pass_late * linked)[:, None, None] * state_early + state_late,
    )


def join_backward(earlier, later):
    live_high, first_high, last_high, pass_high, grad_high = earlier
    live_lower, first_lower, last_lower, pass_lower, grad_lower = later
    linked = match_factor(last_lower, first_high, live_lower, live_high)
    return (
        jnp.maximum(live_high, live_lower),
        jnp.where(live_lower > 0, first_lower, first_high),
        jnp.where(live_high > 0, last_high, last_lower),
        pass_lower * pass_high * linked,
        grad_lower + (pass_lower * linked)[:, None, None] * grad_high,
    )


def shards(
    inputs,
    segments,
    valid_count,
    teacher,
    cotangent,
    w_proj,
    w_decay,
    b_decay,
    w_out,
    gain_ret,
    gain_ffn,
    w_gu,
    w_down,
):
    tokens = inputs[0]
    row_segments = segments[0]
    row_count = tokens.shape[0]
    model_width = tokens.shape[1]
    head_count = w_decay.shape[1]
    head_dim = model_width // head_count
    proj_w, decay_w, out_w = (
        lax.all_gather(w_proj, "dp", axis=0, tiled=True),
        lax.all_gather(w_decay, "dp", axis=0, tiled=True),
        lax.all_gather(w_out, "dp", axis=0, tiled=True),
    )
    scale_one = lax.rsqrt(jnp.mean(tokens * tokens, axis=1, keepdims=True) + 1e-06)
    normed = (tokens * scale_one * gain_ret).astype(jnp.bfloat16)
    projected = jnp.dot(normed, proj_w, preferred_element_type=jnp.float32)
    queries = heads_first(
        (projected[:, :model_width] * head_dim ** (-0.5)).astype(jnp.bfloat16).astype(jnp.float32),
        head_count,
    )
    key_rows = heads_first(
        projected[:, model_width : 2 * model_width].astype(jnp.bfloat16).astype(jnp.float32),
        head_count,
    )
    values = heads_first(
        projected[:, 2 * model_width : 3 * model_width].astype(jnp.bfloat16).astype(jnp.float32),
        head_count,
    )
    outgate = projected[:, 3 * model_width :]
    decay_logit = jnp.dot(normed, decay_w, preferred_element_type=jnp.float32) + b_decay
    logdecay = jax.nn.log_sigmoid(decay_logit) / 16.0
    same_first = (row_segments == row_segments[0]).astype(jnp.float32)
    same_last = (row_segments == row_segments[-1]).astype(jnp.float32)
    order = jnp.arange(row_count, dtype=jnp.int32)
    allowed = (row_segments[:, None] == row_segments[None, :]) & (order[:, None] >= order[None, :])
    cumulative = jnp.cumsum(logdecay, axis=0).T
    through = jnp.exp(cumulative[:, -1]) * same_first[-1]
    own_state = tail_state(key_rows, values, cumulative, same_last)
    first_id = row_segments[0].astype(jnp.float32)
    last_id = row_segments[-1].astype(jnp.float32)
    live_one = jnp.ones((), jnp.float32)
    identity = (
        jnp.zeros((), jnp.float32),
        jnp.zeros((), jnp.float32),
        jnp.zeros((), jnp.float32),
        jnp.ones((head_count,), jnp.float32),
        jnp.zeros_like(own_state),
    )
    before = carried_in(
        (live_one, first_id, last_id, through, own_state), "seq", join_forward, identity
    )
    entering = before[4] * jnp.where(before[2] == first_id, 1.0, 0.0)
    retained = retain(queries, key_rows, values, cumulative, entering, same_first, allowed)
    merged = tokens_first(retained)
    gated_out = finish(merged, outgate, head_count)
    gated_low = gated_out.astype(jnp.bfloat16)
    mixed = tokens + jnp.dot(gated_low, out_w, preferred_element_type=jnp.float32)
    gu_w, down_w = (
        lax.all_gather(w_gu, "dp", axis=0, tiled=True),
        lax.all_gather(w_down, "dp", axis=0, tiled=True),
    )
    hidden_units = down_w.shape[0]
    scale_two = lax.rsqrt(jnp.mean(mixed * mixed, axis=1, keepdims=True) + 1e-06)
    normed_ffn = (mixed * scale_two * gain_ffn).astype(jnp.bfloat16)
    gate_up = jnp.dot(normed_ffn, gu_w, preferred_element_type=jnp.float32)
    gate_part = gate_up[:, :hidden_units]
    up_part = gate_up[:, hidden_units:]
    activated = (jax.nn.silu(gate_part) * up_part).astype(jnp.bfloat16)
    result = mixed + jnp.dot(activated, down_w, preferred_element_type=jnp.float32)
    position = lax.axis_index("seq") * row_count + jnp.arange(row_count, dtype=jnp.int32)
    valid_mask = (position < valid_count[0]).astype(jnp.float32)[:, None]
    mismatch = result - teacher[0]
    grad_out = cotangent[0] + valid_mask * mismatch
    squared_local = jnp.sum(valid_mask * mismatch * mismatch)
    count_local = jnp.sum(valid_mask)
    gu_w, down_w = (
        lax.all_gather(w_gu, "dp", axis=0, tiled=True),
        lax.all_gather(w_down, "dp", axis=0, tiled=True),
    )
    grad_ffn = grad_out.astype(jnp.bfloat16)
    down_grad = contract(activated, grad_ffn, 0, 0)
    grad_act = contract(grad_ffn, down_w, 1, 1)
    sigma = jax.nn.sigmoid(gate_part)
    grad_gate = grad_act * up_part * sigma * (1.0 + gate_part * (1.0 - sigma))
    grad_up = grad_act * gate_part * sigma
    grad_both = jnp.concatenate([grad_gate, grad_up], axis=1).astype(jnp.bfloat16)
    gu_grad = contract(normed_ffn, grad_both, 0, 0)
    grad_normed = contract(grad_both, gu_w, 1, 1)
    ffn_shares = (
        lax.psum_scatter(
            gu_grad.astype(jnp.bfloat16), "dp", scatter_dimension=0, tiled=True
        ).astype(jnp.float32),
        lax.psum_scatter(
            down_grad.astype(jnp.bfloat16), "dp", scatter_dimension=0, tiled=True
        ).astype(jnp.float32),
    )
    grad_mid, gain_ffn_grad = norm_back(grad_normed, mixed, scale_two, gain_ffn)
    grad_mixed = grad_out + grad_mid
    proj_w, decay_w, out_w = (
        lax.all_gather(w_proj, "dp", axis=0, tiled=True),
        lax.all_gather(w_decay, "dp", axis=0, tiled=True),
        lax.all_gather(w_out, "dp", axis=0, tiled=True),
    )
    grad_att = grad_mixed.astype(jnp.bfloat16)
    out_grad = contract(gated_low, grad_att, 0, 0)
    grad_gated = contract(grad_att, out_w, 1, 1)

    def finish_local(merged_rows, gate_rows):
        return finish(merged_rows, gate_rows, head_count)

    unused_value, finish_back = jax.vjp(finish_local, merged, outgate)
    grad_merged, grad_outgate = finish_back(grad_gated)
    grad_retained = heads_first(grad_merged, head_count)
    inflow = jnp.exp(cumulative) * same_first[None, :]
    grad_entering = jnp.einsum(
        "htd,hte->hde", queries * inflow[:, :, None], grad_retained, precision=HIGHEST_PRECISION
    )
    identity_back = (
        jnp.zeros((), jnp.float32),
        jnp.zeros((), jnp.float32),
        jnp.zeros((), jnp.float32),
        jnp.ones((head_count,), jnp.float32),
        jnp.zeros_like(grad_entering),
    )
    behind = carried_in_2(
        (live_one, first_id, last_id, through, grad_entering), "seq", join_backward, identity_back
    )
    returning = behind[4] * jnp.where(behind[1] == last_id, 1.0, 0.0)

    def local_pass(query_part, key_part, value_part, decay_part):
        local_cum = jnp.cumsum(decay_part, axis=0).T
        outputs = retain(query_part, key_part, value_part, local_cum, entering, same_first, allowed)
        leaving = (
            tail_state(key_part, value_part, local_cum, same_last)
            + (jnp.exp(local_cum[:, -1]) * same_first[-1])[:, None, None] * entering
        )
        return (outputs, leaving)

    unused_pair, pass_back = jax.vjp(local_pass, queries, key_rows, values, logdecay)
    grad_q, grad_k, grad_v, grad_logdecay = pass_back((grad_retained, returning))
    grad_logit = grad_logdecay * jax.nn.sigmoid(-decay_logit) / 16.0
    bias_grad = jnp.sum(grad_logit, axis=0)
    grad_logit_low = grad_logit.astype(jnp.bfloat16)
    grad_proj = jnp.concatenate(
        [
            tokens_first(grad_q) * head_dim ** (-0.5),
            tokens_first(grad_k),
            tokens_first(grad_v),
            grad_outgate,
        ],
        axis=1,
    ).astype(jnp.bfloat16)
    proj_grad = contract(normed, grad_proj, 0, 0)
    decay_grad = contract(normed, grad_logit_low, 0, 0)
    grad_normed_one = contract(grad_proj, proj_w, 1, 1) + contract(grad_logit_low, decay_w, 1, 1)
    grad_low, gain_ret_grad = norm_back(grad_normed_one, tokens, scale_one, gain_ret)
    grad_tokens = grad_mixed + grad_low
    ret_shares = (
        lax.psum_scatter(
            proj_grad.astype(jnp.bfloat16), "dp", scatter_dimension=0, tiled=True
        ).astype(jnp.float32),
        lax.psum_scatter(
            decay_grad.astype(jnp.bfloat16), "dp", scatter_dimension=0, tiled=True
        ).astype(jnp.float32),
        lax.psum_scatter(
            out_grad.astype(jnp.bfloat16), "dp", scatter_dimension=0, tiled=True
        ).astype(jnp.float32),
    )
    summed = (
        lax.psum(ret_shares[0].astype(jnp.bfloat16), "seq").astype(jnp.float32),
        lax.psum(ret_shares[1].astype(jnp.bfloat16), "seq").astype(jnp.float32),
        lax.psum(ret_shares[2].astype(jnp.bfloat16), "seq").astype(jnp.float32),
        lax.psum(ffn_shares[0].astype(jnp.bfloat16), "seq").astype(jnp.float32),
        lax.psum(ffn_shares[1].astype(jnp.bfloat16), "seq").astype(jnp.float32),
    )
    totals = lax.psum(
        (gain_ret_grad, gain_ffn_grad, bias_grad, squared_local, count_local), ("dp", "seq")
    )
    mse = totals[3] / (totals[4] * model_width)
    return (
        result[None],
        grad_tokens[None],
        summed[0],
        summed[1],
        totals[2],
        summed[2],
        totals[0],
        totals[1],
        summed[3],
        summed[4],
        mse,
    )


def solution(mesh):
    in_specs = (
        P("dp", "seq", None),
        P("dp", "seq"),
        P("dp"),
        P("dp", "seq", None),
        P("dp", "seq", None),
        P("dp", None),
        P("dp", None),
        P(),
        P("dp", None),
        P(),
        P(),
        P("dp", None),
        P("dp", None),
    )
    out_specs = (
        P("dp", "seq", None),
        P("dp", "seq", None),
        P("dp", None),
        P("dp", None),
        P(),
        P("dp", None),
        P(),
        P(),
        P("dp", None),
        P("dp", None),
        P(),
    )
    return jax.shard_map(shards, mesh=mesh, in_specs=in_specs, out_specs=out_specs, check_vma=False)
```

profile of v0, /device:TPU:0, one launch (start us, length us, event | category | flops | bytes accessed | tf_op | source)
XLA Modules:
  0.0 4341.6 jit_solution(9540350841145052467)
XLA Ops:
  8.0 73.4 %all_gather.71 = bf16[2048,16]{0,1:T(8,128)(2,1)S(1)} all-gather(bf16[256,16]{0,1:T(8,128)(2,1)S(1)} %copy-done.46), channel_id=1, replica_groups=mesh['dp'=8,'seq'=4] {'dp'}, dimensions={0}, use_global_device_ids=true | all-gather | bytes 73728 | tf_op jit(solution)/shard_map/all_gather | solution.py:155
  88.8 562.1 %all-gather.11.cloned.1.call-done = bf16[2048,8192]{1,0:T(8,128)(2,1)} async-done(((bf16[256,8192]{1,0:T(8,128)(2,1)}), bf16[2048,8192]{1,0:T(8,128)(2,1)}) %all-gather.11.cloned.1.call-update) | async-done | bytes 33554448 | tf_op jit(solution)/shard_map/all_gather | solution.py:154
  651.0 17.7 fusion.127
  668.7 3.7 slice_bitcast_fusion.1
  672.4 2.6 copy.158
  675.0 4.6 fusion.15
  686.6 7.3 all-reduce.12
  694.7 4.6 fusion.62
  699.3 15.1 all-gather.19.cloned.1.call-done
  714.3 19.7 while.38
  716.8 1.5 fusion.167
  723.4 1.6 fusion.167
  730.0 1.5 fusion.167
  734.0 2.8 fusion.63
  737.2 3.1 multiply_reduce_fusion.4
  741.6 2.7 fusion.22
  744.4 97.1 %all-gather.13.cloned.1.call-done = bf16[2048,2048]{1,0:T(8,128)(2,1)} async-done(((bf16[256,2048]{1,0:T(8,128)(2,1)}), bf16[2048,2048]{1,0:T(8,128)(2,1)}) %all-gather.13.cloned.1.call-update) | async-done | bytes 8388624 | tf_op jit(solution)/shard_map/all_gather | solution.py:156
  841.4 7.4 multiply_reduce_fusion.3
  848.9 846.2 %all-gather.15.cloned.1.call-done = bf16[2048,11008]{1,0:T(8,128)(2,1)} async-done(((bf16[256,11008]{1,0:T(8,128)(2,1)}), bf16[2048,11008]{1,0:T(8,128)(2,1)}) %all-gather.15.cloned.1.call-update) | async-done | bytes 45088784 | tf_op jit(solution)/shard_map/all_gather | solution.py:203
  1695.1 24.4 fusion.122
  1719.4 6.3 multiply_convert_fusion.2
  1725.8 402.0 %all-gather.17.cloned.1.call-done = bf16[5504,2048]{1,0:T(8,128)(2,1)} async-done(((bf16[688,2048]{1,0:T(8,128)(2,1)}), bf16[5504,2048]{1,0:T(8,128)(2,1)}) %all-gather.17.cloned.1.call-update) | async-done | bytes 22544400 | tf_op jit(solution)/shard_map/all_gather | solution.py:204
  2127.7 14.4 fusion.17
  2142.1 25.3 multiply_convert_fusion.1
  2167.5 21.0 multiply_reduce_fusion
  2188.4 3.6 multiply_add_fusion.1
  2192.1 8.1 multiply_bitcast_fusion.2
  2201.8 2.5 multiply_reduce_fusion.1
  2205.5 6.7 fusion.59
  2212.3 7.0 convolution_convert_fusion.3
  2219.4 1.8 copy-done.16
  2221.2 12.6 convolution_convert_fusion.2
  2236.6 6.8 all-reduce.13
  2243.4 1.6 copy.175
  2245.3 5.6 fusion.93
  2251.0 3.9 fusion.12
  2254.9 3.5 multiply_convert_fusion.3
  2258.3 2.3 copy.161
  2260.6 2.6 copy.176
  2263.2 8.6 fusion.6
  2271.7 25.3 while.39
  2298.3 7.2 fusion.25
  2305.5 2.4 copy.164
  2307.9 4.8 add_convert_fusion
  2312.7 2.3 copy.165
  2315.0 17.0 convolution_convert_fusion.1
  2332.1 21.6 convolution_convert_fusion
  2353.7 2.9 copy.140
  2357.0 2.3 fusion.16
  2359.8 2.5 reduce-window.16
  2363.6 24.6 reduce-scatter.12.cloned.1.call-done
  2388.2 369.4 %reduce-scatter.14.cloned.1.call-done = bf16[688,2048]{1,0:T(8,128)(2,1)} async-done(((bf16[5504,2048]{1,0:T(8,128)(2,1)}), bf16[688,2048]{1,0:T(8,128)(2,1)}) %reduce-scatter.14.cloned.1.call-update) | async-done | bytes 2818064 | tf_op jit(solution)/shard_map/reduce_scatter | solution.py:237
  2757.7 545.9 %reduce-scatter.8.cloned.1.call-done = bf16[256,8192]{1,0:T(8,128)(2,1)} async-done(((bf16[2048,8192]{1,0:T(8,128)(2,1)}), bf16[256,8192]{1,0:T(8,128)(2,1)}) %reduce-scatter.8.cloned.1.call-update) | async-done | bytes 4194320 | tf_op jit(solution)/shard_map/reduce_scatter | solution.py:303
  3303.5 714.3 %reduce-scatter.16.cloned.1.call-done = bf16[256,11008]{1,0:T(8,128)(2,1)} async-done(((bf16[2048,11008]{1,0:T(8,128)(2,1)}), bf16[256,11008]{1,0:T(8,128)(2,1)}) %reduce-scatter.16.cloned.1.call-update) | async-done | bytes 5636112
  4019.1 17.2 fusion.78
  4036.3 3.6 fusion.30
  4039.9 39.9 all-reduce.11
  4081.1 4.8 add_bitcast_fusion
  4086.0 7.0 psum.71
  4093.5 222.6 %all-reduce.17.cloned.1.call-done = (bf16[256,8192]{1,0:T(8,128)(2,1)}, bf16[256,2048]{1,0:T(8,128)(2,1)}, bf16[256,11008]{1,0:T(8,128)(2,1)}, bf16[688,2048]{1,0:T(8,128)(2,1)}) async-done(((bf16[256,8192]{1,0:T(8,128)(2,1)}, bf16[256,2048]{1,0:T(8,128)(2,1)}, bf16[256,11008]{1,0:T(8,128)(2,1)}, bf16[688,2048]{1,0:T(8,128)(2,1)}), (bf16[256,8192]{1,0:T(8,128)(2,1)}, bf16[256,2048]{1,0:T(8,128)(2,1)}, ...) | async-done | bytes 13697040 | tf_op jit(solution)/shard_map/psum | solution.py:314
  4316.1 7.8 convert_element_type.200
  4323.9 4.4 convert_element_type.194
  4328.3 3.2 convert_element_type.202
  4331.6 1.6 convert_element_type.198
  (222 shorter events, 43.4 us)
Async XLA Ops:
  7.2 0.8 copy-start.46
  7.2 74.2 %copy-start = (f32[1,256,2048]{2,1,0:T(8,128)S(1)}, f32[1,256,2048]{2,1,0:T(8,128)}, u32[]{:S(2)}) copy-start(f32[1,256,2048]{2,1,0:T(8,128)} %param.17) | copy-start | bytes 6291460
  7.2 643.8 %all-gather.11.cloned.1.call-start = ((), (), s32[]{:S(2)}) async-start(), calls=%async_computation.5 | async-start | bytes 37748736 | tf_op jit(solution)/shard_map/all_gather | solution.py:154
  7.9 73.7 %copy-start.35 = (f32[2048]{0:T(1024)S(1)}, f32[2048]{0:T(1024)}, u32[]{:S(2)}) copy-start(f32[2048]{0:T(1024)} %param.26) | copy-start | bytes 24580
  7.9 706.4 %all-gather.19.cloned.1.call-start = ((), (), s32[]{:S(2)}) async-start(), calls=%async_computation.13 | async-start | bytes 5242880 | tf_op jit(solution)/shard_map/all_gather | solution.py:11
  81.4 0.6 copy-start.27
  81.6 0.7 copy-start.49
  81.6 1.0 copy-start.42
  81.6 2.4 copy-start.37
  82.3 586.4 %copy-start.10 = (bf16[256,2048]{1,0:T(8,128)(2,1)}, bf16[256,2048]{1,0:T(8,128)(2,1)S(1)}, u32[]{:S(2)}) copy-start(bf16[256,2048]{1,0:T(8,128)(2,1)S(1)} %multiply_convert_fusion.5) | copy-start | bytes 3145732
  82.6 0.6 copy-start.33
  83.9 584.8 %copy-start.29 = (f32[16,2,128]{2,0,1:T(8,128)}, f32[16,2,128]{2,0,1:T(8,128)S(1)}, u32[]{:S(2)}) copy-start(f32[16,2,128]{2,0,1:T(8,128)S(1)} %reduce-window.14) | copy-start | bytes 49156
  84.1 4.1 copy-start.38
  86.8 1.3 copy-start.47
  88.1 0.6 copy-start.40
  88.2 0.6 copy-start.44
  88.8 586.2 %copy-start.31 = (f32[16,256]{1,0:T(8,128)}, f32[16,256]{1,0:T(8,128)S(1)}, u32[]{:S(2)}) copy-start(f32[16,256]{1,0:T(8,128)S(1)} %get-tuple-element.574) | copy-start | bytes 49156
  672.4 7.2 copy-start.2
  679.7 161.8 %all-gather.13.cloned.1.call-start = ((), (), s32[]{:S(2)}) async-start(), calls=%async_computation.6 | async-start | bytes 9437184 | tf_op jit(solution)/shard_map/all_gather | solution.py:156
  680.4 1014.6 %all-gather.15.cloned.1.call-start = ((), (), s32[]{:S(2)}) async-start(), calls=%async_computation.7 | async-start | bytes 50724864 | tf_op jit(solution)/shard_map/all_gather | solution.py:203
  681.0 2.0 copy-start.50
  681.0 1446.7 %all-gather.17.cloned.1.call-start = ((), (), s32[]{:S(2)}) async-start(), calls=%async_computation.8 | async-start | bytes 25362432 | tf_op jit(solution)/shard_map/all_gather | solution.py:204
  681.6 1590.2 %all-gather.21.cloned.1.call-start = ((), (), s32[]{:S(2)}) async-start(), calls=%async_computation.14 | async-start | bytes 2621440 | tf_op jit(solution)/shard_map/all_gather | solution.py:26
  734.0 2.9 copy-start.12
  734.0 3.2 copy-start.21
  736.9 3.4 copy-start.18
  740.3 1.3 copy-start.8
  744.4 950.7 %copy-start.26 = (f32[2048]{0:T(1024)S(1)}, f32[2048]{0:T(1024)}, u32[]{:S(2)}) copy-start(f32[2048]{0:T(1024)} %param.27) | copy-start | bytes 24580
  1719.4 408.3 %copy-start.14 = (f32[256,2048]{1,0:T(8,128)S(1)}, f32[256,2048]{1,0:T(8,128)}, u32[]{:S(2)}) copy-start(f32[256,2048]{1,0:T(8,128)} %get-tuple-element.584) | copy-start | bytes 6291460
  2142.1 25.3 copy-start.15
  2188.4 3.6 copy-start.9
  2192.0 20.3 copy-start.7
  2200.2 1.6 copy-start.19
  2204.2 1.3 copy-start.4
  2212.3 176.0 %reduce-scatter.12.cloned.1.call-start = ((), (), s32[]{:S(2)}) async-start(), calls=%async_computation.11 | async-start | bytes 9437184 | tf_op jit(solution)/shard_map/reduce_scatter | solution.py:309
  2219.3 1.9 copy-start.16
  2219.4 538.3 %reduce-scatter.14.cloned.1.call-start = ((), (), s32[]{:S(2)}) async-start(), calls=%async_computation.12 | async-start | bytes 25362432 | tf_op jit(solution)/shard_map/reduce_scatter | solution.py:237
  2233.9 11.2 copy-start.13
  2233.9 1069.6 %reduce-scatter.8.cloned.1.call-start = ((), (), s32[]{:S(2)}) async-start(), calls=%async_computation.9 | async-start | bytes 37748736 | tf_op jit(solution)/shard_map/reduce_scatter | solution.py:303
  2243.4 1.9 copy-start.5
  2251.0 3.9 copy-start.51
  2260.6 2.6 copy-start.6
  2297.1 1.2 copy-start.25
  2297.1 1.2 copy-start.32
  2298.1 7.4 copy-start.17
  2305.5 2.4 copy-start.3
  2332.0 1685.8 %reduce-scatter.16.cloned.1.call-start = ((), (), s32[]{:S(2)}) async-start(), calls=%async_computation.15 | async-start | bytes 50724864
  2353.6 1732.3 %reduce-scatter.10.cloned.1.call-start = ((), (), s32[]{:S(2)}) async-start(), calls=%async_computation.10 | async-start | bytes 73728 | tf_op jit(solution)/shard_map/reduce_scatter | solution.py:306
  2356.8 2.5 copy-start.30
  2356.8 2.5 copy-start.39
  2356.8 2.5 copy-start.41
  2356.8 2.5 copy-start.48
  2356.9 2.9 copy-start.45
  2356.9 5.6 copy-start.34
  2356.9 5.8 copy-start.11
  2363.6 1952.6 %all-reduce.17.cloned.1.call-start = ((), (), s32[]{:S(2)}) async-start(), calls=%async_computation.16 | async-start | bytes 27394048 | tf_op jit(solution)/shard_map/psum | solution.py:314
  4017.8 1.2 copy-start.22
  4019.1 17.2 copy-start.1
  4019.1 17.2 copy-start.28
  4019.1 17.2 copy-start.36
  4019.1 17.2 copy-start.43
  4316.1 7.8 copy-start.20
  4323.9 4.4 copy-start.23
  4328.3 3.2 copy-start.24
Sparse Core Ops, SparseCore 0:
  9.6 641.3 all-gather.10
  679.8 34.5 all-gather.18
  716.5 124.9 all-gather.12
  842.8 852.1 all-gather.14
  1696.4 431.2 all-gather.16
  2212.4 22.5 all-gather.20
  2239.2 149.0 reduce-scatter.11
  2392.7 364.9 reduce-scatter.13
  2761.4 542.0 reduce-scatter.7
  3307.3 710.4 reduce-scatter.15
  4021.6 52.8 reduce-scatter.9
  4077.0 239.0 all-reduce.16
where the time goes:
time: 4350 us; the launch traced here: 4340 us
  waiting for transfers between devices  3800 us (87%)
  matrix products  255 us (6%)
  blocking collectives  134 us (3%)
  other arithmetic  57.9 us (1%)
  local copies, waits for them, and re-layouts  48.5 us (1%)
    all_gather x1, waiting for transfers between devices, shards(): lax.all_gather(w_gu, 'dp', axis=0, tiled=True)  846 us
    unnamed x13, waiting for transfers between devices  717 us
    all_gather x1, waiting for transfers between devices, shards(): lax.all_gather(w_proj, 'dp', axis=0, tiled=True)  562 us
    reduce_scatter x1, waiting for transfers between devices, shards(): lax.psum_scatter(proj_grad.astype(jnp.bfloat16), 'dp', scatter_dimension=...  546 us
    all_gather x1, waiting for transfers between devices, shards(): lax.all_gather(w_down, 'dp', axis=0, tiled=True)  402 us
    reduce_scatter x1, waiting for transfers between devices, shards(): lax.psum_scatter(down_grad.astype(jnp.bfloat16), 'dp', scatter_dimension=...  369 us
    psum x1, waiting for transfers between devices, shards(): lax.psum(ret_shares[0].astype(jnp.bfloat16), 'seq').astype(jnp.float32)  223 us
    dot_general x10, matrix products, contract(): lax.dot_general(left, right, (((left_dim,), (right_dim,)), ((), ())), pre...  134 us
  transfers between devices with their start and end apart: 12, of which 10 were waited for; matrix products, arithmetic and copies ran while one was open for 5% of the time, Pallas kernels for 0%

commit v1 on v0

v1 whole, which is shorter than its diff:
```python
import jax
import jax.numpy as jnp
from jax import lax
from jax.sharding import PartitionSpec as P

LOW = jnp.bfloat16
WIDE = jnp.float32


def dot(left, right, left_dim=1, right_dim=0):
    return lax.dot_general(
        left, right, (((left_dim,), (right_dim,)), ((), ())), preferred_element_type=WIDE
    )


def batch_dot(left, right, left_dim, right_dim):
    return lax.dot_general(
        left, right, (((left_dim,), (right_dim,)), ((0,), (0,))), preferred_element_type=WIDE
    )


def blocks_at(matrix, places, size, axis):
    return jnp.concatenate(
        [lax.dynamic_slice_in_dim(matrix, place * size, size, axis) for place in places], axis=axis
    )


def pick(index, choices):
    chosen = choices[-1]
    for number in range(len(choices) - 2, -1, -1):
        chosen = jnp.where(index == number, choices[number], chosen)
    return chosen


class Links:
    def __init__(self, dp_count, seq_count):
        self.dp_count, self.seq_count = dp_count, seq_count
        self.ring = dp_count // 2
        self.me_dp, self.me_seq = lax.axis_index("dp"), lax.axis_index("seq")
        self.turn, self.side = self.me_dp // 2, self.me_dp % 2
        self.past = {}

    def send(self, value, axis, pairs, stream=None, depth=2):
        if stream is not None:
            past = self.past.setdefault(stream, [])
            if len(past) >= depth:
                value, unused = lax.optimization_barrier((value, past[-depth]))
        moved = lax.ppermute(value, axis, pairs)
        if stream is not None:
            past.append(moved)
        return moved

    def around(self, value, stream=None):
        pairs = [(d, (d + 2) % self.dp_count) for d in range(self.dp_count)]
        return self.send(value, "dp", pairs, stream)

    def across(self, value, stream=None):
        return self.send(value, "dp", [(d, d ^ 1) for d in range(self.dp_count)], stream)

    def core(self, value):
        return self.send(value, "seq", [(s, s ^ 1) for s in range(self.seq_count)])

    def chip(self, value):
        return self.send(value, "seq", [(s, s ^ 2) for s in range(self.seq_count)])

    def sources(self):
        return [
            ((self.turn - r) % self.ring) * 2 + (self.side ^ e)
            for r in range(self.ring)
            for e in range(2)
        ]

    def places(self):
        return [
            ((self.turn - d // 2) % self.ring) * 2 + (self.side ^ (d % 2))
            for d in range(self.dp_count)
        ]

    def gather(self, block, streams=("ring", "pair")):
        own = [block]
        for unused in range(self.ring - 1):
            own.append(self.around(own[-1], streams[0]))
        other = [self.across(piece, streams[1]) for piece in own]
        return [piece for both in zip(own, other) for piece in both]

    def gather_pairs(self, block, streams=("ring", "pair")):
        pieces = [jnp.stack([block, self.across(block, streams[1])])]
        for unused in range(self.ring - 1):
            pieces.append(self.around(pieces[-1], streams[0]))
        return pieces

    def ring_sum(self, parts, stream="ring"):
        running = parts[1].astype(LOW)
        for r in range(2, self.ring):
            running = (self.around(running, stream).astype(WIDE) + parts[r].astype(WIDE)).astype(LOW)
        return self.around(running, stream).astype(WIDE) + parts[0].astype(WIDE)

    def scatter(self, own, other, streams=("ring", "pair")):
        sums = []
        for r in list(range(1, self.ring)) + [0]:
            come = self.across(other[r], streams[1])
            sums.append((own[r].astype(WIDE) + come.astype(WIDE)).astype(LOW))
        sums = sums[-1:] + sums[:-1]
        return self.ring_sum(sums, streams[0]).astype(LOW)

    def tokens_in(self, value):
        far = self.chip(value)
        near = self.core(value)
        return [value, near, far, self.core(far)]

    def tokens_out(self, parts):
        come_far = self.core(parts[3].astype(LOW))
        come_own = self.core(parts[1].astype(LOW))
        far = (parts[2] + come_far.astype(WIDE)).astype(LOW)
        return parts[0] + come_own.astype(WIDE) + self.chip(far).astype(WIDE)

    def in_order(self, pieces):
        return [
            pick(self.me_seq, [pieces[k ^ s] for s in range(self.seq_count)])
            for k in range(self.seq_count)
        ]


class Placed:
    def __init__(self, links, heads, hidden):
        self.links = links
        self.heads, self.width = heads, heads // links.seq_count
        shard = hidden // links.dp_count
        self.shard = shard
        self.part = -(-shard // (16 * links.seq_count)) * 16
        self.units = self.part * links.dp_count

    def to_rel(self, value):
        links = self.links
        return blocks_at(value, links.sources(), value.shape[1] // links.dp_count, 1)

    def from_rel(self, value):
        links = self.links
        return blocks_at(value, links.places(), value.shape[1] // links.dp_count, 1)

    def proj(self, weight):
        size = weight.shape[1] // (4 * self.heads)
        columns = [(b * self.width + j) * self.links.seq_count for b in range(4) for j in range(self.width)]
        block = blocks_at(weight, [at + self.links.me_seq for at in columns], size, 1)
        return jnp.concatenate(self.links.gather(block), axis=0)

    def decay(self, weight):
        pieces = self.links.gather_pairs(weight, (None, None))
        return jnp.concatenate([piece.reshape(-1, weight.shape[1]) for piece in pieces], axis=0)

    def out(self, weight):
        links = self.links
        size = weight.shape[0] // 2
        own = lax.dynamic_slice_in_dim(weight, (links.me_seq % 2) * size, size, 0)
        block = jnp.where(links.side == links.me_seq // 2, own, links.across(own, "pair"))
        pieces = [block]
        for unused in range(links.ring - 1):
            pieces.append(links.around(pieces[-1], "ring"))
        stacked = jnp.concatenate(pieces, axis=0)
        return blocks_at(stacked, [(links.turn - j) % links.ring for j in range(links.ring)], size, 0)

    def gate_up(self, weight):
        links = self.links
        pieces = []
        for start in range(0, weight.shape[1], self.shard):
            piece = weight[:, start : start + self.shard]
            piece = jnp.pad(piece, ((0, 0), (0, self.part * links.seq_count - self.shard)))
            pieces.append(
                lax.dynamic_slice_in_dim(piece, links.me_seq * self.part, self.part, 1)
            )
        half = len(pieces) // 2
        gate, up = (jnp.concatenate(pieces[:half], axis=1), jnp.concatenate(pieces[half:], axis=1))
        block = jnp.concatenate([gate, up], axis=1)
        return jnp.concatenate(links.gather(block), axis=0)

    def down(self, weight):
        links = self.links
        padded = jnp.pad(weight, ((0, self.part * links.seq_count - self.shard), (0, 0)))
        block = lax.dynamic_slice_in_dim(padded, links.me_seq * self.part, self.part, 0)
        stacked = jnp.concatenate(links.gather(block), axis=0)
        return blocks_at(stacked, links.places(), self.part, 0)

    def grad_down(self, grad):
        links = self.links
        blocks = [
            lax.dynamic_slice_in_dim(grad, place * self.part, self.part, 0) for place in links.sources()
        ]
        total = links.scatter(blocks[0::2], blocks[1::2])
        pieces = links.in_order(links.tokens_in(total))
        return jnp.concatenate(pieces, axis=0)[: self.shard].astype(WIDE)

    def split_rel(self, grad):
        size = grad.shape[0] // self.links.dp_count
        blocks = [grad[i * size : (i + 1) * size] for i in range(self.links.dp_count)]
        return blocks[0::2], blocks[1::2]

    def grad_gate_up(self, grad):
        links = self.links
        total = links.scatter(*self.split_rel(grad))
        pieces = links.in_order(links.tokens_in(total))
        rows = []
        for block in range(2 * links.dp_count):
            whole = jnp.concatenate(
                [piece[:, block * self.part : (block + 1) * self.part] for piece in pieces], axis=1
            )
            rows.append(whole[:, : self.shard])
        return jnp.concatenate(rows, axis=1).astype(WIDE)

    def grad_proj(self, grad):
        links = self.links
        total = links.scatter(*self.split_rel(grad))
        pieces = links.in_order(links.tokens_in(total))
        size = total.shape[1] // (4 * self.width)
        columns = [
            piece[:, at * size : (at + 1) * size] for at in range(4 * self.width) for piece in pieces
        ]
        return jnp.concatenate(columns, axis=1).astype(WIDE)

    def grad_decay(self, grad):
        links = self.links
        own, other = self.split_rel(grad)
        come = links.across(jnp.stack(other).astype(LOW))
        sums = (jnp.stack(own) + come.astype(WIDE)).astype(LOW)
        total = links.ring_sum([sums[r] for r in range(links.ring)], None).astype(LOW)
        pieces = links.in_order(links.tokens_in(total))
        return jnp.stack(pieces, axis=2).reshape(total.shape[0], -1).astype(WIDE)

    def grad_out(self, grad):
        links = self.links
        size = grad.shape[0] // links.ring
        parts = [
            lax.dynamic_slice_in_dim(grad, ((links.turn - r) % links.ring) * size, size, 0)
            for r in range(links.ring)
        ]
        total = links.ring_sum(parts, "ring").astype(LOW)
        come = links.across(total, "pair")
        mine = (total.astype(WIDE) + come.astype(WIDE)).astype(LOW)
        near = links.core(mine)
        first = links.me_seq % 2 == 0
        pair = jnp.concatenate([jnp.where(first, mine, near), jnp.where(first, near, mine)], axis=0)
        far = links.chip(pair)
        return jnp.where(links.me_seq // 2 == links.side, pair, far).astype(WIDE)

    def head_columns(self, table):
        return jnp.concatenate(
            [
                lax.dynamic_slice_in_dim(table, j * self.links.seq_count + self.links.me_seq, 1, table.ndim - 1)
                for j in range(self.width)
            ],
            axis=table.ndim - 1,
        )


class Plain:
    def __init__(self, dp_count, seq_count, heads, hidden):
        self.dp_count, self.seq_count = dp_count, seq_count
        self.me_seq = lax.axis_index("seq")
        self.heads, self.width = heads, heads // seq_count
        self.units = hidden // seq_count

    def to_rel(self, value):
        return value

    def from_rel(self, value):
        return value

    def mine(self, value, axis):
        return lax.dynamic_index_in_dim(value, self.me_seq, axis, keepdims=False)

    def spread(self, value, axis):
        wide = jnp.expand_dims(value, axis)
        wide = jnp.concatenate(
            [jnp.where(self.me_seq == s, wide, jnp.zeros_like(wide)) for s in range(self.seq_count)], axis
        )
        return wide

    def proj(self, weight):
        rows = weight.shape[0]
        block = self.mine(weight.reshape(rows, 4 * self.width, self.seq_count, -1), 2).reshape(rows, -1)
        return lax.all_gather(block, "dp", axis=0, tiled=True)

    def decay(self, weight):
        return lax.all_gather(weight, "dp", axis=0, tiled=True)

    def out(self, weight):
        whole = lax.all_gather(weight, "dp", axis=0, tiled=True)
        columns = whole.shape[1]
        return self.mine(whole.reshape(self.width, self.seq_count, -1, columns), 1).reshape(-1, columns)

    def gate_up(self, weight):
        rows = weight.shape[0]
        block = self.mine(weight.reshape(rows, 2, self.seq_count, -1), 2).reshape(rows, -1)
        return lax.all_gather(block, "dp", axis=0, tiled=True)

    def down(self, weight):
        whole = lax.all_gather(weight, "dp", axis=0, tiled=True)
        return self.mine(whole.reshape(self.seq_count, -1, whole.shape[1]), 0)

    def scatter(self, grad):
        return lax.psum_scatter(grad.astype(LOW), "dp", scatter_dimension=0, tiled=True)

    def both(self, grad):
        return lax.psum(self.scatter(grad), "seq").astype(WIDE)

    def grad_down(self, grad):
        return self.both(self.spread(grad, 0).reshape(-1, grad.shape[1]))

    def grad_out(self, grad):
        columns = grad.shape[1]
        return self.both(self.spread(grad.reshape(self.width, -1, columns), 1).reshape(-1, columns))

    def grad_columns(self, grad, blocks):
        total = self.scatter(grad)
        rows = total.shape[0]
        pieces = lax.all_gather(total.reshape(rows, blocks, -1), "seq", axis=2)
        return pieces.reshape(rows, -1).astype(WIDE)

    def grad_gate_up(self, grad):
        return self.grad_columns(grad, 2)

    def grad_proj(self, grad):
        return self.grad_columns(grad, 4 * self.width)

    def grad_decay(self, grad):
        return self.grad_columns(grad, self.width)

    def head_columns(self, table):
        return self.mine(table.reshape(table.shape[:-1] + (self.width, self.seq_count)), table.ndim)


def rms(value):
    return lax.rsqrt(jnp.mean(value * value, axis=1, keepdims=True) + 1e-06)


def norm_back(grad_normed, source, inverse, gain):
    grad_gain = jnp.sum(grad_normed * source * inverse, axis=0)
    scaled = grad_normed * gain
    grad_source = inverse * (
        scaled - source * inverse * inverse * jnp.mean(scaled * source, axis=1, keepdims=True)
    )
    return (grad_source, grad_gain)


def split_heads(matrix, count):
    return matrix.reshape(matrix.shape[0], count, -1).transpose(1, 0, 2)


def join_heads(tensor):
    return tensor.transpose(1, 0, 2).reshape(tensor.shape[1], -1)


def shards(
    inputs, segments, valid_count, teacher, cotangent, w_proj, w_decay, b_decay, w_out,
    gain_ret, gain_ffn, w_gu, w_down,
):
    dp_count, seq_count = lax.axis_size("dp"), lax.axis_size("seq")
    tokens = inputs[0]
    count, model_width = tokens.shape
    heads = w_decay.shape[1]
    head_dim = model_width // heads
    hidden = w_down.shape[0] * dp_count
    me_seq = lax.axis_index("seq")
    placed = dp_count == 8 and seq_count == 4 and heads == 16
    if placed:
        links = Links(dp_count, seq_count)
        plan = Placed(links, heads, hidden)

        def tokens_in(value):
            return jnp.concatenate(links.tokens_in(value), axis=0)

        def tokens_out(value):
            return links.tokens_out(jnp.split(value, seq_count, axis=0))

        def in_order(value):
            return blocks_at(value, [me_seq ^ k for k in range(seq_count)], count, 0)

        out_order = in_order
    else:
        plan = Plain(dp_count, seq_count, heads, hidden)

        def tokens_in(value):
            return lax.all_gather(value, "seq", axis=0, tiled=True)

        def tokens_out(value):
            return lax.psum_scatter(
                value.astype(LOW), "seq", scatter_dimension=0, tiled=True
            ).astype(WIDE)

        def in_order(value):
            return value

        out_order = in_order
    width = heads // seq_count

    scale_one = rms(tokens)
    normed_here = plan.to_rel((tokens * scale_one * gain_ret).astype(LOW))
    normed = in_order(tokens_in(normed_here))
    row_segments = in_order(tokens_in(jnp.broadcast_to(segments[0][:, None], (count, 128))))[:, 0]
    decay_w = plan.decay(w_decay)
    proj_w = plan.proj(w_proj)
    out_w = plan.out(w_out)
    gu_w = plan.gate_up(w_gu)
    down_w = plan.down(w_down)
    units = plan.units
    row = normed.shape[0]

    own_decay_w = plan.head_columns(decay_w)
    decay_logit = dot(normed, own_decay_w) + plan.head_columns(b_decay)
    cumulative = jnp.cumsum(jax.nn.log_sigmoid(decay_logit) / 16.0, axis=0).T
    projected = dot(normed, proj_w)
    share = width * head_dim
    queries = split_heads((projected[:, :share] * head_dim ** (-0.5)).astype(LOW), width)
    key_rows = split_heads(projected[:, share : 2 * share].astype(LOW), width)
    values = split_heads(projected[:, 2 * share : 3 * share].astype(LOW), width)
    outgate = projected[:, 3 * share :]
    order = jnp.arange(row, dtype=jnp.int32)
    allowed = (row_segments[:, None] == row_segments[None, :]) & (order[:, None] >= order[None, :])
    spread = cumulative[:, :, None] - cumulative[:, None, :]
    table = jnp.where(allowed[None], jnp.exp(jnp.where(allowed[None], spread, 0.0)), 0.0)
    scores = batch_dot(queries, key_rows, 2, 2) * table
    retained = batch_dot(scores.astype(LOW), values, 2, 1)
    power = jnp.mean(retained * retained, axis=2, keepdims=True)
    inverse = lax.rsqrt(jnp.maximum(power, 1.0))
    unit = retained * inverse
    gate_heads = split_heads(outgate, width)
    gate_sigma = jax.nn.sigmoid(gate_heads)
    gated = join_heads((gate_heads * gate_sigma * unit).astype(LOW))
    mixed = tokens + tokens_out(out_order(dot(gated, out_w)))

    scale_two = rms(mixed)
    normed_ffn = tokens_in(plan.to_rel((mixed * scale_two * gain_ffn).astype(LOW)))
    gate_up = dot(normed_ffn, gu_w)
    gate_part, up_part = gate_up[:, :units], gate_up[:, units:]
    sigma = jax.nn.sigmoid(gate_part)
    activated = (gate_part * sigma * up_part).astype(LOW)
    result = mixed + tokens_out(dot(activated, down_w))

    position = me_seq * count + jnp.arange(count, dtype=jnp.int32)
    valid_mask = (position < valid_count[0]).astype(WIDE)[:, None]
    mismatch = result - teacher[0]
    grad_out = cotangent[0] + valid_mask * mismatch
    squared_local = jnp.sum(valid_mask * mismatch * mismatch)
    count_local = jnp.sum(valid_mask)

    grad_ffn = tokens_in(grad_out.astype(LOW))
    down_grad = plan.grad_down(dot(activated, grad_ffn, 0, 0).astype(LOW))
    grad_act = dot(grad_ffn, down_w, 1, 1)
    grad_gate = grad_act * up_part * sigma * (1.0 + gate_part * (1.0 - sigma))
    grad_up = grad_act * gate_part * sigma
    grad_both = jnp.concatenate([grad_gate, grad_up], axis=1).astype(LOW)
    gu_grad = plan.grad_gate_up(dot(normed_ffn, grad_both, 0, 0).astype(LOW))
    grad_normed = plan.from_rel(tokens_out(dot(grad_both, gu_w, 1, 1)))
    grad_mid, gain_ffn_grad = norm_back(grad_normed, mixed, scale_two, gain_ffn)
    grad_mixed = grad_out + grad_mid

    grad_att = in_order(tokens_in(grad_mixed.astype(LOW)))
    out_grad = plan.grad_out(dot(gated, grad_att, 0, 0).astype(LOW))
    grad_gated = split_heads(dot(grad_att, out_w, 1, 1), width)
    grad_outgate = grad_gated * unit * gate_sigma * (1.0 + gate_heads * (1.0 - gate_sigma))
    grad_unit = grad_gated * gate_heads * gate_sigma
    along = jnp.mean(grad_unit * unit, axis=2, keepdims=True)
    grad_retained = inverse * jnp.where(power > 1.0, grad_unit - unit * along, grad_unit)
    grad_low = grad_retained.astype(LOW)
    grad_scores = batch_dot(grad_low, values, 2, 2)
    energy = scores * grad_scores
    grad_pairs = (table * grad_scores).astype(LOW)
    grad_q = batch_dot(grad_pairs, key_rows, 2, 1)
    grad_k = batch_dot(grad_pairs, queries, 1, 1)
    grad_v = batch_dot(scores.astype(LOW), grad_low, 1, 1)
    grad_cum = (jnp.sum(energy, axis=2) - jnp.sum(energy, axis=1)).T
    grad_logdecay = lax.cumsum(grad_cum, axis=0, reverse=True)
    grad_logit = grad_logdecay * jax.nn.sigmoid(-decay_logit) / 16.0
    bias_local = jnp.sum(grad_logit, axis=0)
    grad_logit_low = grad_logit.astype(LOW)
    grad_proj = jnp.concatenate(
        [
            join_heads(part)
            for part in (grad_q * head_dim ** (-0.5), grad_k, grad_v, grad_outgate)
        ],
        axis=1,
    ).astype(LOW)
    proj_grad = plan.grad_proj(dot(normed, grad_proj, 0, 0).astype(LOW))
    decay_grad = plan.grad_decay(dot(normed, grad_logit_low, 0, 0))
    back = dot(grad_proj, proj_w, 1, 1) + dot(grad_logit_low, own_decay_w, 1, 1)
    grad_normed_one = plan.from_rel(tokens_out(out_order(back)))
    grad_first, gain_ret_grad = norm_back(grad_normed_one, tokens, scale_one, gain_ret)
    grad_tokens = grad_mixed + grad_first

    bias_wide = jnp.stack(
        [jnp.where(me_seq == s, bias_local, 0.0) for s in range(seq_count)], axis=1
    ).reshape(heads)
    totals = lax.psum(
        (gain_ret_grad, gain_ffn_grad, bias_wide, squared_local, count_local), ("dp", "seq")
    )
    mse = totals[3] / (totals[4] * model_width)
    return (
        result[None],
        grad_tokens[None],
        proj_grad,
        decay_grad,
        totals[2],
        out_grad,
        totals[0],
        totals[1],
        gu_grad,
        down_grad,
        mse,
    )


def solution(mesh):
    rows = P("dp", None)
    in_specs = (
        P("dp", "seq", None),
        P("dp", "seq"),
        P("dp"),
        P("dp", "seq", None),
        P("dp", "seq", None),
        rows,
        rows,
        P(),
        rows,
        P(),
        P(),
        rows,
        rows,
    )
    out_specs = (
        P("dp", "seq", None),
        P("dp", "seq", None),
        rows,
        rows,
        P(),
        rows,
        P(),
        P(),
        rows,
        rows,
        P(),
    )
    return jax.shard_map(shards, mesh=mesh, in_specs=in_specs, out_specs=out_specs, check_vma=False)
```

time: 4350 us -> 1190 us (0.27)
  waiting for transfers between devices: 3800 us -> 507 us
  local copies, waits for them, and re-layouts: 48.5 us -> 208 us
  blocking collectives: 134 us -> 57.4 us
  starting transfers between devices: 0.48 us -> 68.8 us
  other arithmetic: 57.9 us -> 120 us
  matrix products: 255 us -> 207 us
    all_gather x6 -> x0, waiting for transfers between devices: 1920 us -> none  [the longest x1 846 us: shards(): lax.all_gather(w_gu, 'dp', axis=0, tiled=True)]
    reduce_scatter x4 -> x0, waiting for transfers between devices: 940 us -> none  [the longest x1 546 us: shards(): lax.psum_scatter(proj_grad.astype(jnp.bfloat16), 'dp', scatter_dimension=...]
    unnamed x13 -> x0, waiting for transfers between devices: 717 us -> none
    ppermute x0 -> x99, waiting for transfers between devices: none -> 507 us  [send(): moved = lax.ppermute(value, axis, pairs)]
    psum x1 -> x0, waiting for transfers between devices: 223 us -> none  [shards(): lax.psum(ret_shares[0].astype(jnp.bfloat16), 'seq').astype(jnp.float32)]
    unnamed x124 -> x362, local copies, waits for them, and re-layouts: 21.7 us -> 139 us
    all_gather x1 -> x0, blocking collectives: 73.4 us -> none  [shards(): lax.all_gather(w_decay, 'dp', axis=0, tiled=True)]
    ppermute x0 -> x99, starting transfers between devices: none -> 68.8 us  [send(): moved = lax.ppermute(value, axis, pairs)]
  transfers between devices with their start and end apart: 12 -> 99, of which waited for: 10 -> 41; matrix products, arithmetic and copies ran while one was open for 5% -> 33% of each run, Pallas kernels for 0% -> 0%
where the time goes in v1:
time: 1190 us; the launch traced here: 1170 us
  waiting for transfers between devices  507 us (43%)
  local copies, waits for them, and re-layouts  208 us (17%)
  matrix products  207 us (17%)
  other arithmetic  120 us (10%)
  starting transfers between devices  68.8 us (6%)
  blocking collectives  57.4 us (5%)
    ppermute x99, waiting for transfers between devices, send(): moved = lax.ppermute(value, axis, pairs)  507 us
    dot_general x15, matrix products, dot(): lax.dot_general(left, right, (((left_dim,), (right_dim,)), ((), ())), pre...  153 us
    unnamed x362, local copies, waits for them, and re-layouts  139 us
    ppermute x99, starting transfers between devices, send(): moved = lax.ppermute(value, axis, pairs)  68.8 us
    psum x1, blocking collectives, shards(): lax.psum((gain_ret_grad, gain_ffn_grad, bias_wide, squared_local, count_l...  57.4 us
    dot_general x6, matrix products, batch_dot(): lax.dot_general(left, right, (((left_dim,), (right_dim,)), ((0,), (0,))),...  53.4 us
  transfers between devices with their start and end apart: 99, of which 41 were waited for; matrix products, arithmetic and copies ran while one was open for 33% of the time, Pallas kernels for 0%

profile of v1, /device:TPU:0, one launch (start us, length us, event | category | flops | bytes accessed | tf_op | source)
XLA Modules:
  0.0 1174.7 jit_solution(992640924846360541)
XLA Ops:
  39.8 8.3 fusion.77
  80.4 4.0 collective-permute-done.14
  84.4 5.5 collective-permute-done.15
  90.0 5.5 collective-permute-done.16
  106.5 19.6 %collective-permute-done.6 = bf16[256,2048]{1,0:T(8,128)(2,1)} collective-permute-done((bf16[256,2048]{1,0:T(8,128)(2,1)}, bf16[256,2048]{1,0:T(8,128)(2,1)}, u32[]{:S(2)}, u32[]{:S(2)}) %collective-permute-start.6) | collective-permute-done | bytes 1048608 | tf_op jit(solution)/shard_map/ppermute | solution.py:48
  134.4 16.3 %collective-permute-done.7 = bf16[256,2048]{1,0:T(8,128)(2,1)} collective-permute-done((bf16[256,2048]{1,0:T(8,128)(2,1)}, bf16[256,2048]{1,0:T(8,128)(2,1)}, u32[]{:S(2)}, u32[]{:S(2)}) %collective-permute-start.7) | collective-permute-done | bytes 1048608 | tf_op jit(solution)/shard_map/ppermute | solution.py:48
  159.7 6.2 collective-permute-done.17
  171.6 7.5 collective-permute-done.18
  179.5 6.2 collective-permute-done.9
  186.7 13.2 %fusion.85 = (bf16[1024,2048]{1,0:T(8,128)(2,1)S(1)}, f32[1024,2048]{1,0:T(8,128)}) fusion(bf16[2048,2048]{1,0:T(8,128)(2,1)} %constant_dynamic-update-slice_fusion.24, bf16[256,2048]{1,0:T(8,128)(2,1)S(1)} %copy-done.46, bf16[256,2048]{1,0:T(8,128)(2,1)S(1)} %copy-done.48, bf16[256,2048]{1,0:T(8,128)(2,1)S(1)} %copy-done.50, ...), kind=kOutput, calls=%fused_computation.499 | convolution fusion | flops 8608808960 | bytes 25165824 | tf_op jit(solution)/shard_map/dot_general | solution.py:11
  203.9 4.1 fusion.76
  210.3 7.5 multiply_reduce_fusion.3
  224.7 6.7 collective-permute-done.20
  253.3 28.0 %collective-permute-done.28 = bf16[256,2816]{1,0:T(8,128)(2,1)} collective-permute-done((bf16[256,2816]{1,0:T(8,128)(2,1)S(1)}, bf16[256,2816]{1,0:T(8,128)(2,1)}, u32[]{:S(2)}, u32[]{:S(2)}) %collective-permute-start.28) | collective-permute-done | bytes 1441824 | tf_op jit(solution)/shard_map/ppermute | solution.py:48
  288.1 28.5 %collective-permute-done.30 = bf16[256,2816]{1,0:T(8,128)(2,1)S(1)} collective-permute-done((bf16[256,2816]{1,0:T(8,128)(2,1)}, bf16[256,2816]{1,0:T(8,128)(2,1)S(1)}, u32[]{:S(2)}, u32[]{:S(2)}) %collective-permute-start.30) | collective-permute-done | bytes 1441824 | tf_op jit(solution)/shard_map/ppermute | solution.py:48
  321.6 31.3 %collective-permute-done.32 = bf16[256,2816]{1,0:T(8,128)(2,1)S(1)} collective-permute-done((bf16[256,2816]{1,0:T(8,128)(2,1)S(1)}, bf16[256,2816]{1,0:T(8,128)(2,1)S(1)}, u32[]{:S(2)}, u32[]{:S(2)}) %collective-permute-start.32) | collective-permute-done | bytes 1441824 | tf_op jit(solution)/shard_map/ppermute | solution.py:48
  354.8 11.4 collective-permute-done.35
  368.1 15.9 %collective-permute-done.37 = bf16[176,2048]{1,0:T(8,128)(2,1)S(1)} collective-permute-done((bf16[176,2048]{1,0:T(8,128)(2,1)S(1)}, bf16[176,2048]{1,0:T(8,128)(2,1)S(1)}, u32[]{:S(2)}, u32[]{:S(2)}) %collective-permute-start.37) | collective-permute-done | bytes 720928 | tf_op jit(solution)/shard_map/ppermute | solution.py:48
  384.2 15.9 %collective-permute-done.34 = bf16[176,2048]{1,0:T(8,128)(2,1)S(1)} collective-permute-done((bf16[176,2048]{1,0:T(8,128)(2,1)S(1)}, bf16[176,2048]{1,0:T(8,128)(2,1)S(1)}, u32[]{:S(2)}, u32[]{:S(2)}) %collective-permute-start.34) | collective-permute-done | bytes 720928 | tf_op jit(solution)/shard_map/ppermute | solution.py:48
  404.4 3.6 copy-done.61
  409.0 18.8 %fusion.29 = f32[1024,2816]{1,0:T(8,128)S(1)} fusion(bf16[2048,2816]{1,0:T(8,128)(2,1)} %copy-done.61, bf16[256,2048]{1,0:T(8,128)(2,1)} %collective-permute-done.26, bf16[256,2048]{1,0:T(8,128)(2,1)} %copy-done.93, bf16[256,2048]{1,0:T(8,128)(2,1)} %copy-done.94, bf16[256,2048]{1,0:T(8,128)(2,1)} %copy-done.82), kind=kOutput, calls=%fused_computation.144 | convolution fusion | flops 11827937280 | bytes 27262976 | tf_op jit(solution)/shard_map/dot_general | solution.py:11
  429.9 3.8 copy-done.7
  437.1 7.9 collective-permute-done.40
  445.7 6.7 fusion.86
  457.7 23.2 %collective-permute-done.43 = bf16[256,2048]{1,0:T(8,128)(2,1)S(1)} collective-permute-done((bf16[256,2048]{1,0:T(8,128)(2,1)S(1)}, bf16[256,2048]{1,0:T(8,128)(2,1)S(1)}, u32[]{:S(2)}, u32[]{:S(2)}) %collective-permute-start.43) | collective-permute-done | bytes 1048608 | tf_op jit(solution)/shard_map/ppermute | solution.py:48
  485.5 23.0 %collective-permute-done.45 = bf16[256,2048]{1,0:T(8,128)(2,1)S(1)} collective-permute-done((bf16[256,2048]{1,0:T(8,128)(2,1)S(1)}, bf16[256,2048]{1,0:T(8,128)(2,1)S(1)}, u32[]{:S(2)}, u32[]{:S(2)}) %collective-permute-start.45) | collective-permute-done | bytes 1048608 | tf_op jit(solution)/shard_map/ppermute | solution.py:48
  511.3 16.6 %multiply_convert_fusion.2 = (bf16[1024,1408]{1,0:T(8,128)(2,1)}, bf16[1024,1408]{1,0:T(8,128)(2,1)}) fusion(f32[1024,2816]{1,0:T(8,128)} %copy-done.7, bf16[1408,2048]{1,0:T(8,128)(2,1)} %copy-done.65, bf16[256,2048]{1,0:T(8,128)(2,1)} %collective-permute-done.46, bf16[256,2048]{1,0:T(8,128)(2,1)S(1)} %collective-permute-done.45, ...), kind=kOutput, calls=%fused_computation.10 | convolution fusion | flops 5941100544 | bytes 27262976 | tf_op jit(solution)/shard_map/dot_general | solution.py:11
  527.9 19.4 %fusion.87 = (bf16[1024,2048]{1,0:T(8,128)(2,1)}, f32[1024,2048]{1,0:T(8,128)}) fusion(bf16[2048,2816]{1,0:T(8,128)(2,1)} %copy-done.61, bf16[1024,1408]{1,0:T(8,128)(2,1)} %get-tuple-element.149, bf16[1024,1408]{1,0:T(8,128)(2,1)} %get-tuple-element.148), kind=kOutput, calls=%fused_computation.501 | convolution fusion | flops 11824791552 | bytes 29884416 | tf_op jit(solution)/shard_map/dot_general | solution.py:11
  550.7 7.7 convolution_convert_fusion.2
  564.3 18.5 %convolution_convert_fusion = bf16[2048,2816]{1,0:T(8,128)(2,1)} fusion(bf16[1024,1408]{1,0:T(8,128)(2,1)} %get-tuple-element.149, bf16[1024,1408]{1,0:T(8,128)(2,1)} %get-tuple-element.148, bf16[256,2048]{1,0:T(8,128)(2,1)} %collective-permute-done.26, bf16[256,2048]{1,0:T(8,128)(2,1)} %copy-done.93, bf16[256,2048]{1,0:T(8,128)(2,1)} %copy-done.94, ...), kind=kOutput, calls=%fused_computation.5 | convolution fusion | flops 11845238784 | bytes 21495808 | tf_op jit(solution)/shard_map/dot_general | solution.py:11
  583.5 13.4 %collective-permute-done.61 = bf16[176,2048]{1,0:T(8,128)(2,1)S(1)} collective-permute-done((bf16[176,2048]{1,0:T(8,128)(2,1)}, bf16[176,2048]{1,0:T(8,128)(2,1)S(1)}, u32[]{:S(2)}, u32[]{:S(2)}) %collective-permute-start.61) | collective-permute-done | bytes 720928 | tf_op jit(solution)/shard_map/ppermute | solution.py:48
  602.6 5.3 fusion.74
  607.8 8.8 collective-permute-done.64
  618.4 8.6 collective-permute-done.62
  638.1 19.8 %collective-permute-done.51 = bf16[256,2048]{1,0:T(8,128)(2,1)} collective-permute-done((bf16[256,2048]{1,0:T(8,128)(2,1)}, bf16[256,2048]{1,0:T(8,128)(2,1)}, u32[]{:S(2)}, u32[]{:S(2)}) %collective-permute-start.51) | collective-permute-done | bytes 1048608 | tf_op jit(solution)/shard_map/ppermute | solution.py:48
  662.5 30.3 %collective-permute-done.63 = bf16[256,2816]{1,0:T(8,128)(2,1)} collective-permute-done((bf16[256,2816]{1,0:T(8,128)(2,1)}, bf16[256,2816]{1,0:T(8,128)(2,1)}, u32[]{:S(2)}, u32[]{:S(2)}) %collective-permute-start.63) | collective-permute-done | bytes 1441824 | tf_op jit(solution)/shard_map/ppermute | solution.py:48
  701.7 6.4 multiply_convert_fusion.4
  710.4 7.5 convolution_convert_fusion.4
  717.9 15.3 %fusion.20 = (f32[4,1024]{1,0:T(4,128)S(1)}, f32[4,1024]{1,0:T(4,128)S(1)}, f32[4,1024,1024]{2,1,0:T(8,128)}) fusion(f32[4,1024,1024]{2,1,0:T(8,128)} %copy-done.5, f32[4,1024]{1,0:T(4,128)S(1)} %bitcast.241, pred[1024,1024]{1,0:T(8,128)(4,1)S(1)} %copy-done.53, bf16[4,1024,128]{1,2,0:T(8,128)(2,1)S(1)} %fusion.8, bf16[4,1024,128]{1,2,0:T(8,128)(2,1)S(1)} %bitcast.229), kind=kOutput, calls=%fused_computation.96 | convolution fusion | flops 1103093760 | bytes 36749312 | tf_op jit(solution)/shard_map/dot_general | solution.py:17
  733.2 10.7 convolution_convert_fusion.5
  743.9 10.0 multiply_convert_fusion.5
  753.9 5.0 reduce-window.16
  759.5 4.6 fusion.88
  764.1 4.7 fusion.46
  770.3 16.6 %convolution_add_fusion = f32[1024,2048]{1,0:T(8,128)} fusion(f32[1024,2048]{1,0:T(8,128)} %fusion.46, bf16[2048,2048]{1,0:T(8,128)(2,1)} %constant_dynamic-update-slice_fusion.24, bf16[1024,512]{0,1:T(8,128)(2,1)} %bitcast.230, bf16[1024,512]{0,1:T(8,128)(2,1)} %bitcast.251, bf16[1024,512]{0,1:T(8,128)(2,1)} %bitcast.253, bf16[1024,512]{0,1:T(8,128)(2,1)} %bitcast.255), kind=kOutput, calls=%fused_computation.23 | convolution fusion | flops 8608808960 | bytes 29360128 | tf_op jit(solution)/shard_map/dot_general | solution.py:11
  787.0 12.0 %convolution_convert_fusion.1 = bf16[2048,2048]{0,1:T(8,128)(2,1)S(1)} fusion(bf16[1024,512]{0,1:T(8,128)(2,1)} %bitcast.231, bf16[1024,512]{0,1:T(8,128)(2,1)} %bitcast.252, bf16[1024,512]{0,1:T(8,128)(2,1)} %bitcast.254, bf16[1024,512]{0,1:T(8,128)(2,1)} %bitcast.256, bf16[256,2048]{1,0:T(8,128)(2,1)} %copy-done.45, bf16[256,2048]{1,0:T(8,128)(2,1)} %copy-done.47, ...), kind=kOutput, calls=%fused_computation.6 | convolution fusion | flops 8627683328 | bytes 16777216 | tf_op jit(solution)/shard_map/dot_general | solution.py:11
  802.2 4.5 convolution_convert_fusion.3
  816.5 3.8 add_convert_fusion.4
  822.7 3.9 dynamic-slice_convert_fusion.1
  830.3 25.6 %collective-permute-done.68 = bf16[256,2816]{1,0:T(8,128)(2,1)} collective-permute-done((bf16[256,2816]{1,0:T(8,128)(2,1)}, bf16[256,2816]{1,0:T(8,128)(2,1)}, u32[]{:S(2)}, u32[]{:S(2)}) %collective-permute-start.68) | collective-permute-done | bytes 1441824 | tf_op jit(solution)/shard_map/ppermute | solution.py:48
  868.6 35.8 %collective-permute-done.69 = bf16[128,2048]{1,0:T(8,128)(2,1)S(1)} collective-permute-done((bf16[128,2048]{1,0:T(8,128)(2,1)S(1)}, bf16[128,2048]{1,0:T(8,128)(2,1)S(1)}, u32[]{:S(2)}, u32[]{:S(2)}) %collective-permute-start.69) | collective-permute-done | bytes 524320 | tf_op jit(solution)/shard_map/ppermute | solution.py:48
  906.9 11.6 collective-permute-done.72
  918.7 3.5 add_convert_fusion
  923.7 7.9 collective-permute-done.74
  933.1 20.3 %collective-permute-done.94 = bf16[256,2816]{1,0:T(8,128)(2,1)} collective-permute-done((bf16[256,2816]{1,0:T(8,128)(2,1)}, bf16[256,2816]{1,0:T(8,128)(2,1)}, u32[]{:S(2)}, u32[]{:S(2)}) %collective-permute-start.94) | collective-permute-done | bytes 1441824 | tf_op jit(solution)/shard_map/ppermute | solution.py:48
  956.5 57.4 %all-reduce.16 = (f32[16]{0:T(128)}, f32[2048]{0:T(1024)}, f32[2048]{0:T(1024)}, f32[]{:T(128)}, f32[]{:T(128)}) all-reduce(f32[16]{0:T(128)S(1)} %reshape.274, f32[2048]{0:T(1024)S(1)} %get-tuple-element.129, f32[2048]{0:T(1024)S(1)} %get-tuple-element.127, f32[]{:T(128)} %get-tuple-element.136, ...), channel_id=1, replica_groups=mesh['dp'=8,'seq'=4] {'dp','seq'}, use_global_device_ids=true, to_apply=%region_13.14 | all-reduce | flops 4114 | bytes 32912 | tf_op jit(solution)/shard_map/psum | solution.py:492
  1028.1 14.2 %collective-permute-done.78 = bf16[256,2048]{0,1:T(8,128)(2,1)S(1)} collective-permute-done((bf16[256,2048]{0,1:T(8,128)(2,1)}, bf16[256,2048]{0,1:T(8,128)(2,1)S(1)}, u32[]{:S(2)}, u32[]{:S(2)}) %collective-permute-start.78) | collective-permute-done | bytes 1048608 | tf_op jit(solution)/shard_map/ppermute | solution.py:48
  1042.3 6.6 collective-permute-done.77
  1054.2 8.3 collective-permute-done.80
  1062.5 12.3 %collective-permute-done.79 = bf16[256,2048]{0,1:T(8,128)(2,1)S(1)} collective-permute-done((bf16[256,2048]{0,1:T(8,128)(2,1)S(1)}, bf16[256,2048]{0,1:T(8,128)(2,1)S(1)}, u32[]{:S(2)}, u32[]{:S(2)}) %collective-permute-start.79) | collective-permute-done | bytes 1048608 | tf_op jit(solution)/shard_map/ppermute | solution.py:48
  1085.1 12.6 %collective-permute-done.82 = bf16[256,2048]{0,1:T(8,128)(2,1)} collective-permute-done((bf16[256,2048]{0,1:T(8,128)(2,1)S(1)}, bf16[256,2048]{0,1:T(8,128)(2,1)}, u32[]{:S(2)}, u32[]{:S(2)}) %collective-permute-start.82) | collective-permute-done | bytes 1048608 | tf_op jit(solution)/shard_map/ppermute | solution.py:48
  1102.6 11.6 concatenate.180
  1114.2 7.7 convert_element_type.551
  1166.1 7.0 copy.54
  (677 shorter events, 343.6 us)
Async XLA Ops:
  24.5 74.3 %collective-permute-start.4 = (bf16[256,2048]{1,0:T(8,128)(2,1)}, bf16[256,2048]{1,0:T(8,128)(2,1)}, u32[]{:S(2)}, u32[]{:S(2)}) collective-permute-start(bf16[256,2048]{1,0:T(8,128)(2,1)} %get-tuple-element.205), channel_id=1, source_target_pairs={{0,8},{4,12},{8,16},{12,20},{16,24},{20,28},{24,0},{28,4},{1,9},{5... | collective-permute-start | bytes 3145736 | tf_op jit(solution)/shard_map/ppermute | solution.py:48
  27.5 74.4 %collective-permute-start.3 = (bf16[256,2048]{1,0:T(8,128)(2,1)}, bf16[256,2048]{1,0:T(8,128)(2,1)}, u32[]{:S(2)}, u32[]{:S(2)}) collective-permute-start(bf16[256,2048]{1,0:T(8,128)(2,1)} %get-tuple-element.205), channel_id=1, source_target_pairs={{0,4},{4,0},{8,12},{12,8},{16,20},{20,16},{24,28},{28,24},{1,5},{5... | collective-permute-start | bytes 3145736 | tf_op jit(solution)/shard_map/ppermute | solution.py:48
  29.0 49.8 %collective-permute-start.13 = (bf16[256,16]{0,1:T(8,128)(2,1)}, bf16[256,16]{0,1:T(8,128)(2,1)S(1)}, u32[]{:S(2)}, u32[]{:S(2)}) collective-permute-start(bf16[256,16]{0,1:T(8,128)(2,1)} %param.19), channel_id=1, source_target_pairs={{0,4},{4,0},{8,12},{12,8},{16,20},{20,16},{24,28},{28,24},{1,5},{5... | collective-permute-start | bytes 24584 | tf_op jit(solution)/shard_map/ppermute | solution.py:48
  30.2 65.3 %collective-permute-start.11 = (s32[256,128]{0,1:T(8,128)S(1)}, s32[256,128]{0,1:T(8,128)}, u32[]{:S(2)}, u32[]{:S(2)}) collective-permute-start(s32[256,128]{0,1:T(8,128)S(1)} %broadcast_in_dim.63), channel_id=1, source_target_pairs={{0,2},{1,3},{2,0},{3,1},{4,6},{5,7},{6,4},{7,5},{8,10},{9,11},{10,... | collective-permute-start | bytes 393224 | tf_op jit(solution)/shard_map/ppermute | solution.py:48
  39.3 59.0 %collective-permute-start.1 = (bf16[256,2048]{1,0:T(8,128)(2,1)}, bf16[256,2048]{1,0:T(8,128)(2,1)}, u32[]{:S(2)}, u32[]{:S(2)}) collective-permute-start(bf16[256,2048]{1,0:T(8,128)(2,1)} %constant_dynamic-update-slice_fusion), channel_id=1, source_target_pairs={{0,2},{1,3},{2,0},{3,1},{4,6},{5,7},{6,4},{7,5},{8,10},{9,11},{10,... | collective-permute-start | bytes 3145736 | tf_op jit(solution)/shard_map/ppermute | solution.py:48
  96.8 30.8 %collective-permute-start = (bf16[256,2048]{1,0:T(8,128)(2,1)}, bf16[256,2048]{1,0:T(8,128)(2,1)S(1)}, u32[]{:S(2)}, u32[]{:S(2)}) collective-permute-start(bf16[256,2048]{1,0:T(8,128)(2,1)} %constant_dynamic-update-slice_fusion), channel_id=1, source_target_pairs={{0,1},{1,0},{2,3},{3,2},{4,5},{5,4},{6,7},{7,6},{8,9},{9,8},{10,11... | collective-permute-start | bytes 3145736 | tf_op jit(solution)/shard_map/ppermute | solution.py:48
  98.3 29.3 %collective-permute-start.2 = (bf16[256,2048]{1,0:T(8,128)(2,1)}, bf16[256,2048]{1,0:T(8,128)(2,1)S(1)}, u32[]{:S(2)}, u32[]{:S(2)}) collective-permute-start(bf16[256,2048]{1,0:T(8,128)(2,1)} %collective-permute-done.1), channel_id=1, source_target_pairs={{0,1},{1,0},{2,3},{3,2},{4,5},{5,4},{6,7},{7,6},{8,9},{9,8},{10,11... | collective-permute-start | bytes 3145736 | tf_op jit(solution)/shard_map/ppermute | solution.py:48
  98.7 27.3 %collective-permute-start.6 = (bf16[256,2048]{1,0:T(8,128)(2,1)}, bf16[256,2048]{1,0:T(8,128)(2,1)}, u32[]{:S(2)}, u32[]{:S(2)}) collective-permute-start(bf16[256,2048]{1,0:T(8,128)(2,1)} %collective-permute-done.4), channel_id=1, source_target_pairs={{0,8},{4,12},{8,16},{12,20},{16,24},{20,28},{24,0},{28,4},{1,9},{5... | collective-permute-start | bytes 3145736 | tf_op jit(solution)/shard_map/ppermute | solution.py:48
  100.4 54.1 %collective-permute-start.5 = (bf16[256,2048]{1,0:T(8,128)(2,1)}, bf16[256,2048]{1,0:T(8,128)(2,1)}, u32[]{:S(2)}, u32[]{:S(2)}) collective-permute-start(bf16[256,2048]{1,0:T(8,128)(2,1)} %collective-permute-done.4), channel_id=1, source_target_pairs={{0,4},{4,0},{8,12},{12,8},{16,20},{20,16},{24,28},{28,24},{1,5},{5... | collective-permute-start | bytes 3145736 | tf_op jit(solution)/shard_map/ppermute | solution.py:48
  126.1 33.1 %collective-permute-start.8 = (bf16[256,2048]{1,0:T(8,128)(2,1)}, bf16[256,2048]{1,0:T(8,128)(2,1)}, u32[]{:S(2)}, u32[]{:S(2)}) collective-permute-start(bf16[256,2048]{1,0:T(8,128)(2,1)} %collective-permute-done.6), channel_id=1, source_target_pairs={{0,8},{4,12},{8,16},{12,20},{16,24},{20,28},{24,0},{28,4},{1,9},{5... | collective-permute-start | bytes 3145736 | tf_op jit(solution)/shard_map/ppermute | solution.py:48
  126.1 24.7 %collective-permute-start.7 = (bf16[256,2048]{1,0:T(8,128)(2,1)}, bf16[256,2048]{1,0:T(8,128)(2,1)}, u32[]{:S(2)}, u32[]{:S(2)}) collective-permute-start(bf16[256,2048]{1,0:T(8,128)(2,1)} %collective-permute-done.6), channel_id=1, source_target_pairs={{0,4},{4,0},{8,12},{12,8},{16,20},{20,16},{24,28},{28,24},{1,5},{5... | collective-permute-start | bytes 3145736 | tf_op jit(solution)/shard_map/ppermute | solution.py:48
  159.2 26.5 %collective-permute-start.9 = (bf16[256,2048]{1,0:T(8,128)(2,1)}, bf16[256,2048]{1,0:T(8,128)(2,1)S(1)}, u32[]{:S(2)}, u32[]{:S(2)}) collective-permute-start(bf16[256,2048]{1,0:T(8,128)(2,1)} %collective-permute-done.8), channel_id=1, source_target_pairs={{0,4},{4,0},{8,12},{12,8},{16,20},{20,16},{24,28},{28,24},{1,5},{5... | collective-permute-start | bytes 3145736 | tf_op jit(solution)/shard_map/ppermute | solution.py:48
  179.0 38.8 %collective-permute-start.19 = (bf16[128,2048]{1,0:T(8,128)(2,1)}, bf16[128,2048]{1,0:T(8,128)(2,1)}, u32[]{:S(2)}, u32[]{:S(2)}) collective-permute-start(bf16[128,2048]{1,0:T(8,128)(2,1)} %collective-permute-done.18), channel_id=1, source_target_pairs={{0,8},{4,12},{8,16},{12,20},{16,24},{20,28},{24,0},{28,4},{1,9},{5... | collective-permute-start | bytes 1572872 | tf_op jit(solution)/shard_map/ppermute | solution.py:48
  245.3 36.0 %collective-permute-start.28 = (bf16[256,2816]{1,0:T(8,128)(2,1)S(1)}, bf16[256,2816]{1,0:T(8,128)(2,1)}, u32[]{:S(2)}, u32[]{:S(2)}) collective-permute-start(bf16[256,2816]{1,0:T(8,128)(2,1)S(1)} %concatenate.151), channel_id=1, source_target_pairs={{0,8},{4,12},{8,16},{12,20},{16,24},{20,28},{24,0},{28,4},{1,9},{5... | collective-permute-start | bytes 4325384 | tf_op jit(solution)/shard_map/ppermute | solution.py:48
  245.4 35.9 %collective-permute-start.27 = (bf16[256,2816]{1,0:T(8,128)(2,1)S(1)}, bf16[256,2816]{1,0:T(8,128)(2,1)}, u32[]{:S(2)}, u32[]{:S(2)}) collective-permute-start(bf16[256,2816]{1,0:T(8,128)(2,1)S(1)} %concatenate.151), channel_id=1, source_target_pairs={{0,4},{4,0},{8,12},{12,8},{16,20},{20,16},{24,28},{28,24},{1,5},{5... | collective-permute-start | bytes 4325384 | tf_op jit(solution)/shard_map/ppermute | solution.py:48
  247.1 37.4 %collective-permute-start.21 = (bf16[256,2048]{1,0:T(8,128)(2,1)}, bf16[256,2048]{1,0:T(8,128)(2,1)}, u32[]{:S(2)}, u32[]{:S(2)}) collective-permute-start(bf16[256,2048]{1,0:T(8,128)(2,1)} %get-tuple-element.160), channel_id=1, source_target_pairs={{0,1},{1,0},{2,3},{3,2},{4,5},{5,4},{6,7},{7,6},{8,9},{9,8},{10,11... | collective-permute-start | bytes 3145736 | tf_op jit(solution)/shard_map/ppermute | solution.py:48
  250.6 34.0 %collective-permute-start.23 = (bf16[256,2048]{1,0:T(8,128)(2,1)}, bf16[256,2048]{1,0:T(8,128)(2,1)}, u32[]{:S(2)}, u32[]{:S(2)}) collective-permute-start(bf16[256,2048]{1,0:T(8,128)(2,1)} %add_convert_fusion.15), channel_id=1, source_target_pairs={{0,2},{1,3},{2,0},{3,1},{4,6},{5,7},{6,4},{7,5},{8,10},{9,11},{10,... | collective-permute-start | bytes 3145736 | tf_op jit(solution)/shard_map/ppermute | solution.py:48
  281.3 35.3 %collective-permute-start.30 = (bf16[256,2816]{1,0:T(8,128)(2,1)}, bf16[256,2816]{1,0:T(8,128)(2,1)S(1)}, u32[]{:S(2)}, u32[]{:S(2)}) collective-permute-start(bf16[256,2816]{1,0:T(8,128)(2,1)} %collective-permute-done.28), channel_id=1, source_target_pairs={{0,8},{4,12},{8,16},{12,20},{16,24},{20,28},{24,0},{28,4},{1,9},{5... | collective-permute-start | bytes 4325384 | tf_op jit(solution)/shard_map/ppermute | solution.py:48
  282.8 38.7 %collective-permute-start.29 = (bf16[256,2816]{1,0:T(8,128)(2,1)}, bf16[256,2816]{1,0:T(8,128)(2,1)S(1)}, u32[]{:S(2)}, u32[]{:S(2)}) collective-permute-start(bf16[256,2816]{1,0:T(8,128)(2,1)} %collective-permute-done.28), channel_id=1, source_target_pairs={{0,4},{4,0},{8,12},{12,8},{16,20},{20,16},{24,28},{28,24},{1,5},{5... | collective-permute-start | bytes 4325384 | tf_op jit(solution)/shard_map/ppermute | solution.py:48
  316.6 36.3 %collective-permute-start.32 = (bf16[256,2816]{1,0:T(8,128)(2,1)S(1)}, bf16[256,2816]{1,0:T(8,128)(2,1)S(1)}, u32[]{:S(2)}, u32[]{:S(2)}) collective-permute-start(bf16[256,2816]{1,0:T(8,128)(2,1)S(1)} %collective-permute-done.30), channel_id=1, source_target_pairs={{0,8},{4,12},{8,16},{12,20},{16,24},{20,28},{24,0},{28,4},{1,9},{5... | collective-permute-start | bytes 4325384 | tf_op jit(solution)/shard_map/ppermute | solution.py:48
  316.7 49.5 %collective-permute-start.31 = (bf16[256,2816]{1,0:T(8,128)(2,1)S(1)}, bf16[256,2816]{1,0:T(8,128)(2,1)S(1)}, u32[]{:S(2)}, u32[]{:S(2)}) collective-permute-start(bf16[256,2816]{1,0:T(8,128)(2,1)S(1)} %collective-permute-done.30), channel_id=1, source_target_pairs={{0,4},{4,0},{8,12},{12,8},{16,20},{20,16},{24,28},{28,24},{1,5},{5... | collective-permute-start | bytes 4325384 | tf_op jit(solution)/shard_map/ppermute | solution.py:48
  318.5 36.2 %collective-permute-start.25 = (bf16[256,2048]{1,0:T(8,128)(2,1)S(1)}, bf16[256,2048]{1,0:T(8,128)(2,1)S(1)}, u32[]{:S(2)}, u32[]{:S(2)}) collective-permute-start(bf16[256,2048]{1,0:T(8,128)(2,1)S(1)} %constant_dynamic-update-slice_fusion.51), channel_id=1, source_target_pairs={{0,2},{1,3},{2,0},{3,1},{4,6},{5,7},{6,4},{7,5},{8,10},{9,11},{10,... | collective-permute-start | bytes 3145736 | tf_op jit(solution)/shard_map/ppermute | solution.py:48
  321.4 81.1 %collective-permute-start.24 = (bf16[256,2048]{1,0:T(8,128)(2,1)S(1)}, bf16[256,2048]{1,0:T(8,128)(2,1)S(1)}, u32[]{:S(2)}, u32[]{:S(2)}) collective-permute-start(bf16[256,2048]{1,0:T(8,128)(2,1)S(1)} %constant_dynamic-update-slice_fusion.51), channel_id=1, source_target_pairs={{0,1},{1,0},{2,3},{3,2},{4,5},{5,4},{6,7},{7,6},{8,9},{9,8},{10,11... | collective-permute-start | bytes 3145736 | tf_op jit(solution)/shard_map/ppermute | solution.py:48
  321.4 44.7 %collective-permute-start.35 = (bf16[176,2048]{1,0:T(8,128)(2,1)S(1)}, bf16[176,2048]{1,0:T(8,128)(2,1)S(1)}, u32[]{:S(2)}, u32[]{:S(2)}) collective-permute-start(bf16[176,2048]{1,0:T(8,128)(2,1)S(1)} %get-tuple-element.72), channel_id=1, source_target_pairs={{0,8},{4,12},{8,16},{12,20},{16,24},{20,28},{24,0},{28,4},{1,9},{5... | collective-permute-start | bytes 2162696 | tf_op jit(solution)/shard_map/ppermute | solution.py:48
  352.9 49.0 %collective-permute-start.33 = (bf16[256,2816]{1,0:T(8,128)(2,1)S(1)}, bf16[256,2816]{1,0:T(8,128)(2,1)S(1)}, u32[]{:S(2)}, u32[]{:S(2)}) collective-permute-start(bf16[256,2816]{1,0:T(8,128)(2,1)S(1)} %collective-permute-done.32), channel_id=1, source_target_pairs={{0,4},{4,0},{8,12},{12,8},{16,20},{20,16},{24,28},{28,24},{1,5},{5... | collective-permute-start | bytes 4325384 | tf_op jit(solution)/shard_map/ppermute | solution.py:48
  354.7 54.3 %collective-permute-start.26 = (bf16[256,2048]{1,0:T(8,128)(2,1)S(1)}, bf16[256,2048]{1,0:T(8,128)(2,1)}, u32[]{:S(2)}, u32[]{:S(2)}) collective-permute-start(bf16[256,2048]{1,0:T(8,128)(2,1)S(1)} %collective-permute-done.25), channel_id=1, source_target_pairs={{0,1},{1,0},{2,3},{3,2},{4,5},{5,4},{6,7},{7,6},{8,9},{9,8},{10,11... | collective-permute-start | bytes 3145736 | tf_op jit(solution)/shard_map/ppermute | solution.py:48
  366.2 33.9 %collective-permute-start.34 = (bf16[176,2048]{1,0:T(8,128)(2,1)S(1)}, bf16[176,2048]{1,0:T(8,128)(2,1)S(1)}, u32[]{:S(2)}, u32[]{:S(2)}) collective-permute-start(bf16[176,2048]{1,0:T(8,128)(2,1)S(1)} %get-tuple-element.72), channel_id=1, source_target_pairs={{0,4},{4,0},{8,12},{12,8},{16,20},{20,16},{24,28},{28,24},{1,5},{5... | collective-permute-start | bytes 2162696 | tf_op jit(solution)/shard_map/ppermute | solution.py:48
  384.0 49.7 %collective-permute-start.39 = (bf16[176,2048]{1,0:T(8,128)(2,1)S(1)}, bf16[176,2048]{1,0:T(8,128)(2,1)S(1)}, u32[]{:S(2)}, u32[]{:S(2)}) collective-permute-start(bf16[176,2048]{1,0:T(8,128)(2,1)S(1)} %collective-permute-done.37), channel_id=1, source_target_pairs={{0,8},{4,12},{8,16},{12,20},{16,24},{20,28},{24,0},{28,4},{1,9},{5... | collective-permute-start | bytes 2162696 | tf_op jit(solution)/shard_map/ppermute | solution.py:48
  400.1 35.8 %collective-permute-start.38 = (bf16[176,2048]{1,0:T(8,128)(2,1)S(1)}, bf16[176,2048]{1,0:T(8,128)(2,1)}, u32[]{:S(2)}, u32[]{:S(2)}) collective-permute-start(bf16[176,2048]{1,0:T(8,128)(2,1)S(1)} %collective-permute-done.37), channel_id=1, source_target_pairs={{0,4},{4,0},{8,12},{12,8},{16,20},{20,16},{24,28},{28,24},{1,5},{5... | collective-permute-start | bytes 2162696 | tf_op jit(solution)/shard_map/ppermute | solution.py:48
  401.9 31.8 %collective-permute-start.36 = (bf16[176,2048]{1,0:T(8,128)(2,1)S(1)}, bf16[176,2048]{1,0:T(8,128)(2,1)}, u32[]{:S(2)}, u32[]{:S(2)}) collective-permute-start(bf16[176,2048]{1,0:T(8,128)(2,1)S(1)} %collective-permute-done.35), channel_id=1, source_target_pairs={{0,4},{4,0},{8,12},{12,8},{16,20},{20,16},{24,28},{28,24},{1,5},{5... | collective-permute-start | bytes 2162696 | tf_op jit(solution)/shard_map/ppermute | solution.py:48
  455.6 25.3 %collective-permute-start.43 = (bf16[256,2048]{1,0:T(8,128)(2,1)S(1)}, bf16[256,2048]{1,0:T(8,128)(2,1)S(1)}, u32[]{:S(2)}, u32[]{:S(2)}) collective-permute-start(bf16[256,2048]{1,0:T(8,128)(2,1)S(1)} %fusion.11), channel_id=1, source_target_pairs={{0,2},{1,3},{2,0},{3,1},{4,6},{5,7},{6,4},{7,5},{8,10},{9,11},{10,... | collective-permute-start | bytes 3145736 | tf_op jit(solution)/shard_map/ppermute | solution.py:48
  550.1 79.0 %collective-permute-start.47 = (bf16[256,2048]{1,0:T(8,128)(2,1)S(1)}, bf16[256,2048]{1,0:T(8,128)(2,1)S(1)}, u32[]{:S(2)}, u32[]{:S(2)}) collective-permute-start(bf16[256,2048]{1,0:T(8,128)(2,1)S(1)} %get-tuple-element.195), channel_id=1, source_target_pairs={{0,1},{1,0},{2,3},{3,2},{4,5},{5,4},{6,7},{7,6},{8,9},{9,8},{10,11... | collective-permute-start | bytes 3145736 | tf_op jit(solution)/shard_map/ppermute | solution.py:48
  550.3 48.7 %collective-permute-start.48 = (bf16[256,2048]{1,0:T(8,128)(2,1)}, bf16[256,2048]{1,0:T(8,128)(2,1)}, u32[]{:S(2)}, u32[]{:S(2)}) collective-permute-start(bf16[256,2048]{1,0:T(8,128)(2,1)} %get-tuple-element.196), channel_id=1, source_target_pairs={{0,1},{1,0},{2,3},{3,2},{4,5},{5,4},{6,7},{7,6},{8,9},{9,8},{10,11... | collective-permute-start | bytes 3145736 | tf_op jit(solution)/shard_map/ppermute | solution.py:48
  562.9 34.1 %collective-permute-start.61 = (bf16[176,2048]{1,0:T(8,128)(2,1)}, bf16[176,2048]{1,0:T(8,128)(2,1)S(1)}, u32[]{:S(2)}, u32[]{:S(2)}) collective-permute-start(bf16[176,2048]{1,0:T(8,128)(2,1)} %get-tuple-element.83), channel_id=1, source_target_pairs={{0,4},{4,0},{8,12},{12,8},{16,20},{20,16},{24,28},{28,24},{1,5},{5... | collective-permute-start | bytes 2162696 | tf_op jit(solution)/shard_map/ppermute | solution.py:48
  582.9 44.2 %collective-permute-start.57 = (bf16[176,2048]{1,0:T(8,128)(2,1)S(1)}, bf16[176,2048]{1,0:T(8,128)(2,1)S(1)}, u32[]{:S(2)}, u32[]{:S(2)}) collective-permute-start(bf16[176,2048]{1,0:T(8,128)(2,1)S(1)} %get-tuple-element.79), channel_id=1, source_target_pairs={{0,4},{4,0},{8,12},{12,8},{16,20},{20,16},{24,28},{28,24},{1,5},{5... | collective-permute-start | bytes 2162696 | tf_op jit(solution)/shard_map/ppermute | solution.py:48
  598.3 28.7 %collective-permute-start.62 = (bf16[176,2048]{1,0:T(8,128)(2,1)}, bf16[176,2048]{1,0:T(8,128)(2,1)S(1)}, u32[]{:S(2)}, u32[]{:S(2)}) collective-permute-start(bf16[176,2048]{1,0:T(8,128)(2,1)} %get-tuple-element.84), channel_id=1, source_target_pairs={{0,4},{4,0},{8,12},{12,8},{16,20},{20,16},{24,28},{28,24},{1,5},{5... | collective-permute-start | bytes 2162696 | tf_op jit(solution)/shard_map/ppermute | solution.py:48
  601.2 28.0 %collective-permute-start.49 = (bf16[256,2048]{1,0:T(8,128)(2,1)S(1)}, bf16[256,2048]{1,0:T(8,128)(2,1)S(1)}, u32[]{:S(2)}, u32[]{:S(2)}) collective-permute-start(bf16[256,2048]{1,0:T(8,128)(2,1)S(1)} %fusion.9), channel_id=1, source_target_pairs={{0,2},{1,3},{2,0},{3,1},{4,6},{5,7},{6,4},{7,5},{8,10},{9,11},{10,... | collective-permute-start | bytes 3145736 | tf_op jit(solution)/shard_map/ppermute | solution.py:48
  627.0 34.9 %collective-permute-start.58 = (bf16[256,2816]{1,0:T(8,128)(2,1)}, bf16[256,2816]{1,0:T(8,128)(2,1)}, u32[]{:S(2)}, u32[]{:S(2)}) collective-permute-start(bf16[256,2816]{1,0:T(8,128)(2,1)} %get-tuple-element.80), channel_id=1, source_target_pairs={{0,4},{4,0},{8,12},{12,8},{16,20},{20,16},{24,28},{28,24},{1,5},{5... | collective-permute-start | bytes 4325384 | tf_op jit(solution)/shard_map/ppermute | solution.py:48
  627.7 65.2 %collective-permute-start.63 = (bf16[256,2816]{1,0:T(8,128)(2,1)}, bf16[256,2816]{1,0:T(8,128)(2,1)}, u32[]{:S(2)}, u32[]{:S(2)}) collective-permute-start(bf16[256,2816]{1,0:T(8,128)(2,1)} %get-tuple-element.85), channel_id=1, source_target_pairs={{0,4},{4,0},{8,12},{12,8},{16,20},{20,16},{24,28},{28,24},{1,5},{5... | collective-permute-start | bytes 4325384 | tf_op jit(solution)/shard_map/ppermute | solution.py:48
  638.0 58.1 %collective-permute-start.50 = (bf16[256,2048]{1,0:T(8,128)(2,1)}, bf16[256,2048]{1,0:T(8,128)(2,1)S(1)}, u32[]{:S(2)}, u32[]{:S(2)}) collective-permute-start(bf16[256,2048]{1,0:T(8,128)(2,1)} %get-tuple-element.140), channel_id=1, source_target_pairs={{0,1},{1,0},{2,3},{3,2},{4,5},{5,4},{6,7},{7,6},{8,9},{9,8},{10,11... | collective-permute-start | bytes 3145736 | tf_op jit(solution)/shard_map/ppermute | solution.py:48
  657.9 38.7 %collective-permute-start.52 = (bf16[256,2048]{1,0:T(8,128)(2,1)}, bf16[256,2048]{1,0:T(8,128)(2,1)S(1)}, u32[]{:S(2)}, u32[]{:S(2)}) collective-permute-start(bf16[256,2048]{1,0:T(8,128)(2,1)} %collective-permute-done.51), channel_id=1, source_target_pairs={{0,1},{1,0},{2,3},{3,2},{4,5},{5,4},{6,7},{7,6},{8,9},{9,8},{10,11... | collective-permute-start | bytes 3145736 | tf_op jit(solution)/shard_map/ppermute | solution.py:48
  659.9 160.4 %collective-permute-start.97 = (bf16[176,2048]{1,0:T(8,128)(2,1)S(1)}, bf16[176,2048]{1,0:T(8,128)(2,1)}, u32[]{:S(2)}, u32[]{:S(2)}) collective-permute-start(bf16[176,2048]{1,0:T(8,128)(2,1)S(1)} %add_convert_fusion.16), channel_id=1, source_target_pairs={{0,2},{1,3},{2,0},{3,1},{4,6},{5,7},{6,4},{7,5},{8,10},{9,11},{10,... | collective-permute-start | bytes 2162696 | tf_op jit(solution)/shard_map/ppermute | solution.py:48
  661.9 167.7 %collective-permute-start.59 = (bf16[256,2816]{1,0:T(8,128)(2,1)}, bf16[256,2816]{1,0:T(8,128)(2,1)}, u32[]{:S(2)}, u32[]{:S(2)}) collective-permute-start(bf16[256,2816]{1,0:T(8,128)(2,1)} %get-tuple-element.81), channel_id=1, source_target_pairs={{0,4},{4,0},{8,12},{12,8},{16,20},{20,16},{24,28},{28,24},{1,5},{5... | collective-permute-start | bytes 4325384 | tf_op jit(solution)/shard_map/ppermute | solution.py:48
  696.1 119.9 %collective-permute-start.66 = (bf16[256,2816]{1,0:T(8,128)(2,1)}, bf16[256,2816]{1,0:T(8,128)(2,1)}, u32[]{:S(2)}, u32[]{:S(2)}) collective-permute-start(bf16[256,2816]{1,0:T(8,128)(2,1)} %add_convert_fusion.6), channel_id=1, source_target_pairs={{0,8},{4,12},{8,16},{12,20},{16,24},{20,28},{24,0},{28,4},{1,9},{5... | collective-permute-start | bytes 4325384 | tf_op jit(solution)/shard_map/ppermute | solution.py:48
  696.1 134.2 %collective-permute-start.70 = (bf16[256,2816]{1,0:T(8,128)(2,1)}, bf16[256,2816]{1,0:T(8,128)(2,1)}, u32[]{:S(2)}, u32[]{:S(2)}) collective-permute-start(bf16[256,2816]{1,0:T(8,128)(2,1)} %get-tuple-element.92), channel_id=1, source_target_pairs={{0,4},{4,0},{8,12},{12,8},{16,20},{20,16},{24,28},{28,24},{1,5},{5... | collective-permute-start | bytes 4325384 | tf_op jit(solution)/shard_map/ppermute | solution.py:48
  820.4 35.6 %collective-permute-start.68 = (bf16[256,2816]{1,0:T(8,128)(2,1)}, bf16[256,2816]{1,0:T(8,128)(2,1)}, u32[]{:S(2)}, u32[]{:S(2)}) collective-permute-start(bf16[256,2816]{1,0:T(8,128)(2,1)} %add_convert_fusion.4), channel_id=1, source_target_pairs={{0,8},{4,12},{8,16},{12,20},{16,24},{20,28},{24,0},{28,4},{1,9},{5... | collective-permute-start | bytes 4325384 | tf_op jit(solution)/shard_map/ppermute | solution.py:48
  827.2 77.4 %collective-permute-start.53 = (bf16[256,2048]{1,0:T(8,128)(2,1)}, bf16[256,2048]{1,0:T(8,128)(2,1)S(1)}, u32[]{:S(2)}, u32[]{:S(2)}) collective-permute-start(bf16[256,2048]{1,0:T(8,128)(2,1)} %get-tuple-element.158), channel_id=1, source_target_pairs={{0,1},{1,0},{2,3},{3,2},{4,5},{5,4},{6,7},{7,6},{8,9},{9,8},{10,11... | collective-permute-start | bytes 3145736 | tf_op jit(solution)/shard_map/ppermute | solution.py:48
  827.3 31.5 %collective-permute-start.54 = (bf16[256,2048]{1,0:T(8,128)(2,1)}, bf16[256,2048]{1,0:T(8,128)(2,1)S(1)}, u32[]{:S(2)}, u32[]{:S(2)}) collective-permute-start(bf16[256,2048]{1,0:T(8,128)(2,1)} %get-tuple-element.159), channel_id=1, source_target_pairs={{0,1},{1,0},{2,3},{3,2},{4,5},{5,4},{6,7},{7,6},{8,9},{9,8},{10,11... | collective-permute-start | bytes 3145736 | tf_op jit(solution)/shard_map/ppermute | solution.py:48
  829.7 35.3 %collective-permute-start.60 = (bf16[256,2048]{0,1:T(8,128)(2,1)S(1)}, bf16[256,2048]{0,1:T(8,128)(2,1)S(1)}, u32[]{:S(2)}, u32[]{:S(2)}) collective-permute-start(bf16[256,2048]{0,1:T(8,128)(2,1)S(1)} %copy-done.57), channel_id=1, source_target_pairs={{0,4},{4,0},{8,12},{12,8},{16,20},{20,16},{24,28},{28,24},{1,5},{5... | collective-permute-start | bytes 3145736 | tf_op jit(solution)/shard_map/ppermute | solution.py:48
  858.7 45.9 %collective-permute-start.71 = (bf16[256,2816]{1,0:T(8,128)(2,1)S(1)}, bf16[256,2816]{1,0:T(8,128)(2,1)S(1)}, u32[]{:S(2)}, u32[]{:S(2)}) collective-permute-start(bf16[256,2816]{1,0:T(8,128)(2,1)S(1)} %add_convert_fusion.2), channel_id=1, source_target_pairs={{0,8},{4,12},{8,16},{12,20},{16,24},{20,28},{24,0},{28,4},{1,9},{5... | collective-permute-start | bytes 4325384 | tf_op jit(solution)/shard_map/ppermute | solution.py:48
  860.7 44.0 %collective-permute-start.55 = (bf16[256,2048]{1,0:T(8,128)(2,1)S(1)}, bf16[256,2048]{1,0:T(8,128)(2,1)S(1)}, u32[]{:S(2)}, u32[]{:S(2)}) collective-permute-start(bf16[256,2048]{1,0:T(8,128)(2,1)S(1)} %add_convert_fusion.14), channel_id=1, source_target_pairs={{0,2},{1,3},{2,0},{3,1},{4,6},{5,7},{6,4},{7,5},{8,10},{9,11},{10,... | collective-permute-start | bytes 3145736 | tf_op jit(solution)/shard_map/ppermute | solution.py:48
  865.0 39.5 %collective-permute-start.69 = (bf16[128,2048]{1,0:T(8,128)(2,1)S(1)}, bf16[128,2048]{1,0:T(8,128)(2,1)S(1)}, u32[]{:S(2)}, u32[]{:S(2)}) collective-permute-start(bf16[128,2048]{1,0:T(8,128)(2,1)S(1)} %copy-done.59), channel_id=1, source_target_pairs={{0,8},{4,12},{8,16},{12,20},{16,24},{20,28},{24,0},{28,4},{1,9},{5... | collective-permute-start | bytes 1572872 | tf_op jit(solution)/shard_map/ppermute | solution.py:48
  922.3 31.1 %collective-permute-start.94 = (bf16[256,2816]{1,0:T(8,128)(2,1)}, bf16[256,2816]{1,0:T(8,128)(2,1)}, u32[]{:S(2)}, u32[]{:S(2)}) collective-permute-start(bf16[256,2816]{1,0:T(8,128)(2,1)} %add_convert_fusion), channel_id=1, source_target_pairs={{0,2},{1,3},{2,0},{3,1},{4,6},{5,7},{6,4},{7,5},{8,10},{9,11},{10,... | collective-permute-start | bytes 4325384 | tf_op jit(solution)/shard_map/ppermute | solution.py:48
  932.9 91.2 %collective-permute-start.93 = (bf16[256,2816]{1,0:T(8,128)(2,1)}, bf16[256,2816]{1,0:T(8,128)(2,1)}, u32[]{:S(2)}, u32[]{:S(2)}) collective-permute-start(bf16[256,2816]{1,0:T(8,128)(2,1)} %add_convert_fusion), channel_id=1, source_target_pairs={{0,1},{1,0},{2,3},{3,2},{4,5},{5,4},{6,7},{7,6},{8,9},{9,8},{10,11... | collective-permute-start | bytes 4325384 | tf_op jit(solution)/shard_map/ppermute | solution.py:48
  933.0 88.0 %collective-permute-start.73 = (bf16[256,2048]{0,1:T(8,128)(2,1)}, bf16[256,2048]{0,1:T(8,128)(2,1)}, u32[]{:S(2)}, u32[]{:S(2)}) collective-permute-start(bf16[256,2048]{0,1:T(8,128)(2,1)} %add_convert_fusion.13), channel_id=1, source_target_pairs={{0,8},{4,12},{8,16},{12,20},{16,24},{20,28},{24,0},{28,4},{1,9},{5... | collective-permute-start | bytes 3145736 | tf_op jit(solution)/shard_map/ppermute | solution.py:48
  953.4 70.8 %collective-permute-start.95 = (bf16[256,2816]{1,0:T(8,128)(2,1)}, bf16[256,2816]{1,0:T(8,128)(2,1)}, u32[]{:S(2)}, u32[]{:S(2)}) collective-permute-start(bf16[256,2816]{1,0:T(8,128)(2,1)} %collective-permute-done.94), channel_id=1, source_target_pairs={{0,1},{1,0},{2,3},{3,2},{4,5},{5,4},{6,7},{7,6},{8,9},{9,8},{10,11... | collective-permute-start | bytes 4325384 | tf_op jit(solution)/shard_map/ppermute | solution.py:48
  953.5 61.7 %collective-permute-start.91 = (bf16[128,2048]{1,0:T(8,128)(2,1)S(1)}, bf16[128,2048]{1,0:T(8,128)(2,1)}, u32[]{:S(2)}, u32[]{:S(2)}) collective-permute-start(bf16[128,2048]{1,0:T(8,128)(2,1)S(1)} %add_convert_fusion.23), channel_id=1, source_target_pairs={{0,1},{1,0},{2,3},{3,2},{4,5},{5,4},{6,7},{7,6},{8,9},{9,8},{10,11... | collective-permute-start | bytes 1572872 | tf_op jit(solution)/shard_map/ppermute | solution.py:48
  954.1 66.2 %collective-permute-start.76 = (bf16[256,2048]{0,1:T(8,128)(2,1)}, bf16[256,2048]{0,1:T(8,128)(2,1)}, u32[]{:S(2)}, u32[]{:S(2)}) collective-permute-start(bf16[256,2048]{0,1:T(8,128)(2,1)} %get-tuple-element.98), channel_id=1, source_target_pairs={{0,4},{4,0},{8,12},{12,8},{16,20},{20,16},{24,28},{28,24},{1,5},{5... | collective-permute-start | bytes 3145736 | tf_op jit(solution)/shard_map/ppermute | solution.py:48
  1015.2 27.1 %collective-permute-start.78 = (bf16[256,2048]{0,1:T(8,128)(2,1)}, bf16[256,2048]{0,1:T(8,128)(2,1)S(1)}, u32[]{:S(2)}, u32[]{:S(2)}) collective-permute-start(bf16[256,2048]{0,1:T(8,128)(2,1)} %get-tuple-element.100), channel_id=1, source_target_pairs={{0,4},{4,0},{8,12},{12,8},{16,20},{20,16},{24,28},{28,24},{1,5},{5... | collective-permute-start | bytes 3145736 | tf_op jit(solution)/shard_map/ppermute | solution.py:48
  1020.3 101.7 %collective-permute-start.92 = (bf16[256,2048]{1,0:T(8,128)(2,1)}, bf16[256,2048]{1,0:T(8,128)(2,1)}, u32[]{:S(2)}, u32[]{:S(2)}) collective-permute-start(bf16[256,2048]{1,0:T(8,128)(2,1)} %pad_maximum_fusion.15), channel_id=1, source_target_pairs={{0,2},{1,3},{2,0},{3,1},{4,6},{5,7},{6,4},{7,5},{8,10},{9,11},{10,... | collective-permute-start | bytes 3145736 | tf_op jit(solution)/shard_map/ppermute | solution.py:48
  1021.0 41.5 %collective-permute-start.80 = (bf16[256,2048]{0,1:T(8,128)(2,1)}, bf16[256,2048]{0,1:T(8,128)(2,1)S(1)}, u32[]{:S(2)}, u32[]{:S(2)}) collective-permute-start(bf16[256,2048]{0,1:T(8,128)(2,1)} %get-tuple-element.102), channel_id=1, source_target_pairs={{0,4},{4,0},{8,12},{12,8},{16,20},{20,16},{24,28},{28,24},{1,5},{5... | collective-permute-start | bytes 3145736 | tf_op jit(solution)/shard_map/ppermute | solution.py:48
  1024.1 24.8 %collective-permute-start.77 = (bf16[256,2048]{0,1:T(8,128)(2,1)S(1)}, bf16[256,2048]{0,1:T(8,128)(2,1)S(1)}, u32[]{:S(2)}, u32[]{:S(2)}) collective-permute-start(bf16[256,2048]{0,1:T(8,128)(2,1)S(1)} %add_convert_fusion.11), channel_id=1, source_target_pairs={{0,8},{4,12},{8,16},{12,20},{16,24},{20,28},{24,0},{28,4},{1,9},{5... | collective-permute-start | bytes 3145736 | tf_op jit(solution)/shard_map/ppermute | solution.py:48
  1085.1 38.5 %collective-permute-start.81 = (bf16[256,2048]{0,1:T(8,128)(2,1)S(1)}, bf16[256,2048]{0,1:T(8,128)(2,1)}, u32[]{:S(2)}, u32[]{:S(2)}) collective-permute-start(bf16[256,2048]{0,1:T(8,128)(2,1)S(1)} %add_convert_fusion.7), channel_id=1, source_target_pairs={{0,1},{1,0},{2,3},{3,2},{4,5},{5,4},{6,7},{7,6},{8,9},{9,8},{10,11... | collective-permute-start | bytes 3145736 | tf_op jit(solution)/shard_map/ppermute | solution.py:48
  1097.7 25.9 %collective-permute-start.83 = (bf16[256,2048]{0,1:T(8,128)(2,1)}, bf16[256,2048]{0,1:T(8,128)(2,1)}, u32[]{:S(2)}, u32[]{:S(2)}) collective-permute-start(bf16[256,2048]{0,1:T(8,128)(2,1)} %collective-permute-done.82), channel_id=1, source_target_pairs={{0,1},{1,0},{2,3},{3,2},{4,5},{5,4},{6,7},{7,6},{8,9},{9,8},{10,11... | collective-permute-start | bytes 3145736 | tf_op jit(solution)/shard_map/ppermute | solution.py:48
  (139 other events, 1806.5 us)

commit v2 on v0

v2 whole, which is shorter than its diff:
```python
import functools

import jax
import jax.numpy as jnp
from jax import lax
from jax.experimental import pallas as pl
from jax.experimental.pallas import tpu as pltpu
from jax.sharding import PartitionSpec as P

LOW = jnp.bfloat16
WIDE = jnp.float32
ORDER = (2, 1, 3, 0)
EXTRA = 128
VMEM_BYTES = 56 * 1024 * 1024


def dot(left, right, left_dim=1, right_dim=0):
    return lax.dot_general(
        left, right, (((left_dim,), (right_dim,)), ((), ())), preferred_element_type=WIDE
    )


def blocks_at(matrix, places, size, axis):
    return jnp.concatenate(
        [lax.dynamic_slice_in_dim(matrix, place * size, size, axis) for place in places], axis=axis
    )


def after(value, *tokens):
    return lax.optimization_barrier((value,) + tokens)[0]


def in_vmem():
    return pl.BlockSpec(memory_space=pltpu.VMEM)


def anywhere():
    return pl.BlockSpec(memory_space=pl.ANY)


def cost(*unused):
    return pl.CostEstimate(flops=0, bytes_accessed=0, transcendentals=0)


def pieces_kernel(*refs):
    rows, pieces, target = refs[0], refs[1:-1], refs[-1]
    target[...] = dot(rows[...], jnp.concatenate([piece[...] for piece in pieces], axis=0))


def pieces_product(rows, pieces):
    depth, width = pieces[0].shape
    height, count, tile = rows.shape[0], len(pieces), 256
    return pl.pallas_call(
        pieces_kernel,
        grid=(-(-width // tile),),
        in_specs=[pl.BlockSpec((height, count * depth), lambda i: (0, 0))]
        + [pl.BlockSpec((depth, tile), lambda i: (0, i))] * count,
        out_specs=pl.BlockSpec((height, tile), lambda i: (0, i)),
        out_shape=jax.ShapeDtypeStruct((height, width), WIDE),
        compiler_params=pltpu.CompilerParams(vmem_limit_bytes=VMEM_BYTES),
        cost_estimate=cost(),
    )(rows, *pieces)


def gate_up_kernel(count, *refs):
    rows, gate_w, up_w = refs[0], refs[1 : 1 + count], refs[1 + count : 1 + 2 * count]
    gate, up, activated = refs[1 + 2 * count :]
    tile = gate.shape[1]
    left = jnp.concatenate([piece[...] for piece in gate_w], axis=0)
    right = jnp.concatenate([piece[...] for piece in up_w], axis=0)
    both = dot(rows[...], jnp.concatenate([left, right], axis=1))
    gate_part, up_part = both[:, :tile], both[:, tile:]
    gate[...] = gate_part
    up[...] = up_part
    activated[...] = (gate_part * jax.nn.sigmoid(gate_part) * up_part).astype(LOW)


def gate_up_product(rows, pieces, units):
    height, depth = rows.shape
    tile = 128
    steps, count = units // tile, len(pieces)
    column = pl.BlockSpec((height, tile), lambda i: (0, i))
    size = pieces[0].shape[0]
    return pl.pallas_call(
        functools.partial(gate_up_kernel, count),
        grid=(steps,),
        in_specs=[pl.BlockSpec((height, depth), lambda i: (0, 0))]
        + [pl.BlockSpec((size, tile), lambda i: (0, i))] * count
        + [pl.BlockSpec((size, tile), lambda i: (0, steps + i))] * count,
        out_specs=[column] * 3,
        out_shape=[
            jax.ShapeDtypeStruct((height, units), WIDE),
            jax.ShapeDtypeStruct((height, units), WIDE),
            jax.ShapeDtypeStruct((height, units), LOW),
        ],
        compiler_params=pltpu.CompilerParams(vmem_limit_bytes=VMEM_BYTES),
        cost_estimate=cost(),
    )(rows, *pieces, *pieces)


def in_row_order_kernel(*refs):
    pieces, target = refs[:-1], refs[-1]
    me = lax.axis_index("seq")
    size = pieces[0].shape[0]
    for k, piece in enumerate(pieces):
        target[pl.ds(pl.multiple_of(lax.bitwise_xor(me, k) * size, size), size), :] = piece[...]


def in_row_order(pieces):
    size, width = pieces[0].shape
    return pl.pallas_call(
        in_row_order_kernel,
        in_specs=[in_vmem()] * len(pieces),
        out_specs=in_vmem(),
        out_shape=jax.ShapeDtypeStruct((len(pieces) * size, width), LOW),
        compiler_params=pltpu.CompilerParams(vmem_limit_bytes=VMEM_BYTES),
        cost_estimate=cost(),
    )(*pieces)


def proj_share_kernel(blocks, seq_count, source, decay, target):
    me = lax.axis_index("seq")
    rows, extra = decay.shape
    size = (target.shape[1] - EXTRA) // blocks
    for i in range(blocks):
        place = pl.multiple_of((i * seq_count + me) * size, size)
        target[:, i * size : (i + 1) * size] = source[:, pl.ds(place, size)]
    padded = jnp.concatenate([decay[...], jnp.zeros((rows, EXTRA - extra), LOW)], axis=1)
    target[:, blocks * size :] = padded


def row_shares_kernel(part, shard, seq_count, out, down, out_to, down_to):
    me = lax.axis_index("seq")
    half = out_to.shape[0]
    out_to[...] = out[pl.ds(pl.multiple_of(lax.rem(me, 2) * half, half), half), :]
    sure = shard - part * (seq_count - 1)
    rest = part - sure
    start = pl.multiple_of(me * part, 16)
    down_to[:sure, :] = down[pl.ds(start, sure), :]
    if rest:
        last = pl.multiple_of(jnp.minimum(start + sure, shard - rest), 16)
        rows = down[pl.ds(last, rest), :]
        down_to[sure:, :] = jnp.where(me < seq_count - 1, rows, jnp.zeros_like(rows))


def gate_up_share_kernel(part, shard, dp_count, source, target):
    me = lax.axis_index("seq")
    lane = 128
    window = 384
    columns = source.shape[1]
    half = dp_count * part
    row = lax.broadcasted_iota(jnp.int32, (window, lane), 0)
    col = lax.broadcasted_iota(jnp.int32, (window, lane), 1)
    for tile in range(target.shape[1] // lane):
        first = tile * lane % half
        which = tile * lane // half
        total = None
        for d in range(first // part, (first + lane - 1) // part + 1):
            base = (which * dp_count + d) * shard + me * part
            begin = pl.multiple_of(
                jnp.minimum(lax.div(base, lane) * lane, (columns - window) // lane * lane), lane
            )
            unit = first + col - d * part
            hit = (row + begin == base + unit) & (unit >= 0) & (unit < part)
            hit = hit & (me * part + unit < shard)
            chosen = jnp.where(hit, 1.0, 0.0).astype(LOW)
            piece = jnp.dot(source[:, pl.ds(begin, window)], chosen, preferred_element_type=WIDE)
            total = piece if total is None else total + piece
        target[:, pl.ds(tile * lane, lane)] = total.astype(LOW)


def gate_up_whole_kernel(part, shard, *refs):
    pieces, target, held = refs[:-2], refs[-2], refs[-1]
    me = lax.axis_index("seq")
    lane, window = 128, 256
    count = len(pieces)
    for k in range(count):
        place = lax.bitwise_xor(me, k)
        held[place] = pieces[k][...]
    row = lax.broadcasted_iota(jnp.int32, (window, lane), 0)
    col = lax.broadcasted_iota(jnp.int32, (window, lane), 1)
    width = pieces[0].shape[1]
    for tile in range(target.shape[1] // lane):
        at = tile * lane
        total = None
        while at < (tile + 1) * lane:
            block, inside = divmod(at, shard)
            share, unit = divmod(inside, part)
            stop = min((tile + 1) * lane, block * shard + min((share + 1) * part, shard))
            from_column = block * part + unit
            begin = min(from_column // lane * lane, width - window)
            off = at - tile * lane
            hit = (row + begin - from_column == col - off) & (col >= off) & (col < off + stop - at)
            chosen = jnp.where(hit, 1.0, 0.0).astype(LOW)
            piece = jnp.dot(held[share, :, begin : begin + window], chosen, preferred_element_type=WIDE)
            total = piece if total is None else total + piece
            at = stop
        target[:, tile * lane : (tile + 1) * lane] = total


def proj_whole_kernel(skip, *refs):
    pieces, target = refs[skip:-1], refs[-1]
    me = lax.axis_index("seq")
    size = pieces[0].shape[1]
    for k, piece in enumerate(pieces):
        place = pl.multiple_of(lax.bitwise_xor(me, k) * size, size)
        target[:, pl.ds(place, size)] = piece[...].astype(WIDE)


def down_whole_kernel(part, shard, *refs):
    pieces, target = refs[:-1], refs[-1]
    me = lax.axis_index("seq")
    count = len(pieces)
    sure = shard - part * (count - 1)
    for k, piece in enumerate(pieces):
        place = lax.bitwise_xor(me, k)
        start = pl.multiple_of(place * part, 16)
        target[pl.ds(start, sure), :] = piece[:sure, :].astype(WIDE)
        if sure < part:

            @pl.when(place < count - 1)
            def _(piece=piece, start=start):
                target[pl.ds(pl.multiple_of(start + sure, 16), part - sure), :] = piece[sure:, :].astype(WIDE)


def triangle(size, reverse):
    row = lax.broadcasted_iota(jnp.int32, (size, size), 0)
    col = lax.broadcasted_iota(jnp.int32, (size, size), 1)
    return jnp.where(row <= col if reverse else row >= col, 1.0, 0.0)


def running_sum(table, step, source, target, reverse):
    count, lanes = source.shape
    carry = jnp.zeros((1, lanes), WIDE)
    starts = range(0, count, step)
    for at in reversed(starts) if reverse else starts:
        block = source[at : at + step, :]
        sums = lax.dot_general(
            table, block, (((1,), (0,)), ((), ())),
            precision=lax.Precision.HIGHEST, preferred_element_type=WIDE,
        ) + carry
        target[at : at + step, :] = sums
        carry = carry + jnp.sum(block, axis=0, keepdims=True)


def decay_rows(at, size, cum_col, cum_row, seg_col, seg_row):
    wide = at + size
    spread = cum_col[at:wide] - cum_row[:, :wide]
    order_t = lax.broadcasted_iota(jnp.int32, (size, wide), 0) + at
    order_s = lax.broadcasted_iota(jnp.int32, (size, wide), 1)
    allowed = (seg_col[at:wide] == seg_row[:, :wide]) & (order_t >= order_s)
    return jnp.where(allowed, jnp.exp(jnp.minimum(spread, 0.0)), 0.0)


def lane_of(table, lane):
    lanes = lax.broadcasted_iota(jnp.int32, table.shape, 1)
    return jnp.sum(jnp.where(lanes == lane, table, 0.0), axis=1, keepdims=True)


def forward_kernel(
    step, scale, seq_count, q, k, v, gate, logit, bias, seg_col, seg_row, gated, kept, cum, cum_rows, held
):
    head = pl.program_id(0)
    lane = head * seq_count + lax.axis_index("seq")

    @pl.when(head == 0)
    def _():
        value = logit[...] + bias[...]
        held[...] = (jnp.minimum(value, 0.0) - jnp.log1p(jnp.exp(-jnp.abs(value)))) / 16.0
        running_sum(triangle(step, False), step, held, cum, False)
        cum_rows[...] = cum[...].T

    keys, values = k[...].astype(LOW), v[...].astype(LOW)
    seg_c, seg_r = seg_col[...], seg_row[...]
    cum_c, cum_r = lane_of(cum[...], lane), cum_rows[pl.ds(lane, 1), :]
    for at in range(0, q.shape[0], step):
        stop = at + step
        rows = (q[at:stop, :] * scale).astype(LOW)
        scores = dot(rows, keys[:stop], 1, 1) * decay_rows(at, step, cum_c, cum_r, seg_c, seg_r)
        high = scores.astype(LOW)
        rest = (scores - high.astype(WIDE)).astype(LOW)
        retained = dot(high, values[:stop]) + dot(rest, values[:stop])
        kept[at:stop, :] = retained
        power = jnp.mean(retained * retained, axis=1, keepdims=True)
        unit = retained * lax.rsqrt(jnp.maximum(power, 1.0))
        gates = gate[at:stop, :]
        gated[at:stop, :] = (gates * jax.nn.sigmoid(gates) * unit).astype(LOW)


def backward_kernel(
    step, scale, width, seq_count, q, k, v, gate, logit, bias, kept, grad, cum, cum_rows, seg_col, seg_row,
    grad_proj, bias_sum, grad_k, grad_v, grad_cum, held,
):
    head = pl.program_id(0)
    lane = head * seq_count + lax.axis_index("seq")
    size = q.shape[1]
    keys, values = k[...].astype(LOW), v[...].astype(LOW)
    seg_c, seg_r = seg_col[...], seg_row[...]
    cum_c, cum_r = lane_of(cum[...], lane), cum_rows[pl.ds(lane, 1), :]

    def columns(block):
        return pl.ds(pl.multiple_of((block * width + head) * size, size), size)

    @pl.when(head == 0)
    def _():
        grad_cum[...] = jnp.zeros_like(grad_cum)

    count = q.shape[0]
    lanes = lax.broadcasted_iota(jnp.int32, (step, EXTRA), 1)
    for at in reversed(range(0, count, step)):
        stop = at + step
        first = stop == count
        retained, gates, grads = kept[at:stop, :], gate[at:stop, :], grad[at:stop, :]
        power = jnp.mean(retained * retained, axis=1, keepdims=True)
        inverse = lax.rsqrt(jnp.maximum(power, 1.0))
        unit = retained * inverse
        sigma = jax.nn.sigmoid(gates)
        grad_proj[at:stop, columns(3)] = (
            grads * unit * sigma * (1.0 + gates * (1.0 - sigma))
        ).astype(LOW)
        grad_unit = grads * gates * sigma
        along = jnp.mean(grad_unit * unit, axis=1, keepdims=True)
        grad_low = (inverse * jnp.where(power > 1.0, grad_unit - unit * along, grad_unit)).astype(LOW)
        rows = (q[at:stop, :] * scale).astype(LOW)
        table = decay_rows(at, step, cum_c, cum_r, seg_c, seg_r)
        scores = (dot(rows, keys[:stop], 1, 1) * table).astype(LOW)
        pairs = (table * dot(grad_low, values[:stop], 1, 1)).astype(LOW)
        grad_q = dot(pairs, keys[:stop])
        grad_proj[at:stop, columns(0)] = (grad_q * scale).astype(LOW)
        part_k = dot(pairs, rows, 0, 0)
        part_v = dot(scores, grad_low, 0, 0)
        if first:
            grad_k[:stop, :] = part_k
            grad_v[:stop, :] = part_v
        else:
            grad_k[:stop, :] += part_k
            grad_v[:stop, :] += part_v
        along_q = jnp.sum(rows.astype(WIDE) * grad_q, axis=1, keepdims=True)
        along_k = jnp.sum(keys[at:stop].astype(WIDE) * grad_k[at:stop, :], axis=1, keepdims=True)
        grad_cum[at:stop, :] += jnp.where(lanes == lane, along_q - along_k, 0.0)
    grad_proj[:, columns(1)] = grad_k[...].astype(LOW)
    grad_proj[:, columns(2)] = grad_v[...].astype(LOW)

    @pl.when(head == width - 1)
    def _():
        running_sum(triangle(step, True), step, grad_cum, held, True)
        value = held[...] * jax.nn.sigmoid(-(logit[...] + bias[...])) / 16.0
        bias_sum[...] = jnp.sum(value, axis=0, keepdims=True)
        grad_proj[:, 4 * width * size :] = value.astype(LOW)


def head_specs(row, size, width):
    def block(number):
        return pl.BlockSpec((row, size), lambda h: (0, number * width + h))

    def same(shape):
        return pl.BlockSpec(shape, lambda h: (0, 0))

    logit = pl.BlockSpec((row, EXTRA), lambda h: (0, 4 * width * size // EXTRA))
    return block, same, logit


def retention(projected, bias, seg_col, seg_row, width, size):
    row = projected.shape[0]
    block, same, logit = head_specs(row, size, width)
    pairs = row * row * width * 5 // 8
    return pl.pallas_call(
        functools.partial(forward_kernel, row // 4, size ** (-0.5), lax.axis_size("seq")),
        grid=(width,),
        in_specs=[block(0), block(1), block(2), block(3), logit, same((1, EXTRA)), same((row, 1)), same((1, row))],
        out_specs=[block(0), block(0), same((row, EXTRA)), same((EXTRA, row))],
        out_shape=[
            jax.ShapeDtypeStruct((row, width * size), LOW),
            jax.ShapeDtypeStruct((row, width * size), WIDE),
            jax.ShapeDtypeStruct((row, EXTRA), WIDE),
            jax.ShapeDtypeStruct((EXTRA, row), WIDE),
        ],
        scratch_shapes=[pltpu.VMEM((row, EXTRA), WIDE)],
        compiler_params=pltpu.CompilerParams(vmem_limit_bytes=VMEM_BYTES),
        cost_estimate=cost(pairs * size * 4, projected.size * 6, pairs),
    )(*([projected] * 5), bias, seg_col, seg_row)


def retention_back(projected, bias, kept, grad_gated, cum, cum_rows, seg_col, seg_row, width, size):
    row = projected.shape[0]
    block, same, logit = head_specs(row, size, width)
    pairs = row * row * width * 5 // 8
    return pl.pallas_call(
        functools.partial(backward_kernel, row // 4, size ** (-0.5), width, lax.axis_size("seq")),
        grid=(width,),
        in_specs=[block(0), block(1), block(2), block(3), logit, same((1, EXTRA)), block(0), block(0)]
        + [same((row, EXTRA)), same((EXTRA, row)), same((row, 1)), same((1, row))],
        out_specs=[same((row, 4 * width * size + EXTRA)), same((1, EXTRA))],
        out_shape=[
            jax.ShapeDtypeStruct((row, 4 * width * size + EXTRA), LOW),
            jax.ShapeDtypeStruct((1, EXTRA), WIDE),
        ],
        scratch_shapes=[pltpu.VMEM((row, size), WIDE)] * 2 + [pltpu.VMEM((row, EXTRA), WIDE)] * 2,
        compiler_params=pltpu.CompilerParams(vmem_limit_bytes=VMEM_BYTES),
        cost_estimate=cost(pairs * size * 10, projected.size * 8, pairs),
    )(*([projected] * 5), bias, kept, grad_gated, cum, cum_rows, seg_col, seg_row)


class Order:
    def __init__(self):
        self.last = None

    def put(self, value):
        if self.last is not None:
            value = after(value, self.last)
        self.last = value
        return value


class Links:
    def __init__(self, dp_count, seq_count):
        self.dp_count, self.seq_count = dp_count, seq_count
        self.ring = dp_count // 2
        self.me_dp, self.me_seq = lax.axis_index("dp"), lax.axis_index("seq")
        self.turn, self.side = self.me_dp // 2, self.me_dp % 2

    def around(self, value, by=1):
        count = self.dp_count
        return lax.ppermute(value, "dp", [(d, (d + 2 * by) % count) for d in range(count)])

    def across(self, value):
        return lax.ppermute(value, "dp", [(d, d ^ 1) for d in range(self.dp_count)])

    def across_one_way(self, value, toward):
        pairs = [
            (d * self.seq_count + s, (d ^ 1) * self.seq_count + s)
            for d in range(self.dp_count)
            for s in range(self.seq_count)
            if (d % 2 == s // 2) != toward
        ]
        return lax.ppermute(value, ("dp", "seq"), pairs)

    def core(self, value):
        return lax.ppermute(value, "seq", [(s, s ^ 1) for s in range(self.seq_count)])

    def chip(self, value):
        return lax.ppermute(value, "seq", [(s, s ^ 2) for s in range(self.seq_count)])

    def sources(self):
        return [
            ((self.turn - r) % self.ring) * 2 + (self.side ^ e) for e in range(2) for r in ORDER
        ]

    def spot(self, r):
        found = ORDER.index(0)
        for value in range(1, self.ring):
            found = jnp.where(r == value, ORDER.index(value), found)
        return found

    def places(self):
        found = []
        for d in range(self.dp_count):
            r = (self.turn - d // 2) % self.ring
            found.append(self.spot(r) + (self.side ^ (d % 2)) * self.ring)
        return found

    def total_steps(self):
        def step(axis, count, apart):
            pairs = [(d, d ^ apart) for d in range(count)]
            return lambda value: value + lax.ppermute(value, axis, pairs)

        return [step("seq", self.seq_count, apart) for apart in (1, 2)] + [
            step("dp", self.dp_count, apart) for apart in (1, 2, 4)
        ]

    def own_order(self, rows):
        me = self.me_seq
        return blocks_at(rows, [me ^ 1, me ^ 3, me ^ 2, me], rows.shape[0] // 4, 0)

    def to_rel(self, value):
        return blocks_at(value, self.sources(), value.shape[1] // self.dp_count, 1)

    def from_rel(self, value):
        return blocks_at(value, self.places(), value.shape[1] // self.dp_count, 1)


def sum_low(*parts):
    total = parts[0].astype(WIDE)
    for part in parts[1:]:
        total = total + part.astype(WIDE)
    return total.astype(LOW)


def weight_shares(links, width, part, shard, w_proj, w_decay, w_out, w_down):
    rows, columns = w_proj.shape[0], w_proj.shape[1] // links.seq_count + EXTRA
    model = w_down.shape[1]
    block = min(rows, 64)
    proj = pl.pallas_call(
        functools.partial(proj_share_kernel, 4 * width, links.seq_count),
        grid=(rows // block,),
        in_specs=[
            pl.BlockSpec((block, w_proj.shape[1]), lambda i: (i, 0)),
            pl.BlockSpec((block, w_decay.shape[1]), lambda i: (i, 0)),
        ],
        out_specs=pl.BlockSpec((block, columns), lambda i: (i, 0)),
        out_shape=jax.ShapeDtypeStruct((rows, columns), LOW),
        compiler_params=pltpu.CompilerParams(vmem_limit_bytes=VMEM_BYTES),
        cost_estimate=cost(0, 10 * rows * columns),
    )(w_proj, w_decay)
    out, down = pl.pallas_call(
        functools.partial(row_shares_kernel, part, shard, links.seq_count),
        in_specs=[in_vmem()] * 2,
        out_specs=[in_vmem()] * 2,
        out_shape=[
            jax.ShapeDtypeStruct((w_out.shape[0] // 2, model), LOW),
            jax.ShapeDtypeStruct((part, model), LOW),
        ],
        compiler_params=pltpu.CompilerParams(vmem_limit_bytes=VMEM_BYTES),
        cost_estimate=cost(0, 3 * w_out.size + 3 * w_down.size),
    )(w_out, w_down)
    return proj, out, down


def gate_up_share(links, part, shard, w_gu):
    rows, units = w_gu.shape[0], part * links.dp_count
    return pl.pallas_call(
        functools.partial(gate_up_share_kernel, part, shard, links.dp_count),
        in_specs=[in_vmem()],
        out_specs=in_vmem(),
        out_shape=jax.ShapeDtypeStruct((rows, 2 * units), LOW),
        compiler_params=pltpu.CompilerParams(vmem_limit_bytes=VMEM_BYTES),
        cost_estimate=cost(2 * rows * 768 * 2 * units, 2 * w_gu.size + 4 * rows * units),
    )(w_gu)


def whole_down(part, shard, pieces):
    model = pieces[0].shape[1]
    return pl.pallas_call(
        functools.partial(down_whole_kernel, part, shard),
        in_specs=[in_vmem()] * 4,
        out_specs=in_vmem(),
        out_shape=jax.ShapeDtypeStruct((shard, model), WIDE),
        compiler_params=pltpu.CompilerParams(vmem_limit_bytes=VMEM_BYTES),
        cost_estimate=cost(0, 6 * shard * model),
    )(*pieces)


def whole_gate_up(part, shard, dp_count, pieces):
    rows, columns = pieces[0].shape
    block = min(rows, 64)
    whole = 2 * dp_count * shard
    return pl.pallas_call(
        functools.partial(gate_up_whole_kernel, part, shard),
        grid=(rows // block,),
        in_specs=[pl.BlockSpec((block, columns), lambda i: (i, 0))] * 4,
        out_specs=pl.BlockSpec((block, whole), lambda i: (i, 0)),
        out_shape=jax.ShapeDtypeStruct((rows, whole), WIDE),
        scratch_shapes=[pltpu.VMEM((4, block, columns), LOW)],
        compiler_params=pltpu.CompilerParams(vmem_limit_bytes=VMEM_BYTES),
        cost_estimate=cost(rows * whole * 1024, rows * whole * 6),
    )(*pieces)


def whole_proj(half, number, size, kept, pieces):
    rows = pieces[0].shape[0]
    return pl.pallas_call(
        functools.partial(proj_whole_kernel, len(kept)),
        grid=(half,),
        in_specs=[anywhere()] * len(kept) + [pl.BlockSpec((rows, size), lambda i: (0, i))] * 4,
        out_specs=pl.BlockSpec((rows, 4 * size), lambda i: (0, number * half + i)),
        out_shape=jax.ShapeDtypeStruct((rows, 8 * half * size), WIDE),
        input_output_aliases={0: 0} if kept else {},
        compiler_params=pltpu.CompilerParams(vmem_limit_bytes=VMEM_BYTES),
        cost_estimate=cost(0, rows * half * size * 24),
    )(*kept, *pieces)


def placed_shards(
    inputs, segments, valid_count, teacher, cotangent, w_proj, w_decay, b_decay, w_out,
    gain_ret, gain_ffn, w_gu, w_down,
):
    dp_count, seq_count = lax.axis_size("dp"), lax.axis_size("seq")
    links, order = Links(dp_count, seq_count), Order()
    put = order.put
    tokens = inputs[0]
    count, model_width = tokens.shape
    heads = w_decay.shape[1]
    head_dim = model_width // heads
    width = heads // seq_count
    shard = w_down.shape[0]
    part = -(-shard // (16 * seq_count)) * 16
    units = part * dp_count
    first_core, x_half = links.me_seq % 2 == 0, links.me_seq // 2

    proj_share, out_share, down_share = weight_shares(
        links, width, part, shard, w_proj, w_decay, w_out, w_down
    )
    proj_share = put(proj_share)
    p_ring = links.around(proj_share)
    p_0 = links.across(proj_share)
    scale_one = rms(tokens)
    normed_here = links.to_rel((tokens * scale_one * gain_ret).astype(LOW))
    ids = jnp.broadcast_to(segments[0][:, None].astype(LOW), (count, EXTRA))
    sent = put(jnp.concatenate([normed_here, ids], axis=1))
    n_far, n_near = links.chip(sent), links.core(sent)
    out_share, down_share = put(out_share), put(down_share)
    out_cross = links.across_one_way(out_share, False)
    gu_share = put(gate_up_share(links, part, shard, after(w_gu, sent)))
    p_own_1, p_0 = put(p_ring), put(p_0)
    p_ring, p_1 = links.around(p_own_1), links.across(p_own_1)
    n_near, n_far = put(n_near), put(n_far)
    n_both = put(links.core(n_far))
    normed = put(in_row_order([sent, n_near, n_far, n_both]))
    seg_col = normed[:, model_width : model_width + 1].astype(jnp.int32)
    out_block = put(jnp.where(links.side == x_half, out_share, put(out_cross)))
    p_own_2 = put(p_ring)
    p_ring = links.around(p_own_2)
    p_1 = put(p_1)
    p_2 = links.across(p_own_2)
    p_own_3 = put(p_ring)
    o_ring = links.around(out_block)
    p_2 = put(p_2)
    p_3 = links.across(p_own_3)
    o_own_1 = put(o_ring)
    o_ring = links.around(o_own_1)
    o_own_2 = put(o_ring)
    g_ring = links.around(put(gu_share))
    o_ring = links.around(o_own_2)
    p_3 = put(p_3)
    g_0 = links.across(put(gu_share))
    p_pieces = [p_own_2, p_own_1, p_own_3, proj_share, p_2, p_1, p_3, p_0]
    projected = put(pieces_product(normed, p_pieces))
    bias = jnp.pad(b_decay, (0, EXTRA - heads))[None]
    gated, kept, cum, cum_rows = retention(projected, bias, seg_col, seg_col.T, width, head_dim)
    gated = put(gated)
    o_own_3 = put(o_ring)
    out_w = blocks_at(
        jnp.concatenate([o_own_2, o_own_1, o_own_3, out_block], axis=0),
        [links.spot((links.turn - j) % links.ring) for j in range(links.ring)],
        out_share.shape[0],
        0,
    )

    def tokens_start(rows, weight, dims):
        come = links.core(put(dot(rows[: 2 * count], weight, *dims).astype(LOW)))
        far = dot(rows[2 * count : 3 * count], weight, *dims) + come[count:].astype(WIDE)
        return come, links.chip(put(far.astype(LOW)))

    def tokens_end(started, rows, weight, dims):
        come, arrived = started
        own = dot(rows[3 * count :], weight, *dims)
        return own + come[:count].astype(WIDE) + put(arrived).astype(WIDE)

    gated_own = links.own_order(gated)
    going = tokens_start(gated_own, out_w, (1, 0))
    g_own_1 = put(g_ring)
    g_ring = links.around(g_own_1)
    g_0 = put(g_0)
    g_1 = links.across(g_own_1)
    mixed = put(tokens + tokens_end(going, gated_own, out_w, (1, 0)))
    scale_two = rms(mixed)
    sent = put(links.to_rel((mixed * scale_two * gain_ffn).astype(LOW)))
    n_far, n_near = links.chip(sent), links.core(sent)
    g_own_2 = put(g_ring)
    g_ring = links.around(g_own_2)
    g_1 = put(g_1)
    g_2 = links.across(g_own_2)
    n_far, n_near = put(n_far), put(n_near)
    n_both = put(links.core(n_far))
    normed_ffn = put(jnp.concatenate([n_near, n_both, n_far, sent], axis=0))
    g_own_3 = put(g_ring)
    d_ring = links.around(put(down_share))
    g_2 = put(g_2)
    g_3 = links.across(g_own_3)
    d_own_1 = put(d_ring)
    d_ring = links.around(d_own_1)
    p_pieces = [after(piece, d_own_1) for piece in p_pieces]
    proj_w = put(jnp.concatenate(p_pieces, axis=0))
    g_3 = put(g_3)
    d_0 = links.across(put(down_share))
    d_1 = links.across(d_own_1)
    g_pieces = [g_own_2, g_own_1, g_own_3, gu_share, g_2, g_1, g_3, g_0]
    gate_part, up_part, activated = gate_up_product(normed_ffn, g_pieces, units)
    activated = put(activated)
    d_own_2 = put(d_ring)
    d_ring = links.around(d_own_2)
    d_0, d_1 = put(d_0), put(d_1)
    d_2 = links.across(d_own_2)
    g_pieces = [after(piece, d_1) for piece in g_pieces]
    gu_w = put(jnp.concatenate(g_pieces, axis=0))
    d_own_3 = put(d_ring)
    d_3 = links.across(d_own_3)
    d_2, d_3 = put(d_2), put(d_3)
    stacked = jnp.concatenate(
        [d_own_2, d_own_1, d_own_3, down_share, d_2, d_1, d_3, d_0], axis=0
    )
    down_w = blocks_at(stacked, links.places(), part, 0)
    going = tokens_start(activated, down_w, (1, 0))
    result = mixed + tokens_end(going, activated, down_w, (1, 0))

    position = links.me_seq * count + jnp.arange(count, dtype=jnp.int32)
    valid_mask = (position < valid_count[0]).astype(WIDE)[:, None]
    mismatch = result - teacher[0]
    grad_out = cotangent[0] + valid_mask * mismatch
    squared_local = jnp.sum(valid_mask * mismatch * mismatch)
    count_local = jnp.sum(valid_mask)

    def rows_of(left, right, i, *added):
        size = model_width // dp_count
        total = dot(left[:, i * size : (i + 1) * size], right, 0, 0)
        for more in added:
            total = total + more.astype(WIDE)
        return total.astype(LOW)

    def gather_seq(total):
        far, near = links.chip(total), links.core(total)
        return [total, near, far, links.core(far)]

    sent = put(grad_out.astype(LOW))
    n_far, n_near = links.chip(sent), links.core(sent)
    n_far, n_near = put(n_far), put(n_near)
    n_both = put(links.core(n_far))
    grad_ffn = put(jnp.concatenate([n_near, n_both, n_far, sent], axis=0))
    whole = dot(activated, grad_ffn, 0, 0).astype(LOW)
    places = links.sources()
    d_come = [links.across(put(blocks_at(whole, places[i : i + 2], part, 0))) for i in (4, 6)]
    grad_act = dot(after(grad_ffn, order.last), down_w, 1, 1)
    sigma = jax.nn.sigmoid(gate_part)
    grad_gate = grad_act * up_part * sigma * (1.0 + gate_part * (1.0 - sigma))
    grad_up = grad_act * gate_part * sigma
    grad_both = put(jnp.concatenate([grad_gate, grad_up], axis=1).astype(LOW))
    going = tokens_start(grad_both, gu_w, (1, 1))
    d_come[0] = put(d_come[0])
    g_other = [put(rows_of(after(normed_ffn, order.last), grad_both, 4))]
    d_sums = put(sum_low(blocks_at(whole, places[:2], part, 0), d_come[0]))
    d_second, d_first = jnp.split(d_sums, 2, axis=0)
    d_second, d_first = links.around(d_second, 1), links.around(d_first, -1)
    grad_normed = links.from_rel(tokens_end(going, grad_both, gu_w, (1, 1)))
    grad_mid, gain_ffn_grad = norm_back(grad_normed, mixed, scale_two, gain_ffn)
    grad_mixed = grad_out + grad_mid
    sent = put(grad_mixed.astype(LOW))
    n_far, n_near = links.chip(sent), links.core(sent)
    d_come[1] = put(d_come[1])
    g_come = [links.across(put(g_other[0]))]
    d_second = put(d_second)
    d_third = put(sum_low(blocks_at(whole, places[2:3], part, 0), d_come[1][:part], d_second))
    d_third = links.around(d_third, 1)
    for i in (5, 6, 7):
        g_other.append(put(rows_of(after(normed_ffn, order.last), grad_both, i)))
    n_far, n_near = put(n_far), put(n_near)
    n_both = put(links.core(n_far))
    grad_att = put(in_row_order([sent, n_near, n_far, n_both]))
    grad_gated = put(dot(grad_att, out_w, 1, 1))
    left = blocks_at(gated, [(links.turn - r) % links.ring for r in ORDER], head_dim, 1)
    g_come[0] = put(g_come[0])
    g_come.append(links.across(put(g_other[1])))
    g_second = links.around(put(rows_of(normed_ffn, grad_both, 0, g_come[0])), 1)
    d_first, d_third = put(d_first), put(d_third)
    d_total = put(sum_low(blocks_at(whole, places[3:4], part, 0), d_come[1][part:], d_first, d_third))
    d_pieces = gather_seq(d_total)
    grad_proj, bias_local = retention_back(
        projected, bias, kept, after(grad_gated, d_total), cum, cum_rows, seg_col, seg_col.T, width, head_dim
    )
    grad_proj = put(grad_proj)
    g_come[1] = put(g_come[1])
    g_come.append(links.across(put(g_other[2])))
    g_second = put(g_second)
    g_first = links.around(put(rows_of(normed_ffn, grad_both, 1, g_come[1])), -1)
    back_rows = links.own_order(grad_proj)
    going = tokens_start(back_rows, proj_w, (1, 1))
    p_other = [put(rows_of(normed, after(grad_proj, order.last), 4))]
    g_come[2] = put(g_come[2])
    g_come.append(links.across(put(g_other[3])))
    g_third = put(rows_of(normed_ffn, grad_both, 2, g_come[2], g_second))
    g_first = put(g_first)
    g_third = links.around(g_third, 1)
    for i in (5, 6, 7):
        p_other.append(put(rows_of(normed, grad_proj, i)))
    grad_normed_one = links.from_rel(tokens_end(going, back_rows, proj_w, (1, 1)))
    grad_first, gain_ret_grad = norm_back(grad_normed_one, tokens, scale_one, gain_ret)
    grad_tokens = put(grad_mixed + grad_first)
    scalars = jnp.pad(jnp.stack([squared_local, count_local]), (0, EXTRA - 2))
    totals = put(jnp.concatenate([gain_ret_grad, gain_ffn_grad, bias_local[0], scalars]))
    totals_steps = links.total_steps()
    g_come[3] = put(g_come[3])
    p_come = [links.across(put(p_other[0]))]
    totals = totals_steps[0](totals)
    g_third = put(g_third)
    o_sums = put(dot(left, after(grad_att, order.last), 0, 0).astype(LOW))
    o_second, o_first, o_third, o_mine = jnp.split(o_sums, 4, axis=0)
    o_second, o_first = links.around(o_second, 1), links.around(o_first, -1)
    g_total = put(rows_of(normed_ffn, grad_both, 3, g_come[3], g_first, g_third))
    g_pieces = gather_seq(g_total)
    totals = totals_steps[1](put(totals))
    down_grad = put(whole_down(part, shard, [put(piece) for piece in d_pieces]))
    p_come[0] = put(p_come[0])
    p_come.append(links.across(put(p_other[1])))
    o_second, o_first = put(o_second), put(o_first)
    o_third = put(sum_low(o_third, o_second))
    p_second = links.around(put(rows_of(normed, grad_proj, 0, p_come[0])), 1)
    o_third = links.around(o_third, 1)
    totals = totals_steps[2](put(totals))
    p_come[1] = put(p_come[1])
    p_come.append(links.across(put(p_other[2])))
    p_second, o_third = put(p_second), put(o_third)
    p_first = links.around(put(rows_of(normed, grad_proj, 1, p_come[1])), -1)
    o_total = put(sum_low(o_mine, o_first, o_third))
    o_come = links.across_one_way(o_total, True)
    g_pieces = [put(piece) for piece in g_pieces]
    gu_grad = put(whole_gate_up(part, shard, dp_count, g_pieces))
    totals = totals_steps[3](put(totals))
    p_come[2] = put(p_come[2])
    p_come.append(links.across(put(p_other[3])))
    p_first = put(p_first)
    p_third = links.around(put(rows_of(normed, grad_proj, 2, p_come[2], p_second)), 1)
    o_mine = put(sum_low(o_total, put(o_come)))
    o_near = put(links.core(o_mine))
    pair = jnp.concatenate(
        [jnp.where(first_core, o_mine, o_near), jnp.where(first_core, o_near, o_mine)], axis=0
    )
    o_far = links.chip(put(pair))
    totals = totals_steps[4](put(totals))
    out_grad = put(jnp.where(x_half == links.side, pair, put(o_far)).astype(WIDE))
    totals = put(totals)
    p_come[3], p_third = put(p_come[3]), put(p_third)
    half = 2 * width * head_dim
    proj_grad = []
    p_pieces = []
    for start, stop in ((0, half), (half, 2 * half + EXTRA)):
        total = rows_of(
            normed, grad_proj[:, start:stop], 3,
            p_come[3][:, start:stop], p_first[:, start:stop], p_third[:, start:stop],
        )
        p_pieces.append(gather_seq(put(total)))
    proj_grad = whole_proj(2 * width, 0, head_dim, [], [put(piece) for piece in p_pieces[0]])
    decay_grad = sum(piece[:, half : half + heads].astype(WIDE) for piece in p_pieces[1])
    proj_grad = whole_proj(2 * width, 1, head_dim, [proj_grad], p_pieces[1])

    gain_ret_total, gain_ffn_total = totals[:model_width], totals[model_width : 2 * model_width]
    bias_total = totals[2 * model_width : 2 * model_width + heads]
    at = 2 * model_width + EXTRA
    mse = totals[at] / (totals[at + 1] * model_width)
    return (
        result[None],
        grad_tokens[None],
        proj_grad,
        decay_grad,
        bias_total,
        out_grad,
        gain_ret_total,
        gain_ffn_total,
        gu_grad,
        down_grad,
        mse,
    )


def rms(value):
    return lax.rsqrt(jnp.mean(value * value, axis=1, keepdims=True) + 1e-06)


def norm_back(grad_normed, source, inverse, gain):
    grad_gain = jnp.sum(grad_normed * source * inverse, axis=0)
    scaled = grad_normed * gain
    grad_source = inverse * (
        scaled - source * inverse * inverse * jnp.mean(scaled * source, axis=1, keepdims=True)
    )
    return (grad_source, grad_gain)


def plain_shards(
    inputs, segments, valid_count, teacher, cotangent, w_proj, w_decay, b_decay, w_out,
    gain_ret, gain_ffn, w_gu, w_down,
):
    seq_count = lax.axis_size("seq")
    me_seq = lax.axis_index("seq")
    tokens = inputs[0]
    count, model_width = tokens.shape
    heads = w_decay.shape[1]
    head_dim = model_width // heads
    width = heads // seq_count
    rows = w_proj.shape[0]

    def mine(value, axis):
        return lax.dynamic_index_in_dim(value, me_seq, axis, keepdims=False)

    def spread(value, axis):
        wide = jnp.expand_dims(value, axis)
        return jnp.concatenate(
            [jnp.where(me_seq == s, wide, jnp.zeros_like(wide)) for s in range(seq_count)], axis
        )

    def gather(block):
        return lax.all_gather(block, "dp", axis=0, tiled=True)

    def gather_tokens(value):
        return lax.all_gather(value, "seq", axis=0, tiled=True)

    def sum_tokens(value):
        return lax.psum_scatter(
            value.astype(LOW), "seq", scatter_dimension=0, tiled=True
        ).astype(WIDE)

    def scatter(grad):
        return lax.psum_scatter(grad.astype(LOW), "dp", scatter_dimension=0, tiled=True)

    def sum_rows(grad):
        return lax.psum(scatter(grad), "seq").astype(WIDE)

    def sum_columns(grad, blocks):
        total = scatter(grad)
        pieces = lax.all_gather(total.reshape(total.shape[0], blocks, -1), "seq", axis=2)
        return pieces.reshape(total.shape[0], -1).astype(WIDE)

    decay = jnp.pad(w_decay, ((0, 0), (0, EXTRA - heads)))
    proj = mine(w_proj.reshape(rows, 4 * width, seq_count, -1), 2).reshape(rows, -1)
    proj_w = jnp.concatenate([gather(proj), gather(decay)], axis=1)
    out_w = mine(gather(w_out).reshape(width, seq_count, -1, model_width), 1).reshape(-1, model_width)
    gu_w = gather(mine(w_gu.reshape(rows, 2, seq_count, -1), 2).reshape(rows, -1))
    down_w = mine(gather(w_down).reshape(seq_count, -1, model_width), 0)
    units = down_w.shape[0]

    scale_one = rms(tokens)
    normed = gather_tokens((tokens * scale_one * gain_ret).astype(LOW))
    seg_col = gather_tokens(segments[0])[:, None]
    projected = dot(normed, proj_w)
    bias = jnp.pad(b_decay, (0, EXTRA - heads))[None]
    gated, kept, cum, cum_rows = retention(projected, bias, seg_col, seg_col.T, width, head_dim)
    mixed = tokens + sum_tokens(dot(gated, out_w))
    scale_two = rms(mixed)
    normed_ffn = gather_tokens((mixed * scale_two * gain_ffn).astype(LOW))
    gate_up = dot(normed_ffn, gu_w)
    gate_part, up_part = gate_up[:, :units], gate_up[:, units:]
    sigma = jax.nn.sigmoid(gate_part)
    activated = (gate_part * sigma * up_part).astype(LOW)
    result = mixed + sum_tokens(dot(activated, down_w))

    position = me_seq * count + jnp.arange(count, dtype=jnp.int32)
    valid_mask = (position < valid_count[0]).astype(WIDE)[:, None]
    mismatch = result - teacher[0]
    grad_out = cotangent[0] + valid_mask * mismatch
    squared_local = jnp.sum(valid_mask * mismatch * mismatch)
    count_local = jnp.sum(valid_mask)

    grad_ffn = gather_tokens(grad_out.astype(LOW))
    grad = dot(activated, grad_ffn, 0, 0)
    down_grad = sum_rows(spread(grad, 0).reshape(-1, model_width))
    grad_act = dot(grad_ffn, down_w, 1, 1)
    grad_gate = grad_act * up_part * sigma * (1.0 + gate_part * (1.0 - sigma))
    grad_up = grad_act * gate_part * sigma
    grad_both = jnp.concatenate([grad_gate, grad_up], axis=1).astype(LOW)
    gu_grad = sum_columns(dot(normed_ffn, grad_both, 0, 0), 2)
    grad_normed = sum_tokens(dot(grad_both, gu_w, 1, 1))
    grad_mid, gain_ffn_grad = norm_back(grad_normed, mixed, scale_two, gain_ffn)
    grad_mixed = grad_out + grad_mid
    grad_att = gather_tokens(grad_mixed.astype(LOW))
    grad = dot(gated, grad_att, 0, 0)
    out_grad = sum_rows(spread(grad.reshape(width, -1, model_width), 1).reshape(-1, model_width))
    grad_gated = dot(grad_att, out_w, 1, 1)
    grad_proj, bias_local = retention_back(
        projected, bias, kept, grad_gated, cum, cum_rows, seg_col, seg_col.T, width, head_dim
    )
    share = 4 * width * head_dim
    grad = dot(normed, grad_proj, 0, 0)
    proj_grad = sum_columns(grad[:, :share], 4 * width)
    decay_grad = sum_rows(grad[:, share : share + heads])
    grad_normed_one = sum_tokens(dot(grad_proj, proj_w, 1, 1))
    grad_first, gain_ret_grad = norm_back(grad_normed_one, tokens, scale_one, gain_ret)
    totals = lax.psum(
        (gain_ret_grad, gain_ffn_grad, bias_local[0], squared_local, count_local), ("dp", "seq")
    )
    return (
        result[None],
        (grad_mixed + grad_first)[None],
        proj_grad,
        decay_grad,
        totals[2][:heads],
        out_grad,
        totals[0],
        totals[1],
        gu_grad,
        down_grad,
        totals[3] / (totals[4] * model_width),
    )


def solution(mesh):
    rows = P("dp", None)
    in_specs = (
        P("dp", "seq", None),
        P("dp", "seq"),
        P("dp"),
        P("dp", "seq", None),
        P("dp", "seq", None),
        rows,
        rows,
        P(),
        rows,
        P(),
        P(),
        rows,
        rows,
    )
    out_specs = (
        P("dp", "seq", None),
        P("dp", "seq", None),
        rows,
        rows,
        P(),
        rows,
        P(),
        P(),
        rows,
        rows,
        P(),
    )
    sizes = dict(mesh.shape)
    shards = placed_shards if sizes["dp"] == 8 and sizes["seq"] == 4 else plain_shards
    return jax.shard_map(shards, mesh=mesh, in_specs=in_specs, out_specs=out_specs, check_vma=False)
```

time: 4350 us -> 923 us (0.21)
  waiting for transfers between devices: 3800 us -> 466 us
  blocking collectives: 134 us -> 0 us
  Pallas kernels: 0 us -> 118 us
  matrix products: 255 us -> 157 us
  starting transfers between devices: 0.48 us -> 68.8 us
    all_gather x6 -> x0, waiting for transfers between devices: 1920 us -> none  [the longest x1 846 us: shards(): lax.all_gather(w_gu, 'dp', axis=0, tiled=True)]
    reduce_scatter x4 -> x0, waiting for transfers between devices: 940 us -> none  [the longest x1 546 us: shards(): lax.psum_scatter(proj_grad.astype(jnp.bfloat16), 'dp', scatter_dimension=...]
    unnamed x13 -> x0, waiting for transfers between devices: 717 us -> none
    ppermute x0 -> x87, waiting for transfers between devices: none -> 466 us  [the longest x24 193 us: around(): lax.ppermute(value, 'dp', [(d, (d + 2 * by) % count) for d in range(count)])]
    psum x1 -> x0, waiting for transfers between devices: 223 us -> none  [shards(): lax.psum(ret_shares[0].astype(jnp.bfloat16), 'seq').astype(jnp.float32)]
    pallas_call x0 -> x13, Pallas kernels: none -> 118 us  [the longest x1 20 us: gate_up_product(): pl.pallas_call(functools.partial(gate_up_kernel, count), grid=(steps,), i...]
    dot_general x27 -> x33, matrix products: 255 us -> 157 us  [dot(): lax.dot_general(left, right, (((left_dim,), (right_dim,)), ((), ())), pre...]
    all_gather x1 -> x0, blocking collectives: 73.4 us -> none  [shards(): lax.all_gather(w_decay, 'dp', axis=0, tiled=True)]
  transfers between devices with their start and end apart: 12 -> 87, of which waited for: 10 -> 48; matrix products, arithmetic and copies ran while one was open for 5% -> 18% of each run, Pallas kernels for 0% -> 12%
where the time goes in v2:
time: 923 us; the launch traced here: 911 us
  waiting for transfers between devices  466 us (50%)
  matrix products  157 us (17%)
  Pallas kernels  118 us (13%)
  starting transfers between devices  68.8 us (7%)
  local copies, waits for them, and re-layouts  58 us (6%)
  other arithmetic  37.8 us (4%)
    ppermute x24, waiting for transfers between devices, around(): lax.ppermute(value, 'dp', [(d, (d + 2 * by) % count) for d in range(count)])  193 us
    dot_general x33, matrix products, dot(): lax.dot_general(left, right, (((left_dim,), (right_dim,)), ((), ())), pre...  157 us
    ppermute x22, waiting for transfers between devices, across(): return lax.ppermute(value, 'dp', [(d, d ^ 1) for d in range(self.dp_count)])  121 us
    ppermute x13, waiting for transfers between devices, chip(): lax.ppermute(value, 'seq', [(s, s ^ 2) for s in range(self.seq_count)])  83 us
    unnamed x256, local copies, waits for them, and re-layouts  49.3 us
    ppermute x5, waiting for transfers between devices, step(): return lambda value: value + lax.ppermute(value, axis, pairs)  44.1 us
    ppermute x24, starting transfers between devices, around(): lax.ppermute(value, 'dp', [(d, (d + 2 * by) % count) for d in range(count)])  24.6 us
    pallas_call x1, Pallas kernels, gate_up_product(): pl.pallas_call(functools.partial(gate_up_kernel, count), grid=(steps,), i...  20 us
  transfers between devices with their start and end apart: 87, of which 48 were waited for; matrix products, arithmetic and copies ran while one was open for 18% of the time, Pallas kernels for 12%

profile of v2, /device:TPU:0, one launch (start us, length us, event | category | flops | bytes accessed | tf_op | source)
XLA Modules:
  0.0 911.1 jit_solution(4619098668072890551)
XLA Ops:
  2.1 4.2 shard_map.212.refs_4_
  21.2 5.8 shard_map.213.refs_4_.refs_12_
  27.0 9.2 %collective-permute-done.2.refs_2_ = bf16[256,2176]{1,0:T(8,128)(2,1)} collective-permute-done((bf16[256,2176]{1,0:T(8,128)(2,1)}, bf16[256,2176]{1,0:T(8,128)(2,1)}, u32[]{:S(2)}, u32[]{:S(2)}) %collective-permute-start.2) | collective-permute-done | bytes 1114144 | tf_op jit(solution)/shard_map/ppermute | solution.py:424
  36.3 7.2 collective-permute-done.3.refs_2_
  48.2 4.6 shard_map.215.refs_0_
  52.9 6.8 collective-permute-done.6
  59.8 12.7 %collective-permute-done.5.refs_1_ = bf16[256,2176]{1,0:T(8,128)(2,1)S(1)} collective-permute-done((bf16[256,2176]{1,0:T(8,128)(2,1)}, bf16[256,2176]{1,0:T(8,128)(2,1)S(1)}, u32[]{:S(2)}, u32[]{:S(2)}) %collective-permute-start.5) | collective-permute-done | bytes 1114144 | tf_op jit(solution)/shard_map/ppermute | solution.py:424
  74.3 9.4 %collective-permute-done.8.refs_6_ = bf16[256,2176]{1,0:T(8,128)(2,1)S(1)} collective-permute-done((bf16[256,2176]{1,0:T(8,128)(2,1)}, bf16[256,2176]{1,0:T(8,128)(2,1)S(1)}, u32[]{:S(2)}, u32[]{:S(2)}) %collective-permute-start.8) | collective-permute-done | bytes 1114144 | tf_op jit(solution)/shard_map/ppermute | solution.py:427
  83.7 18.0 %collective-permute-done.7.refs_3_ = bf16[256,2176]{1,0:T(8,128)(2,1)S(1)} collective-permute-done((bf16[256,2176]{1,0:T(8,128)(2,1)S(1)}, bf16[256,2176]{1,0:T(8,128)(2,1)S(1)}, u32[]{:S(2)}, u32[]{:S(2)}) %collective-permute-start.7) | collective-permute-done | bytes 1114144 | tf_op jit(solution)/shard_map/ppermute | solution.py:424
  101.7 5.0 collective-permute-done.9.refs_5_
  106.7 5.0 collective-permute-done.11
  114.6 12.0 %collective-permute-done.12 = bf16[128,2048]{1,0:T(8,128)(2,1)} collective-permute-done((bf16[128,2048]{1,0:T(8,128)(2,1)}, bf16[128,2048]{1,0:T(8,128)(2,1)}, u32[]{:S(2)}, u32[]{:S(2)}) %collective-permute-start.12) | collective-permute-done | bytes 524320 | tf_op jit(solution)/shard_map/ppermute | solution.py:424
  130.5 6.7 collective-permute-done.10.refs_7_
  137.2 16.2 %shard_map.216.q.k.v.gate.logit = f32[1024,2176]{1,0:T(8,128)} custom-call(bf16[1024,2176]{1,0:T(8,128)(2,1)} %shard_map.215.refs_0_, bf16[256,2176]{1,0:T(8,128)(2,1)} %copy-done.27, bf16[256,2176]{1,0:T(8,128)(2,1)} %collective-permute-done.2.refs_2_, bf16[256,2176]{1,0:T(8,128)(2,1)} %copy-done.33, bf16[256,2176]{1,0:T(8,128)(2,1)} %shard_map.212.refs_4_, ...), custom_call_target="tpu_custom_call" | custom-call | tf_op jit(solution)/shard_map/pallas_call | solution.py:53
  153.4 11.7 %shard_map.217 = (bf16[1024,512]{1,0:T(8,128)(2,1)}, f32[1024,512]{1,0:T(8,128)}, f32[1024,128]{1,0:T(8,128)}, f32[128,1024]{1,0:T(8,128)}) custom-call(f32[1024,2176]{1,0:T(8,128)} %shard_map.216.q.k.v.gate.logit, f32[1024,2176]{1,0:T(8,128)} %shard_map.216.q.k.v.gate.logit, f32[1024,2176]{1,0:T(8,128)} %shard_map.216.q.k.v.gate.logit, ...), custom_call_target="tpu_custom_call" | custom-call | tf_op jit(solution)/shard_map/pallas_call | solution.py:367
  170.0 3.8 collective-permute-done.14
  178.8 26.4 %collective-permute-done.17.refs_2_.refs_10_ = bf16[256,2816]{1,0:T(8,128)(2,1)} collective-permute-done((bf16[256,2816]{1,0:T(8,128)(2,1)S(1)}, bf16[256,2816]{1,0:T(8,128)(2,1)}, u32[]{:S(2)}, u32[]{:S(2)}) %collective-permute-start.17) | collective-permute-done | bytes 1441824 | tf_op jit(solution)/shard_map/ppermute | solution.py:424
  214.0 26.9 %collective-permute-done.21.refs_1_.refs_9_ = bf16[256,2816]{1,0:T(8,128)(2,1)S(1)} collective-permute-done((bf16[256,2816]{1,0:T(8,128)(2,1)}, bf16[256,2816]{1,0:T(8,128)(2,1)S(1)}, u32[]{:S(2)}, u32[]{:S(2)}) %collective-permute-start.21) | collective-permute-done | bytes 1441824 | tf_op jit(solution)/shard_map/ppermute | solution.py:424
  247.3 27.6 %collective-permute-done.23.refs_3_.refs_11_ = bf16[256,2816]{1,0:T(8,128)(2,1)S(1)} collective-permute-done((bf16[256,2816]{1,0:T(8,128)(2,1)S(1)}, bf16[256,2816]{1,0:T(8,128)(2,1)S(1)}, u32[]{:S(2)}, u32[]{:S(2)}) %collective-permute-start.23) | collective-permute-done | bytes 1441824 | tf_op jit(solution)/shard_map/ppermute | solution.py:424
  275.4 17.5 %collective-permute-done.26 = bf16[176,2048]{1,0:T(8,128)(2,1)} collective-permute-done((bf16[176,2048]{1,0:T(8,128)(2,1)}, bf16[176,2048]{1,0:T(8,128)(2,1)}, u32[]{:S(2)}, u32[]{:S(2)}) %collective-permute-start.26) | collective-permute-done | bytes 720928 | tf_op jit(solution)/shard_map/ppermute | solution.py:424
  297.9 8.3 collective-permute-done.25.refs_7_.refs_15_
  309.4 20.0 %shard_map.218 = (f32[1024,1408]{1,0:T(8,128)}, f32[1024,1408]{1,0:T(8,128)}, bf16[1024,1408]{1,0:T(8,128)(2,1)}) custom-call(bf16[1024,2048]{1,0:T(8,128)(2,1)} %pad_maximum_fusion.1.refs_0_, bf16[256,2816]{1,0:T(8,128)(2,1)} %copy-done.12, bf16[256,2816]{1,0:T(8,128)(2,1)} %collective-permute-done.17.refs_2_.refs_10_, bf16[256,2816]{1,0:T(8,128)(2,1)} %copy-done.14, ...), custom_call_target="tpu_custom_call" | custom-call | tf_op jit(solution)/shard_map/pallas_call | solution.py:84
  332.4 9.7 %collective-permute-done.29 = bf16[176,2048]{1,0:T(8,128)(2,1)S(1)} collective-permute-done((bf16[176,2048]{1,0:T(8,128)(2,1)}, bf16[176,2048]{1,0:T(8,128)(2,1)S(1)}, u32[]{:S(2)}, u32[]{:S(2)}) %collective-permute-start.29) | collective-permute-done | bytes 720928 | tf_op jit(solution)/shard_map/ppermute | solution.py:427
  350.7 6.9 collective-permute-done.31
  358.9 10.0 %collective-permute-done.32 = bf16[176,2048]{1,0:T(8,128)(2,1)S(1)} collective-permute-done((bf16[176,2048]{1,0:T(8,128)(2,1)S(1)}, bf16[176,2048]{1,0:T(8,128)(2,1)S(1)}, u32[]{:S(2)}, u32[]{:S(2)}) %collective-permute-start.32) | collective-permute-done | bytes 720928 | tf_op jit(solution)/shard_map/ppermute | solution.py:427
  371.3 3.8 convolution_convert_fusion.12
  375.2 4.1 collective-permute-done.33
  383.4 23.0 %collective-permute-done.34 = bf16[256,2048]{1,0:T(8,128)(2,1)S(1)} collective-permute-done((bf16[256,2048]{1,0:T(8,128)(2,1)S(1)}, bf16[256,2048]{1,0:T(8,128)(2,1)S(1)}, u32[]{:S(2)}, u32[]{:S(2)}) %collective-permute-start.34) | collective-permute-done | bytes 1048608 | tf_op jit(solution)/shard_map/ppermute | solution.py:442
  406.4 5.0 fusion.110
  412.9 22.9 %collective-permute-done.36 = bf16[256,2048]{1,0:T(8,128)(2,1)S(1)} collective-permute-done((bf16[256,2048]{1,0:T(8,128)(2,1)S(1)}, bf16[256,2048]{1,0:T(8,128)(2,1)S(1)}, u32[]{:S(2)}, u32[]{:S(2)}) %collective-permute-start.36) | collective-permute-done | bytes 1048608 | tf_op jit(solution)/shard_map/ppermute | solution.py:442
  440.3 6.5 convolution_convert_fusion
  451.2 8.5 fusion.115
  459.8 5.0 multiply_convert_fusion.1
  465.2 12.1 %convolution_convert_fusion.10 = bf16[512,2048]{1,0:T(8,128)(2,1)} fusion(bf16[2048,2816]{1,0:T(8,128)(2,1)} %copy-done.73, bf16[1024,2816]{1,0:T(8,128)(2,1)S(1)} %pad_maximum_fusion), kind=kOutput, calls=%fused_computation.18 | convolution fusion | flops 5906628608 | bytes 16515072 | tf_op jit(solution)/shard_map/dot_general | solution.py:18
  481.8 9.1 add_convert_fusion.9
  492.3 19.8 %collective-permute-done.40 = bf16[352,2048]{1,0:T(8,128)(2,1)} collective-permute-done((bf16[352,2048]{1,0:T(8,128)(2,1)}, bf16[352,2048]{1,0:T(8,128)(2,1)}, u32[]{:S(2)}, u32[]{:S(2)}) %collective-permute-start.40) | collective-permute-done | bytes 1441824 | tf_op jit(solution)/shard_map/ppermute | solution.py:427
  518.3 9.0 convert_add_fusion.1
  553.8 9.4 %collective-permute-done.42.refs_2_ = bf16[256,2048]{1,0:T(8,128)(2,1)} collective-permute-done((bf16[256,2048]{1,0:T(8,128)(2,1)S(1)}, bf16[256,2048]{1,0:T(8,128)(2,1)}, u32[]{:S(2)}, u32[]{:S(2)}) %collective-permute-start.42) | collective-permute-done | bytes 1048608 | tf_op jit(solution)/shard_map/ppermute | solution.py:442
  568.2 4.7 shard_map.219
  572.9 6.4 fusion.108.grad
  579.3 18.2 %collective-permute-done.47 = bf16[256,2816]{1,0:T(8,128)(2,1)} collective-permute-done((bf16[256,2816]{1,0:T(8,128)(2,1)}, bf16[256,2816]{1,0:T(8,128)(2,1)}, u32[]{:S(2)}, u32[]{:S(2)}) %collective-permute-start.47) | collective-permute-done | bytes 1441824 | tf_op jit(solution)/shard_map/ppermute | solution.py:427
  598.0 4.4 add_convert_fusion.3
  605.2 19.1 %shard_map.220 = (bf16[1024,2176]{1,0:T(8,128)(2,1)}, f32[1,128]{1,0:T(1,128)}) custom-call(f32[1024,2176]{1,0:T(8,128)} %shard_map.216.q.k.v.gate.logit, f32[1024,2176]{1,0:T(8,128)} %shard_map.216.q.k.v.gate.logit, f32[1024,2176]{1,0:T(8,128)} %shard_map.216.q.k.v.gate.logit, f32[1024,2176]{1,0:T(8,128)} %shard_map.216.q.k.v.gate.logit, ...), custom_call_target="tpu_custom_call" | custom-call | tf_op jit(solution)/shard_map/pallas_call | solution.py:388
  626.1 10.2 %convolution_convert_fusion.13 = bf16[512,2048]{1,0:T(8,128)(2,1)} fusion(bf16[2048,2176]{1,0:T(8,128)(2,1)} %copy-done.74, bf16[256,2176]{1,0:T(8,128)(2,1)S(1)} %get-tuple-element.434, bf16[256,2176]{1,0:T(8,128)(2,1)S(1)} %get-tuple-element.433), kind=kOutput, calls=%fused_computation.21 | convolution fusion | flops 4568907776 | bytes 13238272 | tf_op jit(solution)/shard_map/dot_general | solution.py:18
  636.2 4.3 add_convert_fusion.2
  644.0 4.9 convolution_convert_fusion.6
  661.3 6.4 add_convert_fusion.8
  672.0 14.3 %collective-permute-done.54 = bf16[256,2816]{1,0:T(8,128)(2,1)S(1)} collective-permute-done((bf16[256,2816]{1,0:T(8,128)(2,1)S(1)}, bf16[256,2816]{1,0:T(8,128)(2,1)S(1)}, u32[]{:S(2)}, u32[]{:S(2)}) %collective-permute-start.54) | collective-permute-done | bytes 1441824 | tf_op jit(solution)/shard_map/ppermute | solution.py:427
  687.8 4.1 add_convert_fusion.1
  695.6 6.4 convert_add_fusion
  709.0 10.4 %collective-permute-done.55 = bf16[256,2816]{1,0:T(8,128)(2,1)} collective-permute-done((bf16[256,2816]{1,0:T(8,128)(2,1)S(1)}, bf16[256,2816]{1,0:T(8,128)(2,1)}, u32[]{:S(2)}, u32[]{:S(2)}) %collective-permute-start.55) | collective-permute-done | bytes 1441824 | tf_op jit(solution)/shard_map/ppermute | solution.py:427
  720.9 5.7 collective-permute-done.58
  737.8 4.6 shard_map.221
  751.1 5.2 collective-permute-done.65
  757.5 11.0 %collective-permute-done.63 = f32[4352]{0:T(1024)S(1)} collective-permute-done((f32[4352]{0:T(1024)S(1)}, f32[4352]{0:T(1024)S(1)}, u32[]{:S(2)}, u32[]{:S(2)}) %collective-permute-start.63) | collective-permute-done | bytes 17440 | tf_op jit(solution)/shard_map/ppermute | solution.py:465
  770.6 15.1 %collective-permute-done.69 = bf16[256,2176]{1,0:T(8,128)(2,1)} collective-permute-done((bf16[256,2176]{1,0:T(8,128)(2,1)S(1)}, bf16[256,2176]{1,0:T(8,128)(2,1)}, u32[]{:S(2)}, u32[]{:S(2)}) %collective-permute-start.69) | collective-permute-done | bytes 1114144 | tf_op jit(solution)/shard_map/ppermute | solution.py:424
  789.2 6.9 collective-permute-done.68
  804.1 11.2 %shard_map.222 = f32[256,11008]{1,0:T(8,128)} custom-call(bf16[256,2816]{1,0:T(8,128)(2,1)} %copy-done.23, bf16[256,2816]{1,0:T(8,128)(2,1)} %copy-done.50, bf16[256,2816]{1,0:T(8,128)(2,1)} %copy-done.49, bf16[256,2816]{1,0:T(8,128)(2,1)} %collective-permute-done.72.refs_3_), custom_call_target="tpu_custom_call" | custom-call | tf_op jit(solution)/shard_map/pallas_call | solution.py:547
  815.3 4.1 collective-permute-done.76
  828.6 26.6 %collective-permute-done.74 = f32[4352]{0:T(1024)S(1)} collective-permute-done((f32[4352]{0:T(1024)S(1)}, f32[4352]{0:T(1024)S(1)}, u32[]{:S(2)}, u32[]{:S(2)}) %collective-permute-start.74) | collective-permute-done | bytes 17440 | tf_op jit(solution)/shard_map/ppermute | solution.py:465
  870.3 14.2 %collective-permute-done.85.refs_3_ = bf16[256,1152]{1,0:T(8,128)(2,1)S(1)} collective-permute-done((bf16[256,1152]{1,0:T(8,128)(2,1)S(1)}, bf16[256,1152]{1,0:T(8,128)(2,1)S(1)}, u32[]{:S(2)}, u32[]{:S(2)}) %collective-permute-start.85) | collective-permute-done | bytes 589856 | tf_op jit(solution)/shard_map/ppermute | solution.py:442
  885.0 6.3 collective-permute-done.82.refs_2_
  896.0 6.2 shard_map.223.refs_0_
  903.2 6.2 shard_map.224
  (478 shorter events, 238.4 us)
Async XLA Ops:
  6.3 29.9 %collective-permute-start.2 = (bf16[256,2176]{1,0:T(8,128)(2,1)}, bf16[256,2176]{1,0:T(8,128)(2,1)}, u32[]{:S(2)}, u32[]{:S(2)}) collective-permute-start(bf16[256,2176]{1,0:T(8,128)(2,1)} %shard_map.212.refs_4_), channel_id=1, source_target_pairs={{0,8},{4,12},{8,16},{12,20},{16,24},{20,28},{24,0},{28,4},{1,9},{5... | collective-permute-start | bytes 3342344 | tf_op jit(solution)/shard_map/ppermute | solution.py:424
  9.3 26.9 %collective-permute-start.1 = (bf16[256,2176]{1,0:T(8,128)(2,1)}, bf16[256,2176]{1,0:T(8,128)(2,1)S(1)}, u32[]{:S(2)}, u32[]{:S(2)}) collective-permute-start(bf16[256,2176]{1,0:T(8,128)(2,1)} %shard_map.212.refs_4_), channel_id=1, source_target_pairs={{0,4},{4,0},{8,12},{12,8},{16,20},{20,16},{24,28},{28,24},{1,5},{5... | collective-permute-start | bytes 3342344 | tf_op jit(solution)/shard_map/ppermute | solution.py:427
  16.3 20.0 %collective-permute-start = (bf16[256,2176]{1,0:T(8,128)(2,1)S(1)}, bf16[256,2176]{1,0:T(8,128)(2,1)S(1)}, u32[]{:S(2)}, u32[]{:S(2)}) collective-permute-start(bf16[256,2176]{1,0:T(8,128)(2,1)S(1)} %constant_dynamic-update-slice_fusion.refs_0_), channel_id=1, source_target_pairs={{0,1},{1,0},{2,3},{3,2},{4,5},{5,4},{6,7},{7,6},{8,9},{9,8},{10,11... | collective-permute-start | bytes 3342344 | tf_op jit(solution)/shard_map/ppermute | solution.py:439
  16.3 27.1 %collective-permute-start.3 = (bf16[256,2176]{1,0:T(8,128)(2,1)S(1)}, bf16[256,2176]{1,0:T(8,128)(2,1)}, u32[]{:S(2)}, u32[]{:S(2)}) collective-permute-start(bf16[256,2176]{1,0:T(8,128)(2,1)S(1)} %constant_dynamic-update-slice_fusion.refs_0_), channel_id=1, source_target_pairs={{0,2},{1,3},{2,0},{3,1},{4,6},{5,7},{6,4},{7,5},{8,10},{9,11},{10,... | collective-permute-start | bytes 3342344 | tf_op jit(solution)/shard_map/ppermute | solution.py:442
  43.4 29.0 %collective-permute-start.5 = (bf16[256,2176]{1,0:T(8,128)(2,1)}, bf16[256,2176]{1,0:T(8,128)(2,1)S(1)}, u32[]{:S(2)}, u32[]{:S(2)}) collective-permute-start(bf16[256,2176]{1,0:T(8,128)(2,1)} %collective-permute-done.2.refs_2_), channel_id=1, source_target_pairs={{0,8},{4,12},{8,16},{12,20},{16,24},{20,28},{24,0},{28,4},{1,9},{5... | collective-permute-start | bytes 3342344 | tf_op jit(solution)/shard_map/ppermute | solution.py:424
  48.2 35.4 %collective-permute-start.8 = (bf16[256,2176]{1,0:T(8,128)(2,1)}, bf16[256,2176]{1,0:T(8,128)(2,1)S(1)}, u32[]{:S(2)}, u32[]{:S(2)}) collective-permute-start(bf16[256,2176]{1,0:T(8,128)(2,1)} %collective-permute-done.2.refs_2_), channel_id=1, source_target_pairs={{0,4},{4,0},{8,12},{12,8},{16,20},{20,16},{24,28},{28,24},{1,5},{5... | collective-permute-start | bytes 3342344 | tf_op jit(solution)/shard_map/ppermute | solution.py:427
  72.4 29.3 %collective-permute-start.7 = (bf16[256,2176]{1,0:T(8,128)(2,1)S(1)}, bf16[256,2176]{1,0:T(8,128)(2,1)S(1)}, u32[]{:S(2)}, u32[]{:S(2)}) collective-permute-start(bf16[256,2176]{1,0:T(8,128)(2,1)S(1)} %collective-permute-done.5.refs_1_), channel_id=1, source_target_pairs={{0,8},{4,12},{8,16},{12,20},{16,24},{20,28},{24,0},{28,4},{1,9},{5... | collective-permute-start | bytes 3342344 | tf_op jit(solution)/shard_map/ppermute | solution.py:424
  72.4 34.3 %collective-permute-start.9 = (bf16[256,2176]{1,0:T(8,128)(2,1)S(1)}, bf16[256,2176]{1,0:T(8,128)(2,1)S(1)}, u32[]{:S(2)}, u32[]{:S(2)}) collective-permute-start(bf16[256,2176]{1,0:T(8,128)(2,1)S(1)} %collective-permute-done.5.refs_1_), channel_id=1, source_target_pairs={{0,4},{4,0},{8,12},{12,8},{16,20},{20,16},{24,28},{28,24},{1,5},{5... | collective-permute-start | bytes 3342344 | tf_op jit(solution)/shard_map/ppermute | solution.py:427
  72.9 38.8 %collective-permute-start.11 = (bf16[128,2048]{1,0:T(8,128)(2,1)S(1)}, bf16[128,2048]{1,0:T(8,128)(2,1)}, u32[]{:S(2)}, u32[]{:S(2)}) collective-permute-start(bf16[128,2048]{1,0:T(8,128)(2,1)S(1)} %broadcast_select_fusion.2), channel_id=1, source_target_pairs={{0,8},{4,12},{8,16},{12,20},{16,24},{20,28},{24,0},{28,4},{1,9},{5... | collective-permute-start | bytes 1572872 | tf_op jit(solution)/shard_map/ppermute | solution.py:424
  111.8 25.4 %collective-permute-start.10 = (bf16[256,2176]{1,0:T(8,128)(2,1)S(1)}, bf16[256,2176]{1,0:T(8,128)(2,1)}, u32[]{:S(2)}, u32[]{:S(2)}) collective-permute-start(bf16[256,2176]{1,0:T(8,128)(2,1)S(1)} %collective-permute-done.7.refs_3_), channel_id=1, source_target_pairs={{0,4},{4,0},{8,12},{12,8},{16,20},{20,16},{24,28},{28,24},{1,5},{5... | collective-permute-start | bytes 3342344 | tf_op jit(solution)/shard_map/ppermute | solution.py:427
  126.5 38.6 %collective-permute-start.13 = (bf16[128,2048]{1,0:T(8,128)(2,1)}, bf16[128,2048]{1,0:T(8,128)(2,1)S(1)}, u32[]{:S(2)}, u32[]{:S(2)}) collective-permute-start(bf16[128,2048]{1,0:T(8,128)(2,1)} %collective-permute-done.12), channel_id=1, source_target_pairs={{0,8},{4,12},{8,16},{12,20},{16,24},{20,28},{24,0},{28,4},{1,9},{5... | collective-permute-start | bytes 1572872 | tf_op jit(solution)/shard_map/ppermute | solution.py:424
  169.3 35.9 %collective-permute-start.17 = (bf16[256,2816]{1,0:T(8,128)(2,1)S(1)}, bf16[256,2816]{1,0:T(8,128)(2,1)}, u32[]{:S(2)}, u32[]{:S(2)}) collective-permute-start(bf16[256,2816]{1,0:T(8,128)(2,1)S(1)} %copy-done.7), channel_id=1, source_target_pairs={{0,8},{4,12},{8,16},{12,20},{16,24},{20,28},{24,0},{28,4},{1,9},{5... | collective-permute-start | bytes 4325384 | tf_op jit(solution)/shard_map/ppermute | solution.py:424
  169.4 36.9 %collective-permute-start.16 = (bf16[256,2816]{1,0:T(8,128)(2,1)S(1)}, bf16[256,2816]{1,0:T(8,128)(2,1)S(1)}, u32[]{:S(2)}, u32[]{:S(2)}) collective-permute-start(bf16[256,2816]{1,0:T(8,128)(2,1)S(1)} %copy-done.7), channel_id=1, source_target_pairs={{0,4},{4,0},{8,12},{12,8},{16,20},{20,16},{24,28},{28,24},{1,5},{5... | collective-permute-start | bytes 4325384 | tf_op jit(solution)/shard_map/ppermute | solution.py:427
  177.3 30.2 %collective-permute-start.15 = (bf16[256,2048]{1,0:T(8,128)(2,1)}, bf16[256,2048]{1,0:T(8,128)(2,1)}, u32[]{:S(2)}, u32[]{:S(2)}) collective-permute-start(bf16[256,2048]{1,0:T(8,128)(2,1)} %add_convert_fusion.11), channel_id=1, source_target_pairs={{0,2},{1,3},{2,0},{3,1},{4,6},{5,7},{6,4},{7,5},{8,10},{9,11},{10,... | collective-permute-start | bytes 3145736 | tf_op jit(solution)/shard_map/ppermute | solution.py:442
  205.2 35.7 %collective-permute-start.21 = (bf16[256,2816]{1,0:T(8,128)(2,1)}, bf16[256,2816]{1,0:T(8,128)(2,1)S(1)}, u32[]{:S(2)}, u32[]{:S(2)}) collective-permute-start(bf16[256,2816]{1,0:T(8,128)(2,1)} %collective-permute-done.17.refs_2_.refs_10_), channel_id=1, source_target_pairs={{0,8},{4,12},{8,16},{12,20},{16,24},{20,28},{24,0},{28,4},{1,9},{5... | collective-permute-start | bytes 4325384 | tf_op jit(solution)/shard_map/ppermute | solution.py:424
  205.7 35.1 %collective-permute-start.20 = (bf16[256,2816]{1,0:T(8,128)(2,1)}, bf16[256,2816]{1,0:T(8,128)(2,1)}, u32[]{:S(2)}, u32[]{:S(2)}) collective-permute-start(bf16[256,2816]{1,0:T(8,128)(2,1)} %collective-permute-done.17.refs_2_.refs_10_), channel_id=1, source_target_pairs={{0,4},{4,0},{8,12},{12,8},{16,20},{20,16},{24,28},{28,24},{1,5},{5... | collective-permute-start | bytes 4325384 | tf_op jit(solution)/shard_map/ppermute | solution.py:427
  212.4 28.5 %collective-permute-start.19 = (bf16[256,2048]{1,0:T(8,128)(2,1)S(1)}, bf16[256,2048]{1,0:T(8,128)(2,1)S(1)}, u32[]{:S(2)}, u32[]{:S(2)}) collective-permute-start(bf16[256,2048]{1,0:T(8,128)(2,1)S(1)} %constant_dynamic-update-slice_fusion.13), channel_id=1, source_target_pairs={{0,2},{1,3},{2,0},{3,1},{4,6},{5,7},{6,4},{7,5},{8,10},{9,11},{10,... | collective-permute-start | bytes 3145736 | tf_op jit(solution)/shard_map/ppermute | solution.py:442
  240.9 34.0 %collective-permute-start.23 = (bf16[256,2816]{1,0:T(8,128)(2,1)S(1)}, bf16[256,2816]{1,0:T(8,128)(2,1)S(1)}, u32[]{:S(2)}, u32[]{:S(2)}) collective-permute-start(bf16[256,2816]{1,0:T(8,128)(2,1)S(1)} %collective-permute-done.21.refs_1_.refs_9_), channel_id=1, source_target_pairs={{0,8},{4,12},{8,16},{12,20},{16,24},{20,28},{24,0},{28,4},{1,9},{5... | collective-permute-start | bytes 4325384 | tf_op jit(solution)/shard_map/ppermute | solution.py:424
  241.4 34.0 %collective-permute-start.24 = (bf16[256,2816]{1,0:T(8,128)(2,1)S(1)}, bf16[256,2816]{1,0:T(8,128)(2,1)S(1)}, u32[]{:S(2)}, u32[]{:S(2)}) collective-permute-start(bf16[256,2816]{1,0:T(8,128)(2,1)S(1)} %collective-permute-done.21.refs_1_.refs_9_), channel_id=1, source_target_pairs={{0,4},{4,0},{8,12},{12,8},{16,20},{20,16},{24,28},{28,24},{1,5},{5... | collective-permute-start | bytes 4325384 | tf_op jit(solution)/shard_map/ppermute | solution.py:427
  274.9 31.3 %collective-permute-start.25 = (bf16[256,2816]{1,0:T(8,128)(2,1)S(1)}, bf16[256,2816]{1,0:T(8,128)(2,1)S(1)}, u32[]{:S(2)}, u32[]{:S(2)}) collective-permute-start(bf16[256,2816]{1,0:T(8,128)(2,1)S(1)} %collective-permute-done.23.refs_3_.refs_11_), channel_id=1, source_target_pairs={{0,4},{4,0},{8,12},{12,8},{16,20},{20,16},{24,28},{28,24},{1,5},{5... | collective-permute-start | bytes 4325384 | tf_op jit(solution)/shard_map/ppermute | solution.py:427
  292.9 36.5 %collective-permute-start.27 = (bf16[176,2048]{1,0:T(8,128)(2,1)}, bf16[176,2048]{1,0:T(8,128)(2,1)}, u32[]{:S(2)}, u32[]{:S(2)}) collective-permute-start(bf16[176,2048]{1,0:T(8,128)(2,1)} %collective-permute-done.26), channel_id=1, source_target_pairs={{0,8},{4,12},{8,16},{12,20},{16,24},{20,28},{24,0},{28,4},{1,9},{5... | collective-permute-start | bytes 2162696 | tf_op jit(solution)/shard_map/ppermute | solution.py:424
  307.4 25.1 %collective-permute-start.30 = (bf16[176,2048]{1,0:T(8,128)(2,1)}, bf16[176,2048]{1,0:T(8,128)(2,1)S(1)}, u32[]{:S(2)}, u32[]{:S(2)}) collective-permute-start(bf16[176,2048]{1,0:T(8,128)(2,1)} %get-tuple-element.259), channel_id=1, source_target_pairs={{0,4},{4,0},{8,12},{12,8},{16,20},{20,16},{24,28},{28,24},{1,5},{5... | collective-permute-start | bytes 2162696 | tf_op jit(solution)/shard_map/ppermute | solution.py:427
  307.9 34.2 %collective-permute-start.29 = (bf16[176,2048]{1,0:T(8,128)(2,1)}, bf16[176,2048]{1,0:T(8,128)(2,1)S(1)}, u32[]{:S(2)}, u32[]{:S(2)}) collective-permute-start(bf16[176,2048]{1,0:T(8,128)(2,1)} %collective-permute-done.26), channel_id=1, source_target_pairs={{0,4},{4,0},{8,12},{12,8},{16,20},{20,16},{24,28},{28,24},{1,5},{5... | collective-permute-start | bytes 2162696 | tf_op jit(solution)/shard_map/ppermute | solution.py:427
  329.4 20.7 %collective-permute-start.28 = (bf16[176,2048]{1,0:T(8,128)(2,1)}, bf16[176,2048]{1,0:T(8,128)(2,1)S(1)}, u32[]{:S(2)}, u32[]{:S(2)}) collective-permute-start(bf16[176,2048]{1,0:T(8,128)(2,1)} %collective-permute-done.27), channel_id=1, source_target_pairs={{0,8},{4,12},{8,16},{12,20},{16,24},{20,28},{24,0},{28,4},{1,9},{5... | collective-permute-start | bytes 2162696 | tf_op jit(solution)/shard_map/ppermute | solution.py:424
  329.5 28.1 %collective-permute-start.31 = (bf16[176,2048]{1,0:T(8,128)(2,1)}, bf16[176,2048]{1,0:T(8,128)(2,1)S(1)}, u32[]{:S(2)}, u32[]{:S(2)}) collective-permute-start(bf16[176,2048]{1,0:T(8,128)(2,1)} %collective-permute-done.27), channel_id=1, source_target_pairs={{0,4},{4,0},{8,12},{12,8},{16,20},{20,16},{24,28},{28,24},{1,5},{5... | collective-permute-start | bytes 2162696 | tf_op jit(solution)/shard_map/ppermute | solution.py:427
  381.1 25.3 %collective-permute-start.34 = (bf16[256,2048]{1,0:T(8,128)(2,1)S(1)}, bf16[256,2048]{1,0:T(8,128)(2,1)S(1)}, u32[]{:S(2)}, u32[]{:S(2)}) collective-permute-start(bf16[256,2048]{1,0:T(8,128)(2,1)S(1)} %add_convert_fusion.10), channel_id=1, source_target_pairs={{0,2},{1,3},{2,0},{3,1},{4,6},{5,7},{6,4},{7,5},{8,10},{9,11},{10,... | collective-permute-start | bytes 3145736 | tf_op jit(solution)/shard_map/ppermute | solution.py:442
  411.4 24.4 %collective-permute-start.36 = (bf16[256,2048]{1,0:T(8,128)(2,1)S(1)}, bf16[256,2048]{1,0:T(8,128)(2,1)S(1)}, u32[]{:S(2)}, u32[]{:S(2)}) collective-permute-start(bf16[256,2048]{1,0:T(8,128)(2,1)S(1)} %get-tuple-element.279), channel_id=1, source_target_pairs={{0,2},{1,3},{2,0},{3,1},{4,6},{5,7},{6,4},{7,5},{8,10},{9,11},{10,... | collective-permute-start | bytes 3145736 | tf_op jit(solution)/shard_map/ppermute | solution.py:442
  412.9 22.9 %collective-permute-start.35 = (bf16[256,2048]{1,0:T(8,128)(2,1)S(1)}, bf16[256,2048]{1,0:T(8,128)(2,1)S(1)}, u32[]{:S(2)}, u32[]{:S(2)}) collective-permute-start(bf16[256,2048]{1,0:T(8,128)(2,1)S(1)} %get-tuple-element.279), channel_id=1, source_target_pairs={{0,1},{1,0},{2,3},{3,2},{4,5},{5,4},{6,7},{7,6},{8,9},{9,8},{10,11... | collective-permute-start | bytes 3145736 | tf_op jit(solution)/shard_map/ppermute | solution.py:439
  477.4 34.7 %collective-permute-start.40 = (bf16[352,2048]{1,0:T(8,128)(2,1)}, bf16[352,2048]{1,0:T(8,128)(2,1)}, u32[]{:S(2)}, u32[]{:S(2)}) collective-permute-start(bf16[352,2048]{1,0:T(8,128)(2,1)} %get-tuple-element.284), channel_id=1, source_target_pairs={{0,4},{4,0},{8,12},{12,8},{16,20},{20,16},{24,28},{28,24},{1,5},{5... | collective-permute-start | bytes 4325384 | tf_op jit(solution)/shard_map/ppermute | solution.py:427
  478.0 64.5 %collective-permute-start.43 = (bf16[352,2048]{1,0:T(8,128)(2,1)}, bf16[352,2048]{1,0:T(8,128)(2,1)}, u32[]{:S(2)}, u32[]{:S(2)}) collective-permute-start(bf16[352,2048]{1,0:T(8,128)(2,1)} %get-tuple-element.285), channel_id=1, source_target_pairs={{0,4},{4,0},{8,12},{12,8},{16,20},{20,16},{24,28},{28,24},{1,5},{5... | collective-permute-start | bytes 4325384 | tf_op jit(solution)/shard_map/ppermute | solution.py:427
  490.8 27.5 %collective-permute-start.39 = (bf16[256,2048]{1,0:T(8,128)(2,1)}, bf16[256,2048]{1,0:T(8,128)(2,1)S(1)}, u32[]{:S(2)}, u32[]{:S(2)}) collective-permute-start(bf16[256,2048]{1,0:T(8,128)(2,1)} %add_convert_fusion.9), channel_id=1, source_target_pairs={{0,2},{1,3},{2,0},{3,1},{4,6},{5,7},{6,4},{7,5},{8,10},{9,11},{10,... | collective-permute-start | bytes 3145736 | tf_op jit(solution)/shard_map/ppermute | solution.py:442
  517.9 24.6 %collective-permute-start.44 = (bf16[176,2048]{1,0:T(8,128)(2,1)S(1)}, bf16[176,2048]{1,0:T(8,128)(2,1)}, u32[]{:S(2)}, u32[]{:S(2)}) collective-permute-start(bf16[176,2048]{1,0:T(8,128)(2,1)S(1)} %get-tuple-element.443), channel_id=1, source_target_pairs={{0,8},{4,12},{8,16},{12,20},{16,24},{20,28},{24,0},{28,4},{1,9},{5... | collective-permute-start | bytes 2162696 | tf_op jit(solution)/shard_map/ppermute | solution.py:424
  539.0 24.2 %collective-permute-start.42 = (bf16[256,2048]{1,0:T(8,128)(2,1)S(1)}, bf16[256,2048]{1,0:T(8,128)(2,1)}, u32[]{:S(2)}, u32[]{:S(2)}) collective-permute-start(bf16[256,2048]{1,0:T(8,128)(2,1)S(1)} %get-tuple-element.298.refs_0_), channel_id=1, source_target_pairs={{0,2},{1,3},{2,0},{3,1},{4,6},{5,7},{6,4},{7,5},{8,10},{9,11},{10,... | collective-permute-start | bytes 3145736 | tf_op jit(solution)/shard_map/ppermute | solution.py:442
  540.5 26.7 %collective-permute-start.41 = (bf16[256,2048]{1,0:T(8,128)(2,1)S(1)}, bf16[256,2048]{1,0:T(8,128)(2,1)}, u32[]{:S(2)}, u32[]{:S(2)}) collective-permute-start(bf16[256,2048]{1,0:T(8,128)(2,1)S(1)} %get-tuple-element.298.refs_0_), channel_id=1, source_target_pairs={{0,1},{1,0},{2,3},{3,2},{4,5},{5,4},{6,7},{7,6},{8,9},{9,8},{10,11... | collective-permute-start | bytes 3145736 | tf_op jit(solution)/shard_map/ppermute | solution.py:439
  563.2 34.3 %collective-permute-start.47 = (bf16[256,2816]{1,0:T(8,128)(2,1)}, bf16[256,2816]{1,0:T(8,128)(2,1)}, u32[]{:S(2)}, u32[]{:S(2)}) collective-permute-start(bf16[256,2816]{1,0:T(8,128)(2,1)} %convolution_convert_fusion.4), channel_id=1, source_target_pairs={{0,4},{4,0},{8,12},{12,8},{16,20},{20,16},{24,28},{28,24},{1,5},{5... | collective-permute-start | bytes 4325384 | tf_op jit(solution)/shard_map/ppermute | solution.py:427
  563.7 39.2 %collective-permute-start.46 = (bf16[176,2048]{1,0:T(8,128)(2,1)}, bf16[176,2048]{1,0:T(8,128)(2,1)}, u32[]{:S(2)}, u32[]{:S(2)}) collective-permute-start(bf16[176,2048]{1,0:T(8,128)(2,1)} %get-tuple-element.442), channel_id=1, source_target_pairs={{0,24},{4,28},{8,0},{12,4},{16,8},{20,12},{24,16},{28,20},{1,25},{... | collective-permute-start | bytes 2162696 | tf_op jit(solution)/shard_map/ppermute | solution.py:424
  567.2 35.7 %collective-permute-start.48 = (bf16[176,2048]{1,0:T(8,128)(2,1)}, bf16[176,2048]{1,0:T(8,128)(2,1)}, u32[]{:S(2)}, u32[]{:S(2)}) collective-permute-start(bf16[176,2048]{1,0:T(8,128)(2,1)} %add_convert_fusion.13), channel_id=1, source_target_pairs={{0,8},{4,12},{8,16},{12,20},{16,24},{20,28},{24,0},{28,4},{1,9},{5... | collective-permute-start | bytes 2162696 | tf_op jit(solution)/shard_map/ppermute | solution.py:424
  597.5 38.7 %collective-permute-start.49 = (bf16[256,2816]{1,0:T(8,128)(2,1)}, bf16[256,2816]{1,0:T(8,128)(2,1)}, u32[]{:S(2)}, u32[]{:S(2)}) collective-permute-start(bf16[256,2816]{1,0:T(8,128)(2,1)} %convolution_convert_fusion.3), channel_id=1, source_target_pairs={{0,4},{4,0},{8,12},{12,8},{16,20},{20,16},{24,28},{28,24},{1,5},{5... | collective-permute-start | bytes 4325384 | tf_op jit(solution)/shard_map/ppermute | solution.py:427
  602.4 38.2 %collective-permute-start.50 = (bf16[256,2816]{1,0:T(8,128)(2,1)}, bf16[256,2816]{1,0:T(8,128)(2,1)S(1)}, u32[]{:S(2)}, u32[]{:S(2)}) collective-permute-start(bf16[256,2816]{1,0:T(8,128)(2,1)} %add_convert_fusion.3), channel_id=1, source_target_pairs={{0,8},{4,12},{8,16},{12,20},{16,24},{20,28},{24,0},{28,4},{1,9},{5... | collective-permute-start | bytes 4325384 | tf_op jit(solution)/shard_map/ppermute | solution.py:424
  640.6 20.8 %collective-permute-start.51 = (bf16[512,2048]{1,0:T(8,128)(2,1)}, bf16[512,2048]{1,0:T(8,128)(2,1)}, u32[]{:S(2)}, u32[]{:S(2)}) collective-permute-start(bf16[512,2048]{1,0:T(8,128)(2,1)} %convolution_convert_fusion.13), channel_id=1, source_target_pairs={{0,1},{1,0},{2,3},{3,2},{4,5},{5,4},{6,7},{7,6},{8,9},{9,8},{10,11... | collective-permute-start | bytes 6291464 | tf_op jit(solution)/shard_map/ppermute | solution.py:439
  642.5 65.5 %collective-permute-start.60 = (bf16[176,2048]{1,0:T(8,128)(2,1)S(1)}, bf16[176,2048]{1,0:T(8,128)(2,1)S(1)}, u32[]{:S(2)}, u32[]{:S(2)}) collective-permute-start(bf16[176,2048]{1,0:T(8,128)(2,1)S(1)} %add_convert_fusion.12.refs_0_), channel_id=1, source_target_pairs={{0,2},{1,3},{2,0},{3,1},{4,6},{5,7},{6,4},{7,5},{8,10},{9,11},{10,... | collective-permute-start | bytes 2162696 | tf_op jit(solution)/shard_map/ppermute | solution.py:442
  652.5 33.8 %collective-permute-start.54 = (bf16[256,2816]{1,0:T(8,128)(2,1)S(1)}, bf16[256,2816]{1,0:T(8,128)(2,1)S(1)}, u32[]{:S(2)}, u32[]{:S(2)}) collective-permute-start(bf16[256,2816]{1,0:T(8,128)(2,1)S(1)} %copy-done.47), channel_id=1, source_target_pairs={{0,4},{4,0},{8,12},{12,8},{16,20},{20,16},{24,28},{28,24},{1,5},{5... | collective-permute-start | bytes 4325384 | tf_op jit(solution)/shard_map/ppermute | solution.py:427
  657.7 37.9 %collective-permute-start.53 = (bf16[256,2816]{1,0:T(8,128)(2,1)S(1)}, bf16[256,2816]{1,0:T(8,128)(2,1)S(1)}, u32[]{:S(2)}, u32[]{:S(2)}) collective-permute-start(bf16[256,2816]{1,0:T(8,128)(2,1)S(1)} %copy-done.48), channel_id=1, source_target_pairs={{0,24},{4,28},{8,0},{12,4},{16,8},{20,12},{24,16},{28,20},{1,25},{... | collective-permute-start | bytes 4325384 | tf_op jit(solution)/shard_map/ppermute | solution.py:424
  667.7 27.8 %collective-permute-start.52 = (bf16[256,2048]{1,0:T(8,128)(2,1)S(1)}, bf16[256,2048]{1,0:T(8,128)(2,1)S(1)}, u32[]{:S(2)}, u32[]{:S(2)}) collective-permute-start(bf16[256,2048]{1,0:T(8,128)(2,1)S(1)} %add_convert_fusion.8), channel_id=1, source_target_pairs={{0,2},{1,3},{2,0},{3,1},{4,6},{5,7},{6,4},{7,5},{8,10},{9,11},{10,... | collective-permute-start | bytes 3145736 | tf_op jit(solution)/shard_map/ppermute | solution.py:442
  686.3 33.1 %collective-permute-start.55 = (bf16[256,2816]{1,0:T(8,128)(2,1)S(1)}, bf16[256,2816]{1,0:T(8,128)(2,1)}, u32[]{:S(2)}, u32[]{:S(2)}) collective-permute-start(bf16[256,2816]{1,0:T(8,128)(2,1)S(1)} %copy-done.46), channel_id=1, source_target_pairs={{0,4},{4,0},{8,12},{12,8},{16,20},{20,16},{24,28},{28,24},{1,5},{5... | collective-permute-start | bytes 4325384 | tf_op jit(solution)/shard_map/ppermute | solution.py:427
  691.9 34.7 %collective-permute-start.58 = (bf16[256,2816]{1,0:T(8,128)(2,1)}, bf16[256,2816]{1,0:T(8,128)(2,1)S(1)}, u32[]{:S(2)}, u32[]{:S(2)}) collective-permute-start(bf16[256,2816]{1,0:T(8,128)(2,1)} %add_convert_fusion.1), channel_id=1, source_target_pairs={{0,8},{4,12},{8,16},{12,20},{16,24},{20,28},{24,0},{28,4},{1,9},{5... | collective-permute-start | bytes 4325384 | tf_op jit(solution)/shard_map/ppermute | solution.py:424
  707.5 29.5 %collective-permute-start.59 = (bf16[176,2048]{1,0:T(8,128)(2,1)S(1)}, bf16[176,2048]{1,0:T(8,128)(2,1)S(1)}, u32[]{:S(2)}, u32[]{:S(2)}) collective-permute-start(bf16[176,2048]{1,0:T(8,128)(2,1)S(1)} %add_convert_fusion.12.refs_0_), channel_id=1, source_target_pairs={{0,1},{1,0},{2,3},{3,2},{4,5},{5,4},{6,7},{7,6},{8,9},{9,8},{10,11... | collective-permute-start | bytes 2162696 | tf_op jit(solution)/shard_map/ppermute | solution.py:439
  708.0 29.8 %collective-permute-start.61 = (bf16[176,2048]{1,0:T(8,128)(2,1)S(1)}, bf16[176,2048]{1,0:T(8,128)(2,1)}, u32[]{:S(2)}, u32[]{:S(2)}) collective-permute-start(bf16[176,2048]{1,0:T(8,128)(2,1)S(1)} %collective-permute-done.60.refs_2_), channel_id=1, source_target_pairs={{0,1},{1,0},{2,3},{3,2},{4,5},{5,4},{6,7},{7,6},{8,9},{9,8},{10,11... | collective-permute-start | bytes 2162696 | tf_op jit(solution)/shard_map/ppermute | solution.py:439
  719.4 25.4 %collective-permute-start.56 = (bf16[256,2176]{1,0:T(8,128)(2,1)}, bf16[256,2176]{1,0:T(8,128)(2,1)}, u32[]{:S(2)}, u32[]{:S(2)}) collective-permute-start(bf16[256,2176]{1,0:T(8,128)(2,1)} %convolution_convert_fusion.5), channel_id=1, source_target_pairs={{0,4},{4,0},{8,12},{12,8},{16,20},{20,16},{24,28},{28,24},{1,5},{5... | collective-permute-start | bytes 3342344 | tf_op jit(solution)/shard_map/ppermute | solution.py:427
  736.5 32.0 %collective-permute-start.71 = (bf16[256,2816]{1,0:T(8,128)(2,1)S(1)}, bf16[256,2816]{1,0:T(8,128)(2,1)S(1)}, u32[]{:S(2)}, u32[]{:S(2)}) collective-permute-start(bf16[256,2816]{1,0:T(8,128)(2,1)S(1)} %add_convert_fusion.refs_0_), channel_id=1, source_target_pairs={{0,2},{1,3},{2,0},{3,1},{4,6},{5,7},{6,4},{7,5},{8,10},{9,11},{10,... | collective-permute-start | bytes 4325384 | tf_op jit(solution)/shard_map/ppermute | solution.py:442
  744.8 24.4 %collective-permute-start.62 = (bf16[256,2176]{1,0:T(8,128)(2,1)}, bf16[256,2176]{1,0:T(8,128)(2,1)S(1)}, u32[]{:S(2)}, u32[]{:S(2)}) collective-permute-start(bf16[256,2176]{1,0:T(8,128)(2,1)} %convolution_convert_fusion.6), channel_id=1, source_target_pairs={{0,4},{4,0},{8,12},{12,8},{16,20},{20,16},{24,28},{28,24},{1,5},{5... | collective-permute-start | bytes 3342344 | tf_op jit(solution)/shard_map/ppermute | solution.py:427
  756.3 29.4 %collective-permute-start.69 = (bf16[256,2176]{1,0:T(8,128)(2,1)S(1)}, bf16[256,2176]{1,0:T(8,128)(2,1)}, u32[]{:S(2)}, u32[]{:S(2)}) collective-permute-start(bf16[256,2176]{1,0:T(8,128)(2,1)S(1)} %add_convert_fusion.7), channel_id=1, source_target_pairs={{0,8},{4,12},{8,16},{12,20},{16,24},{20,28},{24,0},{28,4},{1,9},{5... | collective-permute-start | bytes 3342344 | tf_op jit(solution)/shard_map/ppermute | solution.py:424
  756.8 39.2 %collective-permute-start.68 = (bf16[128,2048]{1,0:T(8,128)(2,1)S(1)}, bf16[128,2048]{1,0:T(8,128)(2,1)S(1)}, u32[]{:S(2)}, u32[]{:S(2)}) collective-permute-start(bf16[128,2048]{1,0:T(8,128)(2,1)S(1)} %add_convert_fusion.18), channel_id=1, source_target_pairs={{0,8},{4,12},{8,16},{12,20},{16,24},{20,28},{24,0},{28,4},{1,9},{5... | collective-permute-start | bytes 1572872 | tf_op jit(solution)/shard_map/ppermute | solution.py:424
  768.5 34.5 %collective-permute-start.70 = (bf16[256,2816]{1,0:T(8,128)(2,1)S(1)}, bf16[256,2816]{1,0:T(8,128)(2,1)S(1)}, u32[]{:S(2)}, u32[]{:S(2)}) collective-permute-start(bf16[256,2816]{1,0:T(8,128)(2,1)S(1)} %add_convert_fusion.refs_0_), channel_id=1, source_target_pairs={{0,1},{1,0},{2,3},{3,2},{4,5},{5,4},{6,7},{7,6},{8,9},{9,8},{10,11... | collective-permute-start | bytes 4325384 | tf_op jit(solution)/shard_map/ppermute | solution.py:439
  768.5 35.6 %collective-permute-start.72 = (bf16[256,2816]{1,0:T(8,128)(2,1)S(1)}, bf16[256,2816]{1,0:T(8,128)(2,1)}, u32[]{:S(2)}, u32[]{:S(2)}) collective-permute-start(bf16[256,2816]{1,0:T(8,128)(2,1)S(1)} %collective-permute-done.71.refs_2_), channel_id=1, source_target_pairs={{0,1},{1,0},{2,3},{3,2},{4,5},{5,4},{6,7},{7,6},{8,9},{9,8},{10,11... | collective-permute-start | bytes 4325384 | tf_op jit(solution)/shard_map/ppermute | solution.py:439
  769.2 46.1 %collective-permute-start.66 = (bf16[256,2176]{1,0:T(8,128)(2,1)}, bf16[256,2176]{1,0:T(8,128)(2,1)}, u32[]{:S(2)}, u32[]{:S(2)}) collective-permute-start(bf16[256,2176]{1,0:T(8,128)(2,1)} %convolution_convert_fusion.7), channel_id=1, source_target_pairs={{0,4},{4,0},{8,12},{12,8},{16,20},{20,16},{24,28},{28,24},{1,5},{5... | collective-permute-start | bytes 3342344 | tf_op jit(solution)/shard_map/ppermute | solution.py:427
  796.0 23.4 %collective-permute-start.76 = (bf16[256,2176]{1,0:T(8,128)(2,1)}, bf16[256,2176]{1,0:T(8,128)(2,1)}, u32[]{:S(2)}, u32[]{:S(2)}) collective-permute-start(bf16[256,2176]{1,0:T(8,128)(2,1)} %add_convert_fusion.6), channel_id=1, source_target_pairs={{0,24},{4,28},{8,0},{12,4},{16,8},{20,12},{24,16},{28,20},{1,25},{... | collective-permute-start | bytes 3342344 | tf_op jit(solution)/shard_map/ppermute | solution.py:424
  801.7 20.9 %collective-permute-start.75 = (bf16[128,2048]{1,0:T(8,128)(2,1)S(1)}, bf16[128,2048]{1,0:T(8,128)(2,1)}, u32[]{:S(2)}, u32[]{:S(2)}) collective-permute-start(bf16[128,2048]{1,0:T(8,128)(2,1)S(1)} %add_convert_fusion.17), channel_id=1, source_target_pairs={{2,6},{3,7},{4,0},{5,1},{10,14},{11,15},{12,8},{13,9},{18,22},{19,... | collective-permute-start | bytes 1572872 | tf_op jit(solution)/shard_map/ppermute | solution.py:436
  826.9 33.0 %collective-permute-start.79 = (bf16[256,2048]{1,0:T(8,128)(2,1)}, bf16[256,2048]{1,0:T(8,128)(2,1)S(1)}, u32[]{:S(2)}, u32[]{:S(2)}) collective-permute-start(bf16[256,2048]{1,0:T(8,128)(2,1)} %pad_maximum_fusion.6), channel_id=1, source_target_pairs={{0,2},{1,3},{2,0},{3,1},{4,6},{5,7},{6,4},{7,5},{8,10},{9,11},{10,... | collective-permute-start | bytes 3145736 | tf_op jit(solution)/shard_map/ppermute | solution.py:442
  826.9 34.7 %collective-permute-start.73 = (bf16[256,2176]{1,0:T(8,128)(2,1)}, bf16[256,2176]{1,0:T(8,128)(2,1)}, u32[]{:S(2)}, u32[]{:S(2)}) collective-permute-start(bf16[256,2176]{1,0:T(8,128)(2,1)} %convolution_convert_fusion.8), channel_id=1, source_target_pairs={{0,4},{4,0},{8,12},{12,8},{16,20},{20,16},{24,28},{28,24},{1,5},{5... | collective-permute-start | bytes 3342344 | tf_op jit(solution)/shard_map/ppermute | solution.py:427
  827.5 34.1 %collective-permute-start.80 = (bf16[256,2176]{1,0:T(8,128)(2,1)S(1)}, bf16[256,2176]{1,0:T(8,128)(2,1)}, u32[]{:S(2)}, u32[]{:S(2)}) collective-permute-start(bf16[256,2176]{1,0:T(8,128)(2,1)S(1)} %add_convert_fusion.5), channel_id=1, source_target_pairs={{0,8},{4,12},{8,16},{12,20},{16,24},{20,28},{24,0},{28,4},{1,9},{5... | collective-permute-start | bytes 3342344 | tf_op jit(solution)/shard_map/ppermute | solution.py:424
  828.6 26.7 %collective-permute-start.74 = (f32[4352]{0:T(1024)S(1)}, f32[4352]{0:T(1024)S(1)}, u32[]{:S(2)}, u32[]{:S(2)}) collective-permute-start(f32[4352]{0:T(1024)S(1)} %copy-done.76), channel_id=1, source_target_pairs={{0,8},{4,12},{8,0},{12,4},{16,24},{20,28},{24,16},{28,20},{1,9},{5... | collective-permute-start | bytes 52232 | tf_op jit(solution)/shard_map/ppermute | solution.py:465
  869.7 21.6 %collective-permute-start.82 = (bf16[256,1024]{1,0:T(8,128)(2,1)S(1)}, bf16[256,1024]{1,0:T(8,128)(2,1)S(1)}, u32[]{:S(2)}, u32[]{:S(2)}) collective-permute-start(bf16[256,1024]{1,0:T(8,128)(2,1)S(1)} %add_convert_fusion.15.refs_0_), channel_id=1, source_target_pairs={{0,2},{1,3},{2,0},{3,1},{4,6},{5,7},{6,4},{7,5},{8,10},{9,11},{10,... | collective-permute-start | bytes 1572872 | tf_op jit(solution)/shard_map/ppermute | solution.py:442
  870.3 31.9 %collective-permute-start.84 = (bf16[256,1152]{1,0:T(8,128)(2,1)S(1)}, bf16[256,1152]{1,0:T(8,128)(2,1)S(1)}, u32[]{:S(2)}, u32[]{:S(2)}) collective-permute-start(bf16[256,1152]{1,0:T(8,128)(2,1)S(1)} %add_convert_fusion.14.refs_1_), channel_id=1, source_target_pairs={{0,1},{1,0},{2,3},{3,2},{4,5},{5,4},{6,7},{7,6},{8,9},{9,8},{10,11... | collective-permute-start | bytes 1769480 | tf_op jit(solution)/shard_map/ppermute | solution.py:439
  (120 other events, 1786.4 us)

commit v3 on v2

--- a/solution.py
+++ b/solution.py
@@ -628,7 +628,8 @@
     bias = jnp.pad(b_decay, (0, EXTRA - heads))[None]
     gated, kept, cum, cum_rows = retention(projected, bias, seg_col, seg_col.T, width, head_dim)
     gated = put(gated)
-    o_own_3 = put(o_ring)
+    o_own_3, g_own_1, g_0 = put(o_ring), put(g_ring), put(g_0)
+    g_ring, g_1 = links.around(g_own_1), links.across(g_own_1)
     out_w = blocks_at(
         jnp.concatenate([o_own_2, o_own_1, o_own_3, out_block], axis=0),
         [links.spot((links.turn - j) % links.ring) for j in range(links.ring)],
@@ -648,25 +649,20 @@
 
     gated_own = links.own_order(gated)
     going = tokens_start(gated_own, out_w, (1, 0))
-    g_own_1 = put(g_ring)
-    g_ring = links.around(g_own_1)
-    g_0 = put(g_0)
-    g_1 = links.across(g_own_1)
+    g_own_2 = put(g_ring)
+    g_ring = links.around(g_own_2)
+    g_1 = put(g_1)
+    g_2 = links.across(g_own_2)
     mixed = put(tokens + tokens_end(going, gated_own, out_w, (1, 0)))
     scale_two = rms(mixed)
     sent = put(links.to_rel((mixed * scale_two * gain_ffn).astype(LOW)))
     n_far, n_near = links.chip(sent), links.core(sent)
-    g_own_2 = put(g_ring)
-    g_ring = links.around(g_own_2)
-    g_1 = put(g_1)
-    g_2 = links.across(g_own_2)
+    g_own_3, g_2 = put(g_ring), put(g_2)
+    g_3 = links.across(g_own_3)
+    d_ring = links.around(put(down_share))
     n_far, n_near = put(n_far), put(n_near)
     n_both = put(links.core(n_far))
     normed_ffn = put(jnp.concatenate([n_near, n_both, n_far, sent], axis=0))
-    g_own_3 = put(g_ring)
-    d_ring = links.around(put(down_share))
-    g_2 = put(g_2)
-    g_3 = links.across(g_own_3)
     d_own_1 = put(d_ring)
     d_ring = links.around(d_own_1)
     p_pieces = [after(piece, d_own_1) for piece in p_pieces]
@@ -718,108 +714,104 @@
     grad_ffn = put(jnp.concatenate([n_near, n_both, n_far, sent], axis=0))
     whole = dot(activated, grad_ffn, 0, 0).astype(LOW)
     places = links.sources()
-    d_come = [links.across(put(blocks_at(whole, places[i : i + 2], part, 0))) for i in (4, 6)]
+    d_go = [put(blocks_at(whole, places[i:k], part, 0)) for i, k in ((4, 5), (5, 6), (6, 8))]
+    d_come = [links.across(d_go[0])]
     grad_act = dot(after(grad_ffn, order.last), down_w, 1, 1)
     sigma = jax.nn.sigmoid(gate_part)
     grad_gate = grad_act * up_part * sigma * (1.0 + gate_part * (1.0 - sigma))
     grad_up = grad_act * gate_part * sigma
     grad_both = put(jnp.concatenate([grad_gate, grad_up], axis=1).astype(LOW))
-    going = tokens_start(grad_both, gu_w, (1, 1))
     d_come[0] = put(d_come[0])
+    d_come.append(links.across(put(d_go[1])))
+    back = after(grad_both, order.last)
+    come = links.core(put(dot(back[: 2 * count], gu_w, 1, 1).astype(LOW)))
+    d_come[1] = put(d_come[1])
+    d_come.append(links.across(put(d_go[2])))
+    far = dot(back[2 * count : 3 * count], gu_w, 1, 1) + come[count:].astype(WIDE)
+    going = come, links.chip(put(far.astype(LOW)))
+    d_first = sum_low(blocks_at(whole, places[1:2], part, 0), d_come[1])
+    d_second = sum_low(blocks_at(whole, places[0:1], part, 0), d_come[0])
+    d_second, d_first = links.around(put(d_second), 1), links.around(put(d_first), -1)
     g_other = [put(rows_of(after(normed_ffn, order.last), grad_both, 4))]
-    d_sums = put(sum_low(blocks_at(whole, places[:2], part, 0), d_come[0]))
-    d_second, d_first = jnp.split(d_sums, 2, axis=0)
-    d_second, d_first = links.around(d_second, 1), links.around(d_first, -1)
+    d_come[2] = put(d_come[2])
+    g_come = [links.across(put(g_other[0]))]
     grad_normed = links.from_rel(tokens_end(going, grad_both, gu_w, (1, 1)))
     grad_mid, gain_ffn_grad = norm_back(grad_normed, mixed, scale_two, gain_ffn)
     grad_mixed = grad_out + grad_mid
     sent = put(grad_mixed.astype(LOW))
     n_far, n_near = links.chip(sent), links.core(sent)
-    d_come[1] = put(d_come[1])
-    g_come = [links.across(put(g_other[0]))]
-    d_second = put(d_second)
-    d_third = put(sum_low(blocks_at(whole, places[2:3], part, 0), d_come[1][:part], d_second))
+    d_second, d_first = put(d_second), put(d_first)
+    d_third = put(sum_low(blocks_at(whole, places[2:3], part, 0), d_come[2][:part], d_second))
     d_third = links.around(d_third, 1)
-    for i in (5, 6, 7):
+    g_come[0] = put(g_come[0])
+    g_other.append(put(rows_of(after(normed_ffn, order.last), grad_both, 5)))
+    g_come.append(links.across(g_other[1]))
+    for i in (6, 7):
         g_other.append(put(rows_of(after(normed_ffn, order.last), grad_both, i)))
     n_far, n_near = put(n_far), put(n_near)
     n_both = put(links.core(n_far))
     grad_att = put(in_row_order([sent, n_near, n_far, n_both]))
-    grad_gated = put(dot(grad_att, out_w, 1, 1))
-    left = blocks_at(gated, [(links.turn - r) % links.ring for r in ORDER], head_dim, 1)
-    g_come[0] = put(g_come[0])
-    g_come.append(links.across(put(g_other[1])))
-    g_second = links.around(put(rows_of(normed_ffn, grad_both, 0, g_come[0])), 1)
-    d_first, d_third = put(d_first), put(d_third)
-    d_total = put(sum_low(blocks_at(whole, places[3:4], part, 0), d_come[1][part:], d_first, d_third))
-    d_pieces = gather_seq(d_total)
-    grad_proj, bias_local = retention_back(
-        projected, bias, kept, after(grad_gated, d_total), cum, cum_rows, seg_col, seg_col.T, width, head_dim
-    )
-    grad_proj = put(grad_proj)
     g_come[1] = put(g_come[1])
     g_come.append(links.across(put(g_other[2])))
-    g_second = put(g_second)
-    g_first = links.around(put(rows_of(normed_ffn, grad_both, 1, g_come[1])), -1)
-    back_rows = links.own_order(grad_proj)
-    going = tokens_start(back_rows, proj_w, (1, 1))
+    grad_gated = put(dot(after(grad_att, order.last), out_w, 1, 1))
+    d_third = put(d_third)
+    g_second = links.around(put(rows_of(normed_ffn, grad_both, 0, after(g_come[0], order.last))), 1)
+    left = blocks_at(gated, [(links.turn - r) % links.ring for r in ORDER], head_dim, 1)
+    o_sums = put(dot(left, after(grad_att, order.last), 0, 0).astype(LOW))
+    o_second, o_first, o_third, o_mine = jnp.split(o_sums, 4, axis=0)
+    o_second, o_first = links.around(o_second, 1), links.around(o_first, -1)
+    grad_proj, bias_local = retention_back(
+        projected, bias, kept, after(grad_gated, order.last), cum, cum_rows, seg_col, seg_col.T, width, head_dim
+    )
+    grad_proj = put(grad_proj)
+    g_second, g_come[2] = put(g_second), put(g_come[2])
+    g_come.append(links.across(put(g_other[3])))
     p_other = [put(rows_of(normed, after(grad_proj, order.last), 4))]
-    g_come[2] = put(g_come[2])
-    g_come.append(links.across(put(g_other[3])))
-    g_third = put(rows_of(normed_ffn, grad_both, 2, g_come[2], g_second))
-    g_first = put(g_first)
-    g_third = links.around(g_third, 1)
-    for i in (5, 6, 7):
-        p_other.append(put(rows_of(normed, grad_proj, i)))
+    back_rows = links.own_order(after(grad_proj, order.last))
+    come = put(dot(back_rows[: 2 * count], proj_w, 1, 1).astype(LOW))
+    come = links.core(come)
+    g_first = links.around(put(rows_of(normed_ffn, grad_both, 1, after(g_come[1], order.last))), -1)
+    o_second, o_first = put(o_second), put(o_first)
+    o_third = links.around(put(sum_low(o_third, o_second)), 1)
+    g_come[3] = put(g_come[3])
+    p_come = [links.across(p_other[0])]
+    g_third = links.around(put(rows_of(normed_ffn, grad_both, 2, after(g_come[2], order.last), g_second)), 1)
+    p_other.append(put(rows_of(normed, after(grad_proj, order.last), 5)))
+    p_come[0] = put(p_come[0])
+    p_come.append(links.across(p_other[1]))
+    far = dot(after(back_rows[2 * count : 3 * count], order.last), proj_w, 1, 1) + come[count:].astype(WIDE)
+    going = come, links.chip(put(far.astype(LOW)))
+    g_first, o_third = put(g_first), put(o_third)
+    p_other.append(put(rows_of(normed, after(grad_proj, order.last), 6)))
+    p_come[1] = put(p_come[1])
+    p_come.append(links.across(p_other[2]))
+    p_second = links.around(put(rows_of(normed, after(grad_proj, order.last), 0, p_come[0])), 1)
+    d_total = put(sum_low(blocks_at(whole, places[3:4], part, 0), d_come[2][part:], d_first, d_third))
+    g_third = put(g_third)
     grad_normed_one = links.from_rel(tokens_end(going, back_rows, proj_w, (1, 1)))
+    d_pieces = gather_seq(after(d_total, order.last))
+    p_other.append(put(rows_of(normed, after(grad_proj, order.last), 7)))
+    p_come[2] = put(p_come[2])
+    p_come.append(links.across(p_other[3]))
+    p_first = links.around(put(rows_of(normed, after(grad_proj, order.last), 1, p_come[1])), -1)
     grad_first, gain_ret_grad = norm_back(grad_normed_one, tokens, scale_one, gain_ret)
     grad_tokens = put(grad_mixed + grad_first)
     scalars = jnp.pad(jnp.stack([squared_local, count_local]), (0, EXTRA - 2))
     totals = put(jnp.concatenate([gain_ret_grad, gain_ffn_grad, bias_local[0], scalars]))
     totals_steps = links.total_steps()
-    g_come[3] = put(g_come[3])
-    p_come = [links.across(put(p_other[0]))]
     totals = totals_steps[0](totals)
-    g_third = put(g_third)
-    o_sums = put(dot(left, after(grad_att, order.last), 0, 0).astype(LOW))
-    o_second, o_first, o_third, o_mine = jnp.split(o_sums, 4, axis=0)
-    o_second, o_first = links.around(o_second, 1), links.around(o_first, -1)
-    g_total = put(rows_of(normed_ffn, grad_both, 3, g_come[3], g_first, g_third))
+    p_second = put(p_second)
+    p_third = links.around(put(rows_of(normed, grad_proj, 2, p_come[2], p_second)), 1)
+    g_total = put(rows_of(normed_ffn, after(grad_both, order.last), 3, g_come[3], g_first, g_third))
     g_pieces = gather_seq(g_total)
     totals = totals_steps[1](put(totals))
+    o_total = put(sum_low(o_mine, o_first, o_third))
+    p_first = put(p_first)
     down_grad = put(whole_down(part, shard, [put(piece) for piece in d_pieces]))
-    p_come[0] = put(p_come[0])
-    p_come.append(links.across(put(p_other[1])))
-    o_second, o_first = put(o_second), put(o_first)
-    o_third = put(sum_low(o_third, o_second))
-    p_second = links.around(put(rows_of(normed, grad_proj, 0, p_come[0])), 1)
-    o_third = links.around(o_third, 1)
-    totals = totals_steps[2](put(totals))
-    p_come[1] = put(p_come[1])
-    p_come.append(links.across(put(p_other[2])))
-    p_second, o_third = put(p_second), put(o_third)
-    p_first = links.around(put(rows_of(normed, grad_proj, 1, p_come[1])), -1)
-    o_total = put(sum_low(o_mine, o_first, o_third))
-    o_come = links.across_one_way(o_total, True)
-    g_pieces = [put(piece) for piece in g_pieces]
-    gu_grad = put(whole_gate_up(part, shard, dp_count, g_pieces))
-    totals = totals_steps[3](put(totals))
-    p_come[2] = put(p_come[2])
-    p_come.append(links.across(put(p_other[3])))
-    p_first = put(p_first)
-    p_third = links.around(put(rows_of(normed, grad_proj, 2, p_come[2], p_second)), 1)
-    o_mine = put(sum_low(o_total, put(o_come)))
-    o_near = put(links.core(o_mine))
-    pair = jnp.concatenate(
-        [jnp.where(first_core, o_mine, o_near), jnp.where(first_core, o_near, o_mine)], axis=0
-    )
-    o_far = links.chip(put(pair))
-    totals = totals_steps[4](put(totals))
-    out_grad = put(jnp.where(x_half == links.side, pair, put(o_far)).astype(WIDE))
+    o_come = links.across_one_way(after(o_total, order.last), True)
     totals = put(totals)
     p_come[3], p_third = put(p_come[3]), put(p_third)
     half = 2 * width * head_dim
-    proj_grad = []
     p_pieces = []
     for start, stop in ((0, half), (half, 2 * half + EXTRA)):
         total = rows_of(
@@ -827,9 +819,21 @@
             p_come[3][:, start:stop], p_first[:, start:stop], p_third[:, start:stop],
         )
         p_pieces.append(gather_seq(put(total)))
-    proj_grad = whole_proj(2 * width, 0, head_dim, [], [put(piece) for piece in p_pieces[0]])
+    o_mine = put(sum_low(o_total, put(o_come)))
+    o_near = put(links.core(o_mine))
+    pair = jnp.concatenate(
+        [jnp.where(first_core, o_mine, o_near), jnp.where(first_core, o_near, o_mine)], axis=0
+    )
+    o_far = links.chip(put(pair))
+    totals = totals_steps[2](totals)
+    g_pieces = [put(piece) for piece in g_pieces]
+    gu_grad = put(whole_gate_up(part, shard, dp_count, g_pieces))
+    totals = totals_steps[4](totals_steps[3](put(totals)))
+    proj_grad = put(whole_proj(2 * width, 0, head_dim, [], [put(piece) for piece in p_pieces[0]]))
+    totals = put(totals)
     decay_grad = sum(piece[:, half : half + heads].astype(WIDE) for piece in p_pieces[1])
     proj_grad = whole_proj(2 * width, 1, head_dim, [proj_grad], p_pieces[1])
+    out_grad = jnp.where(x_half == links.side, pair, put(o_far)).astype(WIDE)
 
     gain_ret_total, gain_ffn_total = totals[:model_width], totals[model_width : 2 * model_width]
     bias_total = totals[2 * model_width : 2 * model_width + heads]

time: 923 us -> 905 us (0.980)
  waiting for transfers between devices: 466 us -> 454 us
    ppermute x5, waiting for transfers between devices: 44.1 us -> 8.73 us  [step(): return lambda value: value + lax.ppermute(value, axis, pairs)]
    ppermute x22 -> x23, waiting for transfers between devices: 121 us -> 136 us  [across(): return lax.ppermute(value, 'dp', [(d, d ^ 1) for d in range(self.dp_count)])]
    ppermute x24, waiting for transfers between devices: 193 us -> 205 us  [around(): lax.ppermute(value, 'dp', [(d, (d + 2 * by) % count) for d in range(count)])]
    unnamed x256 -> x232, local copies, waits for them, and re-layouts: 49.3 us -> 47.9 us
    ppermute x22 -> x23, starting transfers between devices: 19 us -> 18.9 us  [across(): return lax.ppermute(value, 'dp', [(d, d ^ 1) for d in range(self.dp_count)])]
  transfers between devices with their start and end apart: 87 -> 88, of which waited for: 48 -> 46; matrix products, arithmetic and copies ran while one was open for 18% -> 22% of each run, Pallas kernels for 12% -> 13%
where the time goes in v3:
time: 905 us; the launch traced here: 893 us
  waiting for transfers between devices  454 us (50%)
  matrix products  159 us (18%)
  Pallas kernels  118 us (13%)
  starting transfers between devices  62.5 us (7%)
  local copies, waits for them, and re-layouts  56.3 us (6%)
  other arithmetic  37.4 us (4%)
    ppermute x24, waiting for transfers between devices, around(): lax.ppermute(value, 'dp', [(d, (d + 2 * by) % count) for d in range(count)])  205 us
    dot_general x33, matrix products, dot(): lax.dot_general(left, right, (((left_dim,), (right_dim,)), ((), ())), pre...  159 us
    ppermute x23, waiting for transfers between devices, across(): return lax.ppermute(value, 'dp', [(d, d ^ 1) for d in range(self.dp_count)])  136 us
    ppermute x13, waiting for transfers between devices, chip(): lax.ppermute(value, 'seq', [(s, s ^ 2) for s in range(self.seq_count)])  75.1 us
    unnamed x232, local copies, waits for them, and re-layouts  47.9 us
    pallas_call x1, Pallas kernels, gate_up_product(): pl.pallas_call(functools.partial(gate_up_kernel, count), grid=(steps,), i...  20 us
    pallas_call x1, Pallas kernels, retention_back(): pl.pallas_call(functools.partial(backward_kernel, row // 4, size ** (-0.5...  19.6 us
    ppermute x23, starting transfers between devices, across(): return lax.ppermute(value, 'dp', [(d, d ^ 1) for d in range(self.dp_count)])  18.9 us
  transfers between devices with their start and end apart: 88, of which 46 were waited for; matrix products, arithmetic and copies ran while one was open for 22% of the time, Pallas kernels for 13%

profile of v3, /device:TPU:0, one launch (start us, length us, event | category | flops | bytes accessed | tf_op | source)
XLA Modules:
  0.0 892.9 jit_solution(9510460154648656149)
XLA Ops:
  2.1 4.2 shard_map.212.refs_4_
  21.2 5.8 shard_map.213.refs_4_.refs_12_
  27.0 9.2 %collective-permute-done.2.refs_2_ = bf16[256,2176]{1,0:T(8,128)(2,1)} collective-permute-done((bf16[256,2176]{1,0:T(8,128)(2,1)}, bf16[256,2176]{1,0:T(8,128)(2,1)}, u32[]{:S(2)}, u32[]{:S(2)}) %collective-permute-start.2) | collective-permute-done | bytes 1114144 | tf_op jit(solution)/shard_map/ppermute | solution.py:424
  36.3 7.2 collective-permute-done.3.refs_2_
  49.2 4.6 shard_map.215.refs_0_
  53.9 5.8 collective-permute-done.6
  59.7 12.8 %collective-permute-done.5.refs_1_ = bf16[256,2176]{1,0:T(8,128)(2,1)} collective-permute-done((bf16[256,2176]{1,0:T(8,128)(2,1)}, bf16[256,2176]{1,0:T(8,128)(2,1)}, u32[]{:S(2)}, u32[]{:S(2)}) %collective-permute-start.5) | collective-permute-done | bytes 1114144 | tf_op jit(solution)/shard_map/ppermute | solution.py:424
  74.4 9.3 %collective-permute-done.8.refs_6_ = bf16[256,2176]{1,0:T(8,128)(2,1)} collective-permute-done((bf16[256,2176]{1,0:T(8,128)(2,1)}, bf16[256,2176]{1,0:T(8,128)(2,1)}, u32[]{:S(2)}, u32[]{:S(2)}) %collective-permute-start.8) | collective-permute-done | bytes 1114144 | tf_op jit(solution)/shard_map/ppermute | solution.py:427
  83.7 18.4 %collective-permute-done.7.refs_3_ = bf16[256,2176]{1,0:T(8,128)(2,1)} collective-permute-done((bf16[256,2176]{1,0:T(8,128)(2,1)}, bf16[256,2176]{1,0:T(8,128)(2,1)}, u32[]{:S(2)}, u32[]{:S(2)}) %collective-permute-start.7) | collective-permute-done | bytes 1114144 | tf_op jit(solution)/shard_map/ppermute | solution.py:424
  102.6 4.9 collective-permute-done.9.refs_5_
  107.5 4.4 collective-permute-done.11
  114.3 12.2 %collective-permute-done.12 = bf16[128,2048]{1,0:T(8,128)(2,1)} collective-permute-done((bf16[128,2048]{1,0:T(8,128)(2,1)S(1)}, bf16[128,2048]{1,0:T(8,128)(2,1)}, u32[]{:S(2)}, u32[]{:S(2)}) %collective-permute-start.12) | collective-permute-done | bytes 524320 | tf_op jit(solution)/shard_map/ppermute | solution.py:424
  135.4 16.2 %shard_map.216.q.k.v.gate.logit = f32[1024,2176]{1,0:T(8,128)} custom-call(bf16[1024,2176]{1,0:T(8,128)(2,1)} %shard_map.215.refs_0_, bf16[256,2176]{1,0:T(8,128)(2,1)} %collective-permute-done.5.refs_1_, bf16[256,2176]{1,0:T(8,128)(2,1)} %collective-permute-done.2.refs_2_, bf16[256,2176]{1,0:T(8,128)(2,1)} %collective-permute-done.7.refs_3_, ...), custom_call_target="tpu_custom_call" | custom-call | tf_op jit(solution)/shard_map/pallas_call | solution.py:53
  151.6 11.6 %shard_map.217 = (bf16[1024,512]{1,0:T(8,128)(2,1)}, f32[1024,512]{1,0:T(8,128)}, f32[1024,128]{1,0:T(8,128)}, f32[128,1024]{1,0:T(8,128)}) custom-call(f32[1024,2176]{1,0:T(8,128)} %shard_map.216.q.k.v.gate.logit, f32[1024,2176]{1,0:T(8,128)} %shard_map.216.q.k.v.gate.logit, f32[1024,2176]{1,0:T(8,128)} %shard_map.216.q.k.v.gate.logit, ...), custom_call_target="tpu_custom_call" | custom-call | tf_op jit(solution)/shard_map/pallas_call | solution.py:367
  172.8 4.0 collective-permute-done.16
  181.8 26.4 %collective-permute-done.19.refs_1_.refs_9_ = bf16[256,2816]{1,0:T(8,128)(2,1)} collective-permute-done((bf16[256,2816]{1,0:T(8,128)(2,1)S(1)}, bf16[256,2816]{1,0:T(8,128)(2,1)}, u32[]{:S(2)}, u32[]{:S(2)}) %collective-permute-start.19) | collective-permute-done | bytes 1441824 | tf_op jit(solution)/shard_map/ppermute | solution.py:424
  216.9 27.0 %collective-permute-done.23.refs_3_.refs_11_ = bf16[256,2816]{1,0:T(8,128)(2,1)S(1)} collective-permute-done((bf16[256,2816]{1,0:T(8,128)(2,1)}, bf16[256,2816]{1,0:T(8,128)(2,1)S(1)}, u32[]{:S(2)}, u32[]{:S(2)}) %collective-permute-start.23) | collective-permute-done | bytes 1441824 | tf_op jit(solution)/shard_map/ppermute | solution.py:424
  249.0 15.5 %collective-permute-done.26 = bf16[176,2048]{1,0:T(8,128)(2,1)} collective-permute-done((bf16[176,2048]{1,0:T(8,128)(2,1)S(1)}, bf16[176,2048]{1,0:T(8,128)(2,1)}, u32[]{:S(2)}, u32[]{:S(2)}) %collective-permute-start.26) | collective-permute-done | bytes 720928 | tf_op jit(solution)/shard_map/ppermute | solution.py:424
  273.3 4.7 collective-permute-done.25.refs_7_.refs_15_
  281.2 20.0 %shard_map.218 = (f32[1024,1408]{1,0:T(8,128)}, f32[1024,1408]{1,0:T(8,128)}, bf16[1024,1408]{1,0:T(8,128)(2,1)}) custom-call(bf16[1024,2048]{1,0:T(8,128)(2,1)} %pad_maximum_fusion.1.refs_0_, bf16[256,2816]{1,0:T(8,128)(2,1)} %collective-permute-done.19.refs_1_.refs_9_, bf16[256,2816]{1,0:T(8,128)(2,1)} %copy-done.10, bf16[256,2816]{1,0:T(8,128)(2,1)} %copy-done.14, ...), custom_call_target="tpu_custom_call" | custom-call | tf_op jit(solution)/shard_map/pallas_call | solution.py:84
  301.2 11.2 %collective-permute-done.29 = bf16[176,2048]{1,0:T(8,128)(2,1)} collective-permute-done((bf16[176,2048]{1,0:T(8,128)(2,1)}, bf16[176,2048]{1,0:T(8,128)(2,1)}, u32[]{:S(2)}, u32[]{:S(2)}) %collective-permute-start.29) | collective-permute-done | bytes 720928 | tf_op jit(solution)/shard_map/ppermute | solution.py:427
  325.2 6.0 collective-permute-done.28
  333.0 14.0 %collective-permute-done.32 = bf16[176,2048]{1,0:T(8,128)(2,1)S(1)} collective-permute-done((bf16[176,2048]{1,0:T(8,128)(2,1)S(1)}, bf16[176,2048]{1,0:T(8,128)(2,1)S(1)}, u32[]{:S(2)}, u32[]{:S(2)}) %collective-permute-start.32) | collective-permute-done | bytes 720928 | tf_op jit(solution)/shard_map/ppermute | solution.py:427
  354.3 4.1 collective-permute-done.33
  362.5 23.0 %collective-permute-done.34 = bf16[256,2048]{1,0:T(8,128)(2,1)S(1)} collective-permute-done((bf16[256,2048]{1,0:T(8,128)(2,1)S(1)}, bf16[256,2048]{1,0:T(8,128)(2,1)S(1)}, u32[]{:S(2)}, u32[]{:S(2)}) %collective-permute-start.34) | collective-permute-done | bytes 1048608 | tf_op jit(solution)/shard_map/ppermute | solution.py:442
  385.6 5.3 fusion.98
  392.4 23.2 %collective-permute-done.36 = bf16[256,2048]{1,0:T(8,128)(2,1)} collective-permute-done((bf16[256,2048]{1,0:T(8,128)(2,1)}, bf16[256,2048]{1,0:T(8,128)(2,1)}, u32[]{:S(2)}, u32[]{:S(2)}) %collective-permute-start.36) | collective-permute-done | bytes 1048608 | tf_op jit(solution)/shard_map/ppermute | solution.py:442
  421.2 6.5 convolution_convert_fusion
  432.4 8.5 fusion.102
  440.9 5.0 multiply_convert_fusion.1
  449.1 9.0 %convolution_convert_fusion.10 = bf16[512,2048]{1,0:T(8,128)(2,1)S(1)} fusion(bf16[2048,2816]{1,0:T(8,128)(2,1)} %copy-done.59, bf16[1024,2816]{1,0:T(8,128)(2,1)S(1)} %pad_maximum_fusion), kind=kOutput, calls=%fused_computation.23 | convolution fusion | flops 5906628608 | bytes 16515072 | tf_op jit(solution)/shard_map/dot_general | solution.py:18
  459.2 17.6 %collective-permute-done.40 = bf16[176,2048]{1,0:T(8,128)(2,1)S(1)} collective-permute-done((bf16[176,2048]{1,0:T(8,128)(2,1)S(1)}, bf16[176,2048]{1,0:T(8,128)(2,1)S(1)}, u32[]{:S(2)}, u32[]{:S(2)}) %collective-permute-start.40) | collective-permute-done | bytes 720928 | tf_op jit(solution)/shard_map/ppermute | solution.py:427
  477.6 9.2 %add_convert_fusion.6 = bf16[256,2048]{1,0:T(8,128)(2,1)} fusion(bf16[512,2048]{1,0:T(8,128)(2,1)S(1)} %collective-permute-done.39, bf16[2048,2816]{1,0:T(8,128)(2,1)} %copy-done.59, bf16[1024,2816]{1,0:T(8,128)(2,1)S(1)} %pad_maximum_fusion), kind=kOutput, calls=%fused_computation.59 | convolution fusion | flops 2954362880 | bytes 15073280 | tf_op jit(solution)/shard_map/dot_general | solution.py:18
  491.7 4.2 collective-permute-start.47
  495.9 5.4 convolution_convert_fusion.4
  501.4 8.8 collective-permute-done.42
  511.6 9.0 %convert_add_fusion.1 = f32[256,2048]{1,0:T(8,128)} fusion(bf16[256,2048]{1,0:T(8,128)(2,1)} %collective-permute-done.41, bf16[512,2048]{1,0:T(8,128)(2,1)S(1)} %copy-done.68, bf16[2048,2816]{1,0:T(8,128)(2,1)} %copy-done.59, bf16[1024,2816]{1,0:T(8,128)(2,1)S(1)} %bitcast.72), kind=kOutput, calls=%fused_computation.58 | convolution fusion | flops 2954887168 | bytes 17170432 | tf_op jit(solution)/shard_map/dot_general | solution.py:18
  532.7 10.0 %collective-permute-done.45 = bf16[256,2816]{1,0:T(8,128)(2,1)} collective-permute-done((bf16[256,2816]{1,0:T(8,128)(2,1)}, bf16[256,2816]{1,0:T(8,128)(2,1)}, u32[]{:S(2)}, u32[]{:S(2)}) %collective-permute-start.45) | collective-permute-done | bytes 1441824 | tf_op jit(solution)/shard_map/ppermute | solution.py:427
  554.7 4.5 shard_map.219
  559.2 18.0 %collective-permute-done.49 = bf16[256,2816]{1,0:T(8,128)(2,1)} collective-permute-done((bf16[256,2816]{1,0:T(8,128)(2,1)}, bf16[256,2816]{1,0:T(8,128)(2,1)}, u32[]{:S(2)}, u32[]{:S(2)}) %collective-permute-start.49) | collective-permute-done | bytes 1441824 | tf_op jit(solution)/shard_map/ppermute | solution.py:427
  577.2 6.5 fusion.96.grad
  583.7 4.4 fusion
  591.3 4.6 convolution_convert_fusion.9
  595.9 19.6 %shard_map.220 = (bf16[1024,2176]{1,0:T(8,128)(2,1)}, f32[1,128]{1,0:T(1,128)}) custom-call(f32[1024,2176]{1,0:T(8,128)} %shard_map.216.q.k.v.gate.logit, f32[1024,2176]{1,0:T(8,128)} %shard_map.216.q.k.v.gate.logit, f32[1024,2176]{1,0:T(8,128)} %shard_map.216.q.k.v.gate.logit, f32[1024,2176]{1,0:T(8,128)} %shard_map.216.q.k.v.gate.logit, ...), custom_call_target="tpu_custom_call" | custom-call | tf_op jit(solution)/shard_map/pallas_call | solution.py:388
  619.8 4.9 collective-permute-done.52
  625.3 4.9 convolution_convert_fusion.8
  632.8 10.6 %convolution_convert_fusion.13 = bf16[512,2048]{1,0:T(8,128)(2,1)} fusion(bf16[2048,2176]{1,0:T(8,128)(2,1)} %copy-done.60, bf16[256,2176]{1,0:T(8,128)(2,1)S(1)} %get-tuple-element.463, bf16[256,2176]{1,0:T(8,128)(2,1)S(1)} %get-tuple-element.461), kind=kOutput, calls=%fused_computation.26 | convolution fusion | flops 4568907776 | bytes 13238272 | tf_op jit(solution)/shard_map/dot_general | solution.py:18
  649.0 10.2 %collective-permute-done.55 = bf16[256,2816]{1,0:T(8,128)(2,1)S(1)} collective-permute-done((bf16[256,2816]{1,0:T(8,128)(2,1)S(1)}, bf16[256,2816]{1,0:T(8,128)(2,1)S(1)}, u32[]{:S(2)}, u32[]{:S(2)}) %collective-permute-start.55) | collective-permute-done | bytes 1441824 | tf_op jit(solution)/shard_map/ppermute | solution.py:427
  659.1 4.9 add_convert_fusion.1
  667.0 13.1 %collective-permute-done.54 = bf16[256,2176]{1,0:T(8,128)(2,1)} collective-permute-done((bf16[256,2176]{1,0:T(8,128)(2,1)}, bf16[256,2176]{1,0:T(8,128)(2,1)}, u32[]{:S(2)}, u32[]{:S(2)}) %collective-permute-start.54) | collective-permute-done | bytes 1114144 | tf_op jit(solution)/shard_map/ppermute | solution.py:427
  680.7 10.4 %add_convert_fusion.5 = bf16[256,2048]{1,0:T(8,128)(2,1)} fusion(bf16[512,2048]{1,0:T(8,128)(2,1)} %collective-permute-done.53, bf16[256,2176]{1,0:T(8,128)(2,1)S(1)} %copy-done.40, bf16[2048,2176]{1,0:T(8,128)(2,1)} %copy-done.60), kind=kOutput, calls=%fused_computation.55 | convolution fusion | flops 2283274240 | bytes 12124160 | tf_op jit(solution)/shard_map/dot_general | solution.py:18
  694.9 27.9 %collective-permute-done.62 = bf16[256,2816]{1,0:T(8,128)(2,1)S(1)} collective-permute-done((bf16[256,2816]{1,0:T(8,128)(2,1)S(1)}, bf16[256,2816]{1,0:T(8,128)(2,1)S(1)}, u32[]{:S(2)}, u32[]{:S(2)}) %collective-permute-start.62) | collective-permute-done | bytes 1441824 | tf_op jit(solution)/shard_map/ppermute | solution.py:424
  729.6 7.2 convert_add_fusion
  743.2 8.5 collective-permute-done.63
  759.2 4.1 add_convert_fusion.2
  768.2 4.4 collective-permute-done.67
  773.2 33.2 %collective-permute-done.68 = bf16[256,2176]{1,0:T(8,128)(2,1)S(1)} collective-permute-done((bf16[256,2176]{1,0:T(8,128)(2,1)S(1)}, bf16[256,2176]{1,0:T(8,128)(2,1)S(1)}, u32[]{:S(2)}, u32[]{:S(2)}) %collective-permute-start.68) | collective-permute-done | bytes 1114144 | tf_op jit(solution)/shard_map/ppermute | solution.py:424
  810.2 4.6 shard_map.221
  822.6 8.6 collective-permute-done.74
  831.4 8.1 collective-permute-done.77.refs_2_
  843.8 12.2 %collective-permute-done.83.refs_3_ = bf16[256,1152]{1,0:T(8,128)(2,1)} collective-permute-done((bf16[256,1152]{1,0:T(8,128)(2,1)}, bf16[256,1152]{1,0:T(8,128)(2,1)}, u32[]{:S(2)}, u32[]{:S(2)}) %collective-permute-start.83) | collective-permute-done | bytes 589856 | tf_op jit(solution)/shard_map/ppermute | solution.py:442
  857.1 11.2 %shard_map.222 = f32[256,11008]{1,0:T(8,128)} custom-call(bf16[256,2816]{1,0:T(8,128)(2,1)} %copy-done.21, bf16[256,2816]{1,0:T(8,128)(2,1)} %collective-permute-done.76.refs_1_, bf16[256,2816]{1,0:T(8,128)(2,1)} %collective-permute-done.77.refs_2_, bf16[256,2816]{1,0:T(8,128)(2,1)} %collective-permute-done.78.refs_3_), custom_call_target="tpu_custom_call" | custom-call | tf_op jit(solution)/shard_map/pallas_call | solution.py:547
  874.3 6.2 shard_map.223.refs_0_
  883.0 6.3 shard_map.224
  (455 shorter events, 223.6 us)
Async XLA Ops:
  6.3 29.9 %collective-permute-start.2 = (bf16[256,2176]{1,0:T(8,128)(2,1)}, bf16[256,2176]{1,0:T(8,128)(2,1)}, u32[]{:S(2)}, u32[]{:S(2)}) collective-permute-start(bf16[256,2176]{1,0:T(8,128)(2,1)} %shard_map.212.refs_4_), channel_id=1, source_target_pairs={{0,8},{4,12},{8,16},{12,20},{16,24},{20,28},{24,0},{28,4},{1,9},{5... | collective-permute-start | bytes 3342344 | tf_op jit(solution)/shard_map/ppermute | solution.py:424
  9.3 26.9 %collective-permute-start.1 = (bf16[256,2176]{1,0:T(8,128)(2,1)}, bf16[256,2176]{1,0:T(8,128)(2,1)S(1)}, u32[]{:S(2)}, u32[]{:S(2)}) collective-permute-start(bf16[256,2176]{1,0:T(8,128)(2,1)} %shard_map.212.refs_4_), channel_id=1, source_target_pairs={{0,4},{4,0},{8,12},{12,8},{16,20},{20,16},{24,28},{28,24},{1,5},{5... | collective-permute-start | bytes 3342344 | tf_op jit(solution)/shard_map/ppermute | solution.py:427
  16.3 20.0 %collective-permute-start = (bf16[256,2176]{1,0:T(8,128)(2,1)S(1)}, bf16[256,2176]{1,0:T(8,128)(2,1)S(1)}, u32[]{:S(2)}, u32[]{:S(2)}) collective-permute-start(bf16[256,2176]{1,0:T(8,128)(2,1)S(1)} %constant_dynamic-update-slice_fusion.refs_0_), channel_id=1, source_target_pairs={{0,1},{1,0},{2,3},{3,2},{4,5},{5,4},{6,7},{7,6},{8,9},{9,8},{10,11... | collective-permute-start | bytes 3342344 | tf_op jit(solution)/shard_map/ppermute | solution.py:439
  16.3 27.1 %collective-permute-start.3 = (bf16[256,2176]{1,0:T(8,128)(2,1)S(1)}, bf16[256,2176]{1,0:T(8,128)(2,1)}, u32[]{:S(2)}, u32[]{:S(2)}) collective-permute-start(bf16[256,2176]{1,0:T(8,128)(2,1)S(1)} %constant_dynamic-update-slice_fusion.refs_0_), channel_id=1, source_target_pairs={{0,2},{1,3},{2,0},{3,1},{4,6},{5,7},{6,4},{7,5},{8,10},{9,11},{10,... | collective-permute-start | bytes 3342344 | tf_op jit(solution)/shard_map/ppermute | solution.py:442
  43.4 29.1 %collective-permute-start.5 = (bf16[256,2176]{1,0:T(8,128)(2,1)}, bf16[256,2176]{1,0:T(8,128)(2,1)}, u32[]{:S(2)}, u32[]{:S(2)}) collective-permute-start(bf16[256,2176]{1,0:T(8,128)(2,1)} %collective-permute-done.2.refs_2_), channel_id=1, source_target_pairs={{0,8},{4,12},{8,16},{12,20},{16,24},{20,28},{24,0},{28,4},{1,9},{5... | collective-permute-start | bytes 3342344 | tf_op jit(solution)/shard_map/ppermute | solution.py:424
  48.2 35.4 %collective-permute-start.8 = (bf16[256,2176]{1,0:T(8,128)(2,1)}, bf16[256,2176]{1,0:T(8,128)(2,1)}, u32[]{:S(2)}, u32[]{:S(2)}) collective-permute-start(bf16[256,2176]{1,0:T(8,128)(2,1)} %collective-permute-done.2.refs_2_), channel_id=1, source_target_pairs={{0,4},{4,0},{8,12},{12,8},{16,20},{20,16},{24,28},{28,24},{1,5},{5... | collective-permute-start | bytes 3342344 | tf_op jit(solution)/shard_map/ppermute | solution.py:427
  72.5 29.6 %collective-permute-start.7 = (bf16[256,2176]{1,0:T(8,128)(2,1)}, bf16[256,2176]{1,0:T(8,128)(2,1)}, u32[]{:S(2)}, u32[]{:S(2)}) collective-permute-start(bf16[256,2176]{1,0:T(8,128)(2,1)} %collective-permute-done.5.refs_1_), channel_id=1, source_target_pairs={{0,8},{4,12},{8,16},{12,20},{16,24},{20,28},{24,0},{28,4},{1,9},{5... | collective-permute-start | bytes 3342344 | tf_op jit(solution)/shard_map/ppermute | solution.py:424
  72.5 35.0 %collective-permute-start.9 = (bf16[256,2176]{1,0:T(8,128)(2,1)}, bf16[256,2176]{1,0:T(8,128)(2,1)}, u32[]{:S(2)}, u32[]{:S(2)}) collective-permute-start(bf16[256,2176]{1,0:T(8,128)(2,1)} %collective-permute-done.5.refs_1_), channel_id=1, source_target_pairs={{0,4},{4,0},{8,12},{12,8},{16,20},{20,16},{24,28},{28,24},{1,5},{5... | collective-permute-start | bytes 3342344 | tf_op jit(solution)/shard_map/ppermute | solution.py:427
  73.0 38.9 %collective-permute-start.11 = (bf16[128,2048]{1,0:T(8,128)(2,1)S(1)}, bf16[128,2048]{1,0:T(8,128)(2,1)S(1)}, u32[]{:S(2)}, u32[]{:S(2)}) collective-permute-start(bf16[128,2048]{1,0:T(8,128)(2,1)S(1)} %broadcast_select_fusion.2), channel_id=1, source_target_pairs={{0,8},{4,12},{8,16},{12,20},{16,24},{20,28},{24,0},{28,4},{1,9},{5... | collective-permute-start | bytes 1572872 | tf_op jit(solution)/shard_map/ppermute | solution.py:424
  102.1 28.6 %collective-permute-start.10 = (bf16[256,2176]{1,0:T(8,128)(2,1)}, bf16[256,2176]{1,0:T(8,128)(2,1)}, u32[]{:S(2)}, u32[]{:S(2)}) collective-permute-start(bf16[256,2176]{1,0:T(8,128)(2,1)} %collective-permute-done.7.refs_3_), channel_id=1, source_target_pairs={{0,4},{4,0},{8,12},{12,8},{16,20},{20,16},{24,28},{28,24},{1,5},{5... | collective-permute-start | bytes 3342344 | tf_op jit(solution)/shard_map/ppermute | solution.py:427
  126.5 36.7 %collective-permute-start.13 = (bf16[128,2048]{1,0:T(8,128)(2,1)}, bf16[128,2048]{1,0:T(8,128)(2,1)S(1)}, u32[]{:S(2)}, u32[]{:S(2)}) collective-permute-start(bf16[128,2048]{1,0:T(8,128)(2,1)} %collective-permute-done.12), channel_id=1, source_target_pairs={{0,8},{4,12},{8,16},{12,20},{16,24},{20,28},{24,0},{28,4},{1,9},{5... | collective-permute-start | bytes 1572872 | tf_op jit(solution)/shard_map/ppermute | solution.py:424
  128.3 42.9 %collective-permute-start.15 = (bf16[256,2816]{1,0:T(8,128)(2,1)S(1)}, bf16[256,2816]{1,0:T(8,128)(2,1)S(1)}, u32[]{:S(2)}, u32[]{:S(2)}) collective-permute-start(bf16[256,2816]{1,0:T(8,128)(2,1)S(1)} %copy-done.5), channel_id=1, source_target_pairs={{0,8},{4,12},{8,16},{12,20},{16,24},{20,28},{24,0},{28,4},{1,9},{5... | collective-permute-start | bytes 4325384 | tf_op jit(solution)/shard_map/ppermute | solution.py:424
  130.7 40.5 %collective-permute-start.14 = (bf16[256,2816]{1,0:T(8,128)(2,1)S(1)}, bf16[256,2816]{1,0:T(8,128)(2,1)S(1)}, u32[]{:S(2)}, u32[]{:S(2)}) collective-permute-start(bf16[256,2816]{1,0:T(8,128)(2,1)S(1)} %copy-done.5), channel_id=1, source_target_pairs={{0,4},{4,0},{8,12},{12,8},{16,20},{20,16},{24,28},{28,24},{1,5},{5... | collective-permute-start | bytes 4325384 | tf_op jit(solution)/shard_map/ppermute | solution.py:427
  172.3 35.9 %collective-permute-start.19 = (bf16[256,2816]{1,0:T(8,128)(2,1)S(1)}, bf16[256,2816]{1,0:T(8,128)(2,1)}, u32[]{:S(2)}, u32[]{:S(2)}) collective-permute-start(bf16[256,2816]{1,0:T(8,128)(2,1)S(1)} %collective-permute-done.15.refs_2_.refs_10_), channel_id=1, source_target_pairs={{0,8},{4,12},{8,16},{12,20},{16,24},{20,28},{24,0},{28,4},{1,9},{5... | collective-permute-start | bytes 4325384 | tf_op jit(solution)/shard_map/ppermute | solution.py:424
  172.3 37.0 %collective-permute-start.18 = (bf16[256,2816]{1,0:T(8,128)(2,1)S(1)}, bf16[256,2816]{1,0:T(8,128)(2,1)S(1)}, u32[]{:S(2)}, u32[]{:S(2)}) collective-permute-start(bf16[256,2816]{1,0:T(8,128)(2,1)S(1)} %collective-permute-done.15.refs_2_.refs_10_), channel_id=1, source_target_pairs={{0,4},{4,0},{8,12},{12,8},{16,20},{20,16},{24,28},{28,24},{1,5},{5... | collective-permute-start | bytes 4325384 | tf_op jit(solution)/shard_map/ppermute | solution.py:427
  180.3 30.1 %collective-permute-start.17 = (bf16[256,2048]{1,0:T(8,128)(2,1)}, bf16[256,2048]{1,0:T(8,128)(2,1)}, u32[]{:S(2)}, u32[]{:S(2)}) collective-permute-start(bf16[256,2048]{1,0:T(8,128)(2,1)} %add_convert_fusion.8), channel_id=1, source_target_pairs={{0,2},{1,3},{2,0},{3,1},{4,6},{5,7},{6,4},{7,5},{8,10},{9,11},{10,... | collective-permute-start | bytes 3145736 | tf_op jit(solution)/shard_map/ppermute | solution.py:442
  208.2 35.7 %collective-permute-start.23 = (bf16[256,2816]{1,0:T(8,128)(2,1)}, bf16[256,2816]{1,0:T(8,128)(2,1)S(1)}, u32[]{:S(2)}, u32[]{:S(2)}) collective-permute-start(bf16[256,2816]{1,0:T(8,128)(2,1)} %collective-permute-done.19.refs_1_.refs_9_), channel_id=1, source_target_pairs={{0,8},{4,12},{8,16},{12,20},{16,24},{20,28},{24,0},{28,4},{1,9},{5... | collective-permute-start | bytes 4325384 | tf_op jit(solution)/shard_map/ppermute | solution.py:424
  208.7 35.2 %collective-permute-start.22 = (bf16[256,2816]{1,0:T(8,128)(2,1)}, bf16[256,2816]{1,0:T(8,128)(2,1)}, u32[]{:S(2)}, u32[]{:S(2)}) collective-permute-start(bf16[256,2816]{1,0:T(8,128)(2,1)} %collective-permute-done.19.refs_1_.refs_9_), channel_id=1, source_target_pairs={{0,4},{4,0},{8,12},{12,8},{16,20},{20,16},{24,28},{28,24},{1,5},{5... | collective-permute-start | bytes 4325384 | tf_op jit(solution)/shard_map/ppermute | solution.py:427
  215.3 28.6 %collective-permute-start.21 = (bf16[256,2048]{1,0:T(8,128)(2,1)S(1)}, bf16[256,2048]{1,0:T(8,128)(2,1)S(1)}, u32[]{:S(2)}, u32[]{:S(2)}) collective-permute-start(bf16[256,2048]{1,0:T(8,128)(2,1)S(1)} %constant_dynamic-update-slice_fusion.13), channel_id=1, source_target_pairs={{0,2},{1,3},{2,0},{3,1},{4,6},{5,7},{6,4},{7,5},{8,10},{9,11},{10,... | collective-permute-start | bytes 3145736 | tf_op jit(solution)/shard_map/ppermute | solution.py:442
  216.9 27.8 %collective-permute-start.20 = (bf16[256,2048]{1,0:T(8,128)(2,1)S(1)}, bf16[256,2048]{1,0:T(8,128)(2,1)S(1)}, u32[]{:S(2)}, u32[]{:S(2)}) collective-permute-start(bf16[256,2048]{1,0:T(8,128)(2,1)S(1)} %constant_dynamic-update-slice_fusion.13), channel_id=1, source_target_pairs={{0,1},{1,0},{2,3},{3,2},{4,5},{5,4},{6,7},{7,6},{8,9},{9,8},{10,11... | collective-permute-start | bytes 3145736 | tf_op jit(solution)/shard_map/ppermute | solution.py:439
  244.0 20.4 %collective-permute-start.26 = (bf16[176,2048]{1,0:T(8,128)(2,1)S(1)}, bf16[176,2048]{1,0:T(8,128)(2,1)}, u32[]{:S(2)}, u32[]{:S(2)}) collective-permute-start(bf16[176,2048]{1,0:T(8,128)(2,1)S(1)} %copy-done.43), channel_id=1, source_target_pairs={{0,8},{4,12},{8,16},{12,20},{16,24},{20,28},{24,0},{28,4},{1,9},{5... | collective-permute-start | bytes 2162696 | tf_op jit(solution)/shard_map/ppermute | solution.py:424
  244.1 33.9 %collective-permute-start.25 = (bf16[256,2816]{1,0:T(8,128)(2,1)S(1)}, bf16[256,2816]{1,0:T(8,128)(2,1)S(1)}, u32[]{:S(2)}, u32[]{:S(2)}) collective-permute-start(bf16[256,2816]{1,0:T(8,128)(2,1)S(1)} %collective-permute-done.23.refs_3_.refs_11_), channel_id=1, source_target_pairs={{0,4},{4,0},{8,12},{12,8},{16,20},{20,16},{24,28},{28,24},{1,5},{5... | collective-permute-start | bytes 4325384 | tf_op jit(solution)/shard_map/ppermute | solution.py:427
  264.5 36.7 %collective-permute-start.27 = (bf16[176,2048]{1,0:T(8,128)(2,1)}, bf16[176,2048]{1,0:T(8,128)(2,1)}, u32[]{:S(2)}, u32[]{:S(2)}) collective-permute-start(bf16[176,2048]{1,0:T(8,128)(2,1)} %collective-permute-done.26), channel_id=1, source_target_pairs={{0,8},{4,12},{8,16},{12,20},{16,24},{20,28},{24,0},{28,4},{1,9},{5... | collective-permute-start | bytes 2162696 | tf_op jit(solution)/shard_map/ppermute | solution.py:424
  279.1 22.0 %collective-permute-start.30 = (bf16[176,2048]{1,0:T(8,128)(2,1)S(1)}, bf16[176,2048]{1,0:T(8,128)(2,1)}, u32[]{:S(2)}, u32[]{:S(2)}) collective-permute-start(bf16[176,2048]{1,0:T(8,128)(2,1)S(1)} %copy-done.43), channel_id=1, source_target_pairs={{0,4},{4,0},{8,12},{12,8},{16,20},{20,16},{24,28},{28,24},{1,5},{5... | collective-permute-start | bytes 2162696 | tf_op jit(solution)/shard_map/ppermute | solution.py:427
  279.7 32.7 %collective-permute-start.29 = (bf16[176,2048]{1,0:T(8,128)(2,1)}, bf16[176,2048]{1,0:T(8,128)(2,1)}, u32[]{:S(2)}, u32[]{:S(2)}) collective-permute-start(bf16[176,2048]{1,0:T(8,128)(2,1)} %collective-permute-done.26), channel_id=1, source_target_pairs={{0,4},{4,0},{8,12},{12,8},{16,20},{20,16},{24,28},{28,24},{1,5},{5... | collective-permute-start | bytes 2162696 | tf_op jit(solution)/shard_map/ppermute | solution.py:427
  312.4 18.8 %collective-permute-start.28 = (bf16[176,2048]{1,0:T(8,128)(2,1)}, bf16[176,2048]{1,0:T(8,128)(2,1)S(1)}, u32[]{:S(2)}, u32[]{:S(2)}) collective-permute-start(bf16[176,2048]{1,0:T(8,128)(2,1)} %collective-permute-done.27), channel_id=1, source_target_pairs={{0,8},{4,12},{8,16},{12,20},{16,24},{20,28},{24,0},{28,4},{1,9},{5... | collective-permute-start | bytes 2162696 | tf_op jit(solution)/shard_map/ppermute | solution.py:424
  312.4 19.3 %collective-permute-start.31 = (bf16[176,2048]{1,0:T(8,128)(2,1)}, bf16[176,2048]{1,0:T(8,128)(2,1)S(1)}, u32[]{:S(2)}, u32[]{:S(2)}) collective-permute-start(bf16[176,2048]{1,0:T(8,128)(2,1)} %collective-permute-done.27), channel_id=1, source_target_pairs={{0,4},{4,0},{8,12},{12,8},{16,20},{20,16},{24,28},{28,24},{1,5},{5... | collective-permute-start | bytes 2162696 | tf_op jit(solution)/shard_map/ppermute | solution.py:427
  360.3 25.3 %collective-permute-start.34 = (bf16[256,2048]{1,0:T(8,128)(2,1)S(1)}, bf16[256,2048]{1,0:T(8,128)(2,1)S(1)}, u32[]{:S(2)}, u32[]{:S(2)}) collective-permute-start(bf16[256,2048]{1,0:T(8,128)(2,1)S(1)} %add_convert_fusion.7), channel_id=1, source_target_pairs={{0,2},{1,3},{2,0},{3,1},{4,6},{5,7},{6,4},{7,5},{8,10},{9,11},{10,... | collective-permute-start | bytes 3145736 | tf_op jit(solution)/shard_map/ppermute | solution.py:442
  390.9 24.7 %collective-permute-start.36 = (bf16[256,2048]{1,0:T(8,128)(2,1)}, bf16[256,2048]{1,0:T(8,128)(2,1)}, u32[]{:S(2)}, u32[]{:S(2)}) collective-permute-start(bf16[256,2048]{1,0:T(8,128)(2,1)} %get-tuple-element.293), channel_id=1, source_target_pairs={{0,2},{1,3},{2,0},{3,1},{4,6},{5,7},{6,4},{7,5},{8,10},{9,11},{10,... | collective-permute-start | bytes 3145736 | tf_op jit(solution)/shard_map/ppermute | solution.py:442
  392.4 23.2 %collective-permute-start.35 = (bf16[256,2048]{1,0:T(8,128)(2,1)}, bf16[256,2048]{1,0:T(8,128)(2,1)}, u32[]{:S(2)}, u32[]{:S(2)}) collective-permute-start(bf16[256,2048]{1,0:T(8,128)(2,1)} %get-tuple-element.293), channel_id=1, source_target_pairs={{0,1},{1,0},{2,3},{3,2},{4,5},{5,4},{6,7},{7,6},{8,9},{9,8},{10,11... | collective-permute-start | bytes 3145736 | tf_op jit(solution)/shard_map/ppermute | solution.py:439
  458.1 19.5 %collective-permute-start.39 = (bf16[512,2048]{1,0:T(8,128)(2,1)S(1)}, bf16[512,2048]{1,0:T(8,128)(2,1)S(1)}, u32[]{:S(2)}, u32[]{:S(2)}) collective-permute-start(bf16[512,2048]{1,0:T(8,128)(2,1)S(1)} %convolution_convert_fusion.10), channel_id=1, source_target_pairs={{0,1},{1,0},{2,3},{3,2},{4,5},{5,4},{6,7},{7,6},{8,9},{9,8},{10,11... | collective-permute-start | bytes 6291464 | tf_op jit(solution)/shard_map/ppermute | solution.py:439
  476.7 33.5 %collective-permute-start.42 = (bf16[352,2048]{1,0:T(8,128)(2,1)}, bf16[352,2048]{1,0:T(8,128)(2,1)}, u32[]{:S(2)}, u32[]{:S(2)}) collective-permute-start(bf16[352,2048]{1,0:T(8,128)(2,1)} %pad_maximum_fusion.4), channel_id=1, source_target_pairs={{0,4},{4,0},{8,12},{12,8},{16,20},{20,16},{24,28},{28,24},{1,5},{5... | collective-permute-start | bytes 4325384 | tf_op jit(solution)/shard_map/ppermute | solution.py:427
  486.8 24.8 %collective-permute-start.41 = (bf16[256,2048]{1,0:T(8,128)(2,1)}, bf16[256,2048]{1,0:T(8,128)(2,1)}, u32[]{:S(2)}, u32[]{:S(2)}) collective-permute-start(bf16[256,2048]{1,0:T(8,128)(2,1)} %add_convert_fusion.6), channel_id=1, source_target_pairs={{0,2},{1,3},{2,0},{3,1},{4,6},{5,7},{6,4},{7,5},{8,10},{9,11},{10,... | collective-permute-start | bytes 3145736 | tf_op jit(solution)/shard_map/ppermute | solution.py:442
  491.7 38.2 %collective-permute-start.46 = (bf16[176,2048]{1,0:T(8,128)(2,1)}, bf16[176,2048]{1,0:T(8,128)(2,1)}, u32[]{:S(2)}, u32[]{:S(2)}) collective-permute-start(bf16[176,2048]{1,0:T(8,128)(2,1)} %get-tuple-element.312), channel_id=1, source_target_pairs={{0,8},{4,12},{8,16},{12,20},{16,24},{20,28},{24,0},{28,4},{1,9},{5... | collective-permute-start | bytes 2162696 | tf_op jit(solution)/shard_map/ppermute | solution.py:424
  491.7 38.2 %collective-permute-start.47 = (bf16[176,2048]{1,0:T(8,128)(2,1)}, bf16[176,2048]{1,0:T(8,128)(2,1)}, u32[]{:S(2)}, u32[]{:S(2)}) collective-permute-start(bf16[176,2048]{1,0:T(8,128)(2,1)} %get-tuple-element.313), channel_id=1, source_target_pairs={{0,24},{4,28},{8,0},{12,4},{16,8},{20,12},{24,16},{28,20},{1,25},{... | collective-permute-start | bytes 2162696 | tf_op jit(solution)/shard_map/ppermute | solution.py:424
  510.2 32.6 %collective-permute-start.45 = (bf16[256,2816]{1,0:T(8,128)(2,1)}, bf16[256,2816]{1,0:T(8,128)(2,1)}, u32[]{:S(2)}, u32[]{:S(2)}) collective-permute-start(bf16[256,2816]{1,0:T(8,128)(2,1)} %convolution_convert_fusion.4), channel_id=1, source_target_pairs={{0,4},{4,0},{8,12},{12,8},{16,20},{20,16},{24,28},{28,24},{1,5},{5... | collective-permute-start | bytes 4325384 | tf_op jit(solution)/shard_map/ppermute | solution.py:427
  528.4 23.5 %collective-permute-start.44 = (bf16[256,2048]{1,0:T(8,128)(2,1)S(1)}, bf16[256,2048]{1,0:T(8,128)(2,1)S(1)}, u32[]{:S(2)}, u32[]{:S(2)}) collective-permute-start(bf16[256,2048]{1,0:T(8,128)(2,1)S(1)} %get-tuple-element.320.refs_0_), channel_id=1, source_target_pairs={{0,2},{1,3},{2,0},{3,1},{4,6},{5,7},{6,4},{7,5},{8,10},{9,11},{10,... | collective-permute-start | bytes 3145736 | tf_op jit(solution)/shard_map/ppermute | solution.py:442
  529.9 22.2 %collective-permute-start.43 = (bf16[256,2048]{1,0:T(8,128)(2,1)S(1)}, bf16[256,2048]{1,0:T(8,128)(2,1)S(1)}, u32[]{:S(2)}, u32[]{:S(2)}) collective-permute-start(bf16[256,2048]{1,0:T(8,128)(2,1)S(1)} %get-tuple-element.320.refs_0_), channel_id=1, source_target_pairs={{0,1},{1,0},{2,3},{3,2},{4,5},{5,4},{6,7},{7,6},{8,9},{9,8},{10,11... | collective-permute-start | bytes 3145736 | tf_op jit(solution)/shard_map/ppermute | solution.py:439
  545.5 31.6 %collective-permute-start.49 = (bf16[256,2816]{1,0:T(8,128)(2,1)}, bf16[256,2816]{1,0:T(8,128)(2,1)}, u32[]{:S(2)}, u32[]{:S(2)}) collective-permute-start(bf16[256,2816]{1,0:T(8,128)(2,1)} %convolution_convert_fusion.3), channel_id=1, source_target_pairs={{0,4},{4,0},{8,12},{12,8},{16,20},{20,16},{24,28},{28,24},{1,5},{5... | collective-permute-start | bytes 4325384 | tf_op jit(solution)/shard_map/ppermute | solution.py:427
  551.9 31.8 %collective-permute-start.50 = (bf16[176,2048]{1,0:T(8,128)(2,1)}, bf16[176,2048]{1,0:T(8,128)(2,1)}, u32[]{:S(2)}, u32[]{:S(2)}) collective-permute-start(bf16[176,2048]{1,0:T(8,128)(2,1)} %add_convert_fusion.10), channel_id=1, source_target_pairs={{0,8},{4,12},{8,16},{12,20},{16,24},{20,28},{24,0},{28,4},{1,9},{5... | collective-permute-start | bytes 2162696 | tf_op jit(solution)/shard_map/ppermute | solution.py:424
  588.1 36.5 %collective-permute-start.52 = (bf16[256,2816]{1,0:T(8,128)(2,1)}, bf16[256,2816]{1,0:T(8,128)(2,1)}, u32[]{:S(2)}, u32[]{:S(2)}) collective-permute-start(bf16[256,2816]{1,0:T(8,128)(2,1)} %fusion), channel_id=1, source_target_pairs={{0,8},{4,12},{8,16},{12,20},{16,24},{20,28},{24,0},{28,4},{1,9},{5... | collective-permute-start | bytes 4325384 | tf_op jit(solution)/shard_map/ppermute | solution.py:424
  588.1 36.5 %collective-permute-start.51 = (bf16[256,2816]{1,0:T(8,128)(2,1)}, bf16[256,2816]{1,0:T(8,128)(2,1)}, u32[]{:S(2)}, u32[]{:S(2)}) collective-permute-start(bf16[256,2816]{1,0:T(8,128)(2,1)} %convolution_convert_fusion.2), channel_id=1, source_target_pairs={{0,4},{4,0},{8,12},{12,8},{16,20},{20,16},{24,28},{28,24},{1,5},{5... | collective-permute-start | bytes 4325384 | tf_op jit(solution)/shard_map/ppermute | solution.py:427
  615.6 31.1 %collective-permute-start.56 = (bf16[128,2048]{1,0:T(8,128)(2,1)S(1)}, bf16[128,2048]{1,0:T(8,128)(2,1)S(1)}, u32[]{:S(2)}, u32[]{:S(2)}) collective-permute-start(bf16[128,2048]{1,0:T(8,128)(2,1)S(1)} %get-tuple-element.466), channel_id=1, source_target_pairs={{0,8},{4,12},{8,16},{12,20},{16,24},{20,28},{24,0},{28,4},{1,9},{5... | collective-permute-start | bytes 1572872 | tf_op jit(solution)/shard_map/ppermute | solution.py:424
  617.4 29.5 %collective-permute-start.57 = (bf16[128,2048]{1,0:T(8,128)(2,1)S(1)}, bf16[128,2048]{1,0:T(8,128)(2,1)S(1)}, u32[]{:S(2)}, u32[]{:S(2)}) collective-permute-start(bf16[128,2048]{1,0:T(8,128)(2,1)S(1)} %get-tuple-element.465), channel_id=1, source_target_pairs={{0,24},{4,28},{8,0},{12,4},{16,8},{20,12},{24,16},{28,20},{1,25},{... | collective-permute-start | bytes 1572872 | tf_op jit(solution)/shard_map/ppermute | solution.py:424
  624.6 34.5 %collective-permute-start.55 = (bf16[256,2816]{1,0:T(8,128)(2,1)S(1)}, bf16[256,2816]{1,0:T(8,128)(2,1)S(1)}, u32[]{:S(2)}, u32[]{:S(2)}) collective-permute-start(bf16[256,2816]{1,0:T(8,128)(2,1)S(1)} %convolution_convert_fusion.1), channel_id=1, source_target_pairs={{0,4},{4,0},{8,12},{12,8},{16,20},{20,16},{24,28},{28,24},{1,5},{5... | collective-permute-start | bytes 4325384 | tf_op jit(solution)/shard_map/ppermute | solution.py:427
  630.2 49.8 %collective-permute-start.54 = (bf16[256,2176]{1,0:T(8,128)(2,1)}, bf16[256,2176]{1,0:T(8,128)(2,1)}, u32[]{:S(2)}, u32[]{:S(2)}) collective-permute-start(bf16[256,2176]{1,0:T(8,128)(2,1)} %convolution_convert_fusion.8), channel_id=1, source_target_pairs={{0,4},{4,0},{8,12},{12,8},{16,20},{20,16},{24,28},{28,24},{1,5},{5... | collective-permute-start | bytes 3342344 | tf_op jit(solution)/shard_map/ppermute | solution.py:427
  643.4 37.4 %collective-permute-start.53 = (bf16[512,2048]{1,0:T(8,128)(2,1)}, bf16[512,2048]{1,0:T(8,128)(2,1)}, u32[]{:S(2)}, u32[]{:S(2)}) collective-permute-start(bf16[512,2048]{1,0:T(8,128)(2,1)} %convolution_convert_fusion.13), channel_id=1, source_target_pairs={{0,1},{1,0},{2,3},{3,2},{4,5},{5,4},{6,7},{7,6},{8,9},{9,8},{10,11... | collective-permute-start | bytes 6291464 | tf_op jit(solution)/shard_map/ppermute | solution.py:439
  646.7 76.2 %collective-permute-start.62 = (bf16[256,2816]{1,0:T(8,128)(2,1)S(1)}, bf16[256,2816]{1,0:T(8,128)(2,1)S(1)}, u32[]{:S(2)}, u32[]{:S(2)}) collective-permute-start(bf16[256,2816]{1,0:T(8,128)(2,1)S(1)} %fusion.1), channel_id=1, source_target_pairs={{0,24},{4,28},{8,0},{12,4},{16,8},{20,12},{24,16},{28,20},{1,25},{... | collective-permute-start | bytes 4325384 | tf_op jit(solution)/shard_map/ppermute | solution.py:424
  646.9 75.9 %collective-permute-start.61 = (bf16[128,2048]{1,0:T(8,128)(2,1)S(1)}, bf16[128,2048]{1,0:T(8,128)(2,1)S(1)}, u32[]{:S(2)}, u32[]{:S(2)}) collective-permute-start(bf16[128,2048]{1,0:T(8,128)(2,1)S(1)} %add_convert_fusion.17), channel_id=1, source_target_pairs={{0,8},{4,12},{8,16},{12,20},{16,24},{20,28},{24,0},{28,4},{1,9},{5... | collective-permute-start | bytes 1572872 | tf_op jit(solution)/shard_map/ppermute | solution.py:424
  664.1 65.5 %collective-permute-start.59 = (bf16[256,2816]{1,0:T(8,128)(2,1)}, bf16[256,2816]{1,0:T(8,128)(2,1)S(1)}, u32[]{:S(2)}, u32[]{:S(2)}) collective-permute-start(bf16[256,2816]{1,0:T(8,128)(2,1)} %add_convert_fusion.1), channel_id=1, source_target_pairs={{0,8},{4,12},{8,16},{12,20},{16,24},{20,28},{24,0},{28,4},{1,9},{5... | collective-permute-start | bytes 4325384 | tf_op jit(solution)/shard_map/ppermute | solution.py:424
  680.0 45.9 %collective-permute-start.60 = (bf16[256,2176]{1,0:T(8,128)(2,1)}, bf16[256,2176]{1,0:T(8,128)(2,1)S(1)}, u32[]{:S(2)}, u32[]{:S(2)}) collective-permute-start(bf16[256,2176]{1,0:T(8,128)(2,1)} %convolution_convert_fusion.7), channel_id=1, source_target_pairs={{0,4},{4,0},{8,12},{12,8},{16,20},{20,16},{24,28},{28,24},{1,5},{5... | collective-permute-start | bytes 3342344 | tf_op jit(solution)/shard_map/ppermute | solution.py:427
  691.2 38.4 %collective-permute-start.58 = (bf16[256,2048]{1,0:T(8,128)(2,1)}, bf16[256,2048]{1,0:T(8,128)(2,1)}, u32[]{:S(2)}, u32[]{:S(2)}) collective-permute-start(bf16[256,2048]{1,0:T(8,128)(2,1)} %add_convert_fusion.5), channel_id=1, source_target_pairs={{0,2},{1,3},{2,0},{3,1},{4,6},{5,7},{6,4},{7,5},{8,10},{9,11},{10,... | collective-permute-start | bytes 3145736 | tf_op jit(solution)/shard_map/ppermute | solution.py:442
  725.3 26.5 %collective-permute-start.63 = (bf16[256,2176]{1,0:T(8,128)(2,1)}, bf16[256,2176]{1,0:T(8,128)(2,1)}, u32[]{:S(2)}, u32[]{:S(2)}) collective-permute-start(bf16[256,2176]{1,0:T(8,128)(2,1)} %convolution_convert_fusion.6), channel_id=1, source_target_pairs={{0,4},{4,0},{8,12},{12,8},{16,20},{20,16},{24,28},{28,24},{1,5},{5... | collective-permute-start | bytes 3342344 | tf_op jit(solution)/shard_map/ppermute | solution.py:427
  729.6 29.6 %collective-permute-start.66 = (bf16[256,2176]{1,0:T(8,128)(2,1)}, bf16[256,2176]{1,0:T(8,128)(2,1)}, u32[]{:S(2)}, u32[]{:S(2)}) collective-permute-start(bf16[256,2176]{1,0:T(8,128)(2,1)} %add_convert_fusion.4), channel_id=1, source_target_pairs={{0,8},{4,12},{8,16},{12,20},{16,24},{20,28},{24,0},{28,4},{1,9},{5... | collective-permute-start | bytes 3342344 | tf_op jit(solution)/shard_map/ppermute | solution.py:424
  753.3 61.5 %collective-permute-start.64 = (bf16[256,2176]{1,0:T(8,128)(2,1)}, bf16[256,2176]{1,0:T(8,128)(2,1)}, u32[]{:S(2)}, u32[]{:S(2)}) collective-permute-start(bf16[256,2176]{1,0:T(8,128)(2,1)} %convolution_convert_fusion.5), channel_id=1, source_target_pairs={{0,4},{4,0},{8,12},{12,8},{16,20},{20,16},{24,28},{28,24},{1,5},{5... | collective-permute-start | bytes 3342344 | tf_op jit(solution)/shard_map/ppermute | solution.py:427
  755.5 50.9 %collective-permute-start.68 = (bf16[256,2176]{1,0:T(8,128)(2,1)S(1)}, bf16[256,2176]{1,0:T(8,128)(2,1)S(1)}, u32[]{:S(2)}, u32[]{:S(2)}) collective-permute-start(bf16[256,2176]{1,0:T(8,128)(2,1)S(1)} %add_convert_fusion.3), channel_id=1, source_target_pairs={{0,24},{4,28},{8,0},{12,4},{16,8},{20,12},{24,16},{28,20},{1,25},{... | collective-permute-start | bytes 3342344 | tf_op jit(solution)/shard_map/ppermute | solution.py:424
  763.3 53.0 %collective-permute-start.72 = (bf16[256,2176]{1,0:T(8,128)(2,1)}, bf16[256,2176]{1,0:T(8,128)(2,1)}, u32[]{:S(2)}, u32[]{:S(2)}) collective-permute-start(bf16[256,2176]{1,0:T(8,128)(2,1)} %add_convert_fusion.2), channel_id=1, source_target_pairs={{0,8},{4,12},{8,16},{12,20},{16,24},{20,28},{24,0},{28,4},{1,9},{5... | collective-permute-start | bytes 3342344 | tf_op jit(solution)/shard_map/ppermute | solution.py:424
  772.6 36.6 %collective-permute-start.69 = (bf16[176,2048]{1,0:T(8,128)(2,1)S(1)}, bf16[176,2048]{1,0:T(8,128)(2,1)S(1)}, u32[]{:S(2)}, u32[]{:S(2)}) collective-permute-start(bf16[176,2048]{1,0:T(8,128)(2,1)S(1)} %add_convert_fusion.9.refs_0_), channel_id=1, source_target_pairs={{0,1},{1,0},{2,3},{3,2},{4,5},{5,4},{6,7},{7,6},{8,9},{9,8},{10,11... | collective-permute-start | bytes 2162696 | tf_op jit(solution)/shard_map/ppermute | solution.py:439
  772.7 37.5 %collective-permute-start.71 = (bf16[176,2048]{1,0:T(8,128)(2,1)S(1)}, bf16[176,2048]{1,0:T(8,128)(2,1)}, u32[]{:S(2)}, u32[]{:S(2)}) collective-permute-start(bf16[176,2048]{1,0:T(8,128)(2,1)S(1)} %collective-permute-done.70.refs_2_), channel_id=1, source_target_pairs={{0,1},{1,0},{2,3},{3,2},{4,5},{5,4},{6,7},{7,6},{8,9},{9,8},{10,11... | collective-permute-start | bytes 2162696 | tf_op jit(solution)/shard_map/ppermute | solution.py:439
  806.4 33.1 %collective-permute-start.77 = (bf16[256,2816]{1,0:T(8,128)(2,1)S(1)}, bf16[256,2816]{1,0:T(8,128)(2,1)}, u32[]{:S(2)}, u32[]{:S(2)}) collective-permute-start(bf16[256,2816]{1,0:T(8,128)(2,1)S(1)} %add_convert_fusion.refs_0_), channel_id=1, source_target_pairs={{0,2},{1,3},{2,0},{3,1},{4,6},{5,7},{6,4},{7,5},{8,10},{9,11},{10,... | collective-permute-start | bytes 4325384 | tf_op jit(solution)/shard_map/ppermute | solution.py:442
  810.2 45.9 %collective-permute-start.76 = (bf16[256,2816]{1,0:T(8,128)(2,1)S(1)}, bf16[256,2816]{1,0:T(8,128)(2,1)}, u32[]{:S(2)}, u32[]{:S(2)}) collective-permute-start(bf16[256,2816]{1,0:T(8,128)(2,1)S(1)} %add_convert_fusion.refs_0_), channel_id=1, source_target_pairs={{0,1},{1,0},{2,3},{3,2},{4,5},{5,4},{6,7},{7,6},{8,9},{9,8},{10,11... | collective-permute-start | bytes 4325384 | tf_op jit(solution)/shard_map/ppermute | solution.py:439
  841.1 27.2 %collective-permute-start.80 = (bf16[256,1024]{1,0:T(8,128)(2,1)}, bf16[256,1024]{1,0:T(8,128)(2,1)}, u32[]{:S(2)}, u32[]{:S(2)}) collective-permute-start(bf16[256,1024]{1,0:T(8,128)(2,1)} %add_convert_fusion.15.refs_0_), channel_id=1, source_target_pairs={{0,2},{1,3},{2,0},{3,1},{4,6},{5,7},{6,4},{7,5},{8,10},{9,11},{10,... | collective-permute-start | bytes 1572872 | tf_op jit(solution)/shard_map/ppermute | solution.py:442
  843.8 28.3 %collective-permute-start.82 = (bf16[256,1152]{1,0:T(8,128)(2,1)}, bf16[256,1152]{1,0:T(8,128)(2,1)}, u32[]{:S(2)}, u32[]{:S(2)}) collective-permute-start(bf16[256,1152]{1,0:T(8,128)(2,1)} %add_convert_fusion.13.refs_1_), channel_id=1, source_target_pairs={{0,1},{1,0},{2,3},{3,2},{4,5},{5,4},{6,7},{7,6},{8,9},{9,8},{10,11... | collective-permute-start | bytes 1769480 | tf_op jit(solution)/shard_map/ppermute | solution.py:439
  856.0 33.8 %collective-permute-start.87 = (bf16[256,2048]{1,0:T(8,128)(2,1)S(1)}, bf16[256,2048]{1,0:T(8,128)(2,1)S(1)}, u32[]{:S(2)}, u32[]{:S(2)}) collective-permute-start(bf16[256,2048]{1,0:T(8,128)(2,1)S(1)} %pad_maximum_fusion.5), channel_id=1, source_target_pairs={{0,2},{1,3},{2,0},{3,1},{4,6},{5,7},{6,4},{7,5},{8,10},{9,11},{10,... | collective-permute-start | bytes 3145736 | tf_op jit(solution)/shard_map/ppermute | solution.py:442
  (109 other events, 1396.7 us)

commit v4 on v3

--- a/solution.py
+++ b/solution.py
@@ -746,6 +746,7 @@
     g_come[0] = put(g_come[0])
     g_other.append(put(rows_of(after(normed_ffn, order.last), grad_both, 5)))
     g_come.append(links.across(g_other[1]))
+    g_second = links.around(put(rows_of(normed_ffn, grad_both, 0, after(g_come[0], order.last))), 1)
     for i in (6, 7):
         g_other.append(put(rows_of(after(normed_ffn, order.last), grad_both, i)))
     n_far, n_near = put(n_far), put(n_near)
@@ -753,9 +754,9 @@
     grad_att = put(in_row_order([sent, n_near, n_far, n_both]))
     g_come[1] = put(g_come[1])
     g_come.append(links.across(put(g_other[2])))
+    g_first = links.around(put(rows_of(normed_ffn, grad_both, 1, after(g_come[1], order.last))), -1)
+    d_third, g_second = put(d_third), put(g_second)
     grad_gated = put(dot(after(grad_att, order.last), out_w, 1, 1))
-    d_third = put(d_third)
-    g_second = links.around(put(rows_of(normed_ffn, grad_both, 0, after(g_come[0], order.last))), 1)
     left = blocks_at(gated, [(links.turn - r) % links.ring for r in ORDER], head_dim, 1)
     o_sums = put(dot(left, after(grad_att, order.last), 0, 0).astype(LOW))
     o_second, o_first, o_third, o_mine = jnp.split(o_sums, 4, axis=0)
@@ -764,13 +765,12 @@
         projected, bias, kept, after(grad_gated, order.last), cum, cum_rows, seg_col, seg_col.T, width, head_dim
     )
     grad_proj = put(grad_proj)
-    g_second, g_come[2] = put(g_second), put(g_come[2])
+    g_first, g_come[2] = put(g_first), put(g_come[2])
     g_come.append(links.across(put(g_other[3])))
     p_other = [put(rows_of(normed, after(grad_proj, order.last), 4))]
     back_rows = links.own_order(after(grad_proj, order.last))
     come = put(dot(back_rows[: 2 * count], proj_w, 1, 1).astype(LOW))
     come = links.core(come)
-    g_first = links.around(put(rows_of(normed_ffn, grad_both, 1, after(g_come[1], order.last))), -1)
     o_second, o_first = put(o_second), put(o_first)
     o_third = links.around(put(sum_low(o_third, o_second)), 1)
     g_come[3] = put(g_come[3])
@@ -781,13 +781,14 @@
     p_come.append(links.across(p_other[1]))
     far = dot(after(back_rows[2 * count : 3 * count], order.last), proj_w, 1, 1) + come[count:].astype(WIDE)
     going = come, links.chip(put(far.astype(LOW)))
-    g_first, o_third = put(g_first), put(o_third)
+    o_third = put(o_third)
     p_other.append(put(rows_of(normed, after(grad_proj, order.last), 6)))
     p_come[1] = put(p_come[1])
     p_come.append(links.across(p_other[2]))
     p_second = links.around(put(rows_of(normed, after(grad_proj, order.last), 0, p_come[0])), 1)
     d_total = put(sum_low(blocks_at(whole, places[3:4], part, 0), d_come[2][part:], d_first, d_third))
     g_third = put(g_third)
+    g_total = put(rows_of(normed_ffn, after(grad_both, order.last), 3, g_come[3], g_first, g_third))
     grad_normed_one = links.from_rel(tokens_end(going, back_rows, proj_w, (1, 1)))
     d_pieces = gather_seq(after(d_total, order.last))
     p_other.append(put(rows_of(normed, after(grad_proj, order.last), 7)))
@@ -802,8 +803,8 @@
     totals = totals_steps[0](totals)
     p_second = put(p_second)
     p_third = links.around(put(rows_of(normed, grad_proj, 2, p_come[2], p_second)), 1)
-    g_total = put(rows_of(normed_ffn, after(grad_both, order.last), 3, g_come[3], g_first, g_third))
-    g_pieces = gather_seq(g_total)
+    g_far = put(links.chip(g_total))
+    g_pieces = [g_total, links.core(g_total), g_far, links.core(g_far)]
     totals = totals_steps[1](put(totals))
     o_total = put(sum_low(o_mine, o_first, o_third))
     p_first = put(p_first)

time: 905 us -> 877 us (0.969)
  waiting for transfers between devices: 454 us -> 425 us
    ppermute x23, waiting for transfers between devices: 136 us -> 119 us  [across(): return lax.ppermute(value, 'dp', [(d, d ^ 1) for d in range(self.dp_count)])]
    ppermute x24, waiting for transfers between devices: 205 us -> 192 us  [around(): lax.ppermute(value, 'dp', [(d, (d + 2 * by) % count) for d in range(count)])]
    ppermute x13, waiting for transfers between devices: 75.1 us -> 85.4 us  [chip(): lax.ppermute(value, 'seq', [(s, s ^ 2) for s in range(self.seq_count)])]
    unnamed x232 -> x254, local copies, waits for them, and re-layouts: 47.9 us -> 43 us
  transfers between devices with their start and end apart: 88 -> 88, of which waited for: 46 -> 46; matrix products, arithmetic and copies ran while one was open for 22% -> 23% of each run, Pallas kernels for 13% -> 13%
where the time goes in v4:
time: 877 us; the launch traced here: 865 us
  waiting for transfers between devices  425 us (48%)
  matrix products  159 us (18%)
  Pallas kernels  119 us (14%)
  starting transfers between devices  65.9 us (8%)
  local copies, waits for them, and re-layouts  49.8 us (6%)
  other arithmetic  39.9 us (5%)
    ppermute x24, waiting for transfers between devices, around(): lax.ppermute(value, 'dp', [(d, (d + 2 * by) % count) for d in range(count)])  192 us
    dot_general x33, matrix products, dot(): lax.dot_general(left, right, (((left_dim,), (right_dim,)), ((), ())), pre...  159 us
    ppermute x23, waiting for transfers between devices, across(): return lax.ppermute(value, 'dp', [(d, d ^ 1) for d in range(self.dp_count)])  119 us
    ppermute x13, waiting for transfers between devices, chip(): lax.ppermute(value, 'seq', [(s, s ^ 2) for s in range(self.seq_count)])  85.4 us
    unnamed x254, local copies, waits for them, and re-layouts  43 us
    ppermute x23, starting transfers between devices, across(): return lax.ppermute(value, 'dp', [(d, d ^ 1) for d in range(self.dp_count)])  22.2 us
    pallas_call x1, Pallas kernels, gate_up_product(): pl.pallas_call(functools.partial(gate_up_kernel, count), grid=(steps,), i...  20 us
    pallas_call x1, Pallas kernels, retention_back(): pl.pallas_call(functools.partial(backward_kernel, row // 4, size ** (-0.5...  19.6 us
  transfers between devices with their start and end apart: 88, of which 46 were waited for; matrix products, arithmetic and copies ran while one was open for 23% of the time, Pallas kernels for 13%

profile of v4, /device:TPU:0, one launch (start us, length us, event | category | flops | bytes accessed | tf_op | source)
XLA Modules:
  0.0 864.7 jit_solution(5531869715714249803)
XLA Ops:
  2.1 4.2 shard_map.212.refs_4_
  21.2 5.8 shard_map.213.refs_4_.refs_12_
  27.0 9.2 %collective-permute-done.2.refs_2_ = bf16[256,2176]{1,0:T(8,128)(2,1)} collective-permute-done((bf16[256,2176]{1,0:T(8,128)(2,1)}, bf16[256,2176]{1,0:T(8,128)(2,1)}, u32[]{:S(2)}, u32[]{:S(2)}) %collective-permute-start.2) | collective-permute-done | bytes 1114144 | tf_op jit(solution)/shard_map/ppermute | solution.py:424
  36.3 7.2 collective-permute-done.3.refs_2_
  48.3 4.7 shard_map.215.refs_0_
  52.9 6.8 collective-permute-done.6
  59.8 12.7 %collective-permute-done.5.refs_1_ = bf16[256,2176]{1,0:T(8,128)(2,1)S(1)} collective-permute-done((bf16[256,2176]{1,0:T(8,128)(2,1)}, bf16[256,2176]{1,0:T(8,128)(2,1)S(1)}, u32[]{:S(2)}, u32[]{:S(2)}) %collective-permute-start.5) | collective-permute-done | bytes 1114144 | tf_op jit(solution)/shard_map/ppermute | solution.py:424
  74.3 9.4 %collective-permute-done.8.refs_6_ = bf16[256,2176]{1,0:T(8,128)(2,1)S(1)} collective-permute-done((bf16[256,2176]{1,0:T(8,128)(2,1)}, bf16[256,2176]{1,0:T(8,128)(2,1)S(1)}, u32[]{:S(2)}, u32[]{:S(2)}) %collective-permute-start.8) | collective-permute-done | bytes 1114144 | tf_op jit(solution)/shard_map/ppermute | solution.py:427
  83.7 18.1 %collective-permute-done.7.refs_3_ = bf16[256,2176]{1,0:T(8,128)(2,1)} collective-permute-done((bf16[256,2176]{1,0:T(8,128)(2,1)S(1)}, bf16[256,2176]{1,0:T(8,128)(2,1)}, u32[]{:S(2)}, u32[]{:S(2)}) %collective-permute-start.7) | collective-permute-done | bytes 1114144 | tf_op jit(solution)/shard_map/ppermute | solution.py:424
  102.3 5.1 collective-permute-done.9.refs_5_
  107.5 4.3 collective-permute-done.11
  114.1 12.5 %collective-permute-done.12 = bf16[128,2048]{1,0:T(8,128)(2,1)} collective-permute-done((bf16[128,2048]{1,0:T(8,128)(2,1)}, bf16[128,2048]{1,0:T(8,128)(2,1)}, u32[]{:S(2)}, u32[]{:S(2)}) %collective-permute-start.12) | collective-permute-done | bytes 524320 | tf_op jit(solution)/shard_map/ppermute | solution.py:424
  135.4 16.2 %shard_map.216.q.k.v.gate.logit = f32[1024,2176]{1,0:T(8,128)} custom-call(bf16[1024,2176]{1,0:T(8,128)(2,1)} %shard_map.215.refs_0_, bf16[256,2176]{1,0:T(8,128)(2,1)} %copy-done.25, bf16[256,2176]{1,0:T(8,128)(2,1)} %collective-permute-done.2.refs_2_, bf16[256,2176]{1,0:T(8,128)(2,1)} %collective-permute-done.7.refs_3_, ...), custom_call_target="tpu_custom_call" | custom-call | tf_op jit(solution)/shard_map/pallas_call | solution.py:53
  151.6 11.6 %shard_map.217 = (bf16[1024,512]{1,0:T(8,128)(2,1)}, f32[1024,512]{1,0:T(8,128)}, f32[1024,128]{1,0:T(8,128)}, f32[128,1024]{1,0:T(8,128)}) custom-call(f32[1024,2176]{1,0:T(8,128)} %shard_map.216.q.k.v.gate.logit, f32[1024,2176]{1,0:T(8,128)} %shard_map.216.q.k.v.gate.logit, f32[1024,2176]{1,0:T(8,128)} %shard_map.216.q.k.v.gate.logit, ...), custom_call_target="tpu_custom_call" | custom-call | tf_op jit(solution)/shard_map/pallas_call | solution.py:367
  167.3 3.9 collective-permute-done.15.refs_2_.refs_10_
  172.9 4.0 collective-permute-done.16
  181.8 26.4 %collective-permute-done.19.refs_1_.refs_9_ = bf16[256,2816]{1,0:T(8,128)(2,1)} collective-permute-done((bf16[256,2816]{1,0:T(8,128)(2,1)S(1)}, bf16[256,2816]{1,0:T(8,128)(2,1)}, u32[]{:S(2)}, u32[]{:S(2)}) %collective-permute-start.19) | collective-permute-done | bytes 1441824 | tf_op jit(solution)/shard_map/ppermute | solution.py:424
  209.1 4.2 bitcast_add_fusion
  216.1 27.6 %collective-permute-done.23.refs_3_.refs_11_ = bf16[256,2816]{1,0:T(8,128)(2,1)S(1)} collective-permute-done((bf16[256,2816]{1,0:T(8,128)(2,1)}, bf16[256,2816]{1,0:T(8,128)(2,1)S(1)}, u32[]{:S(2)}, u32[]{:S(2)}) %collective-permute-start.23) | collective-permute-done | bytes 1441824 | tf_op jit(solution)/shard_map/ppermute | solution.py:424
  248.7 15.7 %collective-permute-done.26 = bf16[176,2048]{1,0:T(8,128)(2,1)} collective-permute-done((bf16[176,2048]{1,0:T(8,128)(2,1)}, bf16[176,2048]{1,0:T(8,128)(2,1)}, u32[]{:S(2)}, u32[]{:S(2)}) %collective-permute-start.26) | collective-permute-done | bytes 720928 | tf_op jit(solution)/shard_map/ppermute | solution.py:424
  270.6 7.2 collective-permute-done.25.refs_7_.refs_15_
  279.8 20.0 %shard_map.218 = (f32[1024,1408]{1,0:T(8,128)}, f32[1024,1408]{1,0:T(8,128)}, bf16[1024,1408]{1,0:T(8,128)(2,1)}) custom-call(bf16[1024,2048]{1,0:T(8,128)(2,1)} %pad_maximum_fusion.1.refs_0_, bf16[256,2816]{1,0:T(8,128)(2,1)} %collective-permute-done.19.refs_1_.refs_9_, bf16[256,2816]{1,0:T(8,128)(2,1)} %copy-done.10, bf16[256,2816]{1,0:T(8,128)(2,1)} %copy-done.14, ...), custom_call_target="tpu_custom_call" | custom-call | tf_op jit(solution)/shard_map/pallas_call | solution.py:84
  299.9 11.4 %collective-permute-done.29 = bf16[176,2048]{1,0:T(8,128)(2,1)} collective-permute-done((bf16[176,2048]{1,0:T(8,128)(2,1)}, bf16[176,2048]{1,0:T(8,128)(2,1)}, u32[]{:S(2)}, u32[]{:S(2)}) %collective-permute-start.29) | collective-permute-done | bytes 720928 | tf_op jit(solution)/shard_map/ppermute | solution.py:427
  324.1 6.0 collective-permute-done.28
  333.1 12.9 %collective-permute-done.32 = bf16[176,2048]{1,0:T(8,128)(2,1)S(1)} collective-permute-done((bf16[176,2048]{1,0:T(8,128)(2,1)S(1)}, bf16[176,2048]{1,0:T(8,128)(2,1)S(1)}, u32[]{:S(2)}, u32[]{:S(2)}) %collective-permute-start.32) | collective-permute-done | bytes 720928 | tf_op jit(solution)/shard_map/ppermute | solution.py:427
  349.4 4.0 convolution_convert_fusion.12
  353.5 4.1 collective-permute-done.33
  361.6 23.0 %collective-permute-done.34 = bf16[256,2048]{1,0:T(8,128)(2,1)S(1)} collective-permute-done((bf16[256,2048]{1,0:T(8,128)(2,1)S(1)}, bf16[256,2048]{1,0:T(8,128)(2,1)S(1)}, u32[]{:S(2)}, u32[]{:S(2)}) %collective-permute-start.34) | collective-permute-done | bytes 1048608 | tf_op jit(solution)/shard_map/ppermute | solution.py:442
  384.7 5.0 fusion.98
  391.2 23.0 %collective-permute-done.36 = bf16[256,2048]{1,0:T(8,128)(2,1)} collective-permute-done((bf16[256,2048]{1,0:T(8,128)(2,1)S(1)}, bf16[256,2048]{1,0:T(8,128)(2,1)}, u32[]{:S(2)}, u32[]{:S(2)}) %collective-permute-start.36) | collective-permute-done | bytes 1048608 | tf_op jit(solution)/shard_map/ppermute | solution.py:442
  419.4 6.5 convolution_convert_fusion
  429.1 8.5 fusion.102
  437.6 6.0 multiply_convert_fusion.1
  446.6 10.6 %convolution_convert_fusion.10 = bf16[512,2048]{1,0:T(8,128)(2,1)S(1)} fusion(bf16[2048,2816]{1,0:T(8,128)(2,1)} %copy-done.69, bf16[1024,2816]{1,0:T(8,128)(2,1)S(1)} %pad_maximum_fusion), kind=kOutput, calls=%fused_computation.23 | convolution fusion | flops 5906628608 | bytes 16515072 | tf_op jit(solution)/shard_map/dot_general | solution.py:18
  458.9 16.9 %collective-permute-done.40 = bf16[176,2048]{1,0:T(8,128)(2,1)S(1)} collective-permute-done((bf16[176,2048]{1,0:T(8,128)(2,1)S(1)}, bf16[176,2048]{1,0:T(8,128)(2,1)S(1)}, u32[]{:S(2)}, u32[]{:S(2)}) %collective-permute-start.40) | collective-permute-done | bytes 720928 | tf_op jit(solution)/shard_map/ppermute | solution.py:427
  477.4 9.2 %add_convert_fusion.6 = bf16[256,2048]{1,0:T(8,128)(2,1)} fusion(bf16[512,2048]{1,0:T(8,128)(2,1)S(1)} %collective-permute-done.39, bf16[2048,2816]{1,0:T(8,128)(2,1)} %copy-done.69, bf16[1024,2816]{1,0:T(8,128)(2,1)S(1)} %pad_maximum_fusion), kind=kOutput, calls=%fused_computation.59 | convolution fusion | flops 2954362880 | bytes 15073280 | tf_op jit(solution)/shard_map/dot_general | solution.py:18
  491.4 3.8 collective-permute-start.47
  495.3 5.5 convolution_convert_fusion.4
  500.7 8.4 collective-permute-done.42
  511.4 13.4 %convert_add_fusion.1 = f32[256,2048]{1,0:T(8,128)} fusion(bf16[256,2048]{1,0:T(8,128)(2,1)} %collective-permute-done.41, bf16[512,2048]{1,0:T(8,128)(2,1)} %copy-done.77, bf16[2048,2816]{1,0:T(8,128)(2,1)} %copy-done.69, bf16[1024,2816]{1,0:T(8,128)(2,1)S(1)} %bitcast.72), kind=kOutput, calls=%fused_computation.58 | convolution fusion | flops 2954887168 | bytes 17170432 | tf_op jit(solution)/shard_map/dot_general | solution.py:18
  537.0 4.6 collective-permute-done.45
  546.0 4.2 fusion
  560.0 5.0 shard_map.219
  565.0 11.2 %collective-permute-done.51 = bf16[256,2816]{1,0:T(8,128)(2,1)} collective-permute-done((bf16[256,2816]{1,0:T(8,128)(2,1)}, bf16[256,2816]{1,0:T(8,128)(2,1)}, u32[]{:S(2)}, u32[]{:S(2)}) %collective-permute-start.51) | collective-permute-done | bytes 1441824 | tf_op jit(solution)/shard_map/ppermute | solution.py:427
  577.8 4.4 fusion.1
  583.5 24.7 %collective-permute-done.50 = bf16[176,2048]{1,0:T(8,128)(2,1)} collective-permute-done((bf16[176,2048]{1,0:T(8,128)(2,1)}, bf16[176,2048]{1,0:T(8,128)(2,1)}, u32[]{:S(2)}, u32[]{:S(2)}) %collective-permute-start.50) | collective-permute-done | bytes 720928 | tf_op jit(solution)/shard_map/ppermute | solution.py:424
  614.3 19.6 %shard_map.220 = (bf16[1024,2176]{1,0:T(8,128)(2,1)}, f32[1,128]{1,0:T(1,128)}) custom-call(f32[1024,2176]{1,0:T(8,128)} %shard_map.216.q.k.v.gate.logit, f32[1024,2176]{1,0:T(8,128)} %shard_map.216.q.k.v.gate.logit, f32[1024,2176]{1,0:T(8,128)} %shard_map.216.q.k.v.gate.logit, f32[1024,2176]{1,0:T(8,128)} %shard_map.216.q.k.v.gate.logit, ...), custom_call_target="tpu_custom_call" | custom-call | tf_op jit(solution)/shard_map/pallas_call | solution.py:388
  634.3 4.8 collective-permute-done.53
  639.8 3.9 convolution_convert_fusion.8
  643.9 9.3 %convolution_convert_fusion.13 = bf16[512,2048]{1,0:T(8,128)(2,1)S(1)} fusion(bf16[2048,2176]{1,0:T(8,128)(2,1)} %copy-done.70, bf16[256,2176]{1,0:T(8,128)(2,1)S(1)} %get-tuple-element.465, bf16[256,2176]{1,0:T(8,128)(2,1)S(1)} %get-tuple-element.463), kind=kOutput, calls=%fused_computation.26 | convolution fusion | flops 4568907776 | bytes 13238272 | tf_op jit(solution)/shard_map/dot_general | solution.py:18
  658.8 10.2 %collective-permute-done.58 = bf16[128,2048]{1,0:T(8,128)(2,1)S(1)} collective-permute-done((bf16[128,2048]{1,0:T(8,128)(2,1)S(1)}, bf16[128,2048]{1,0:T(8,128)(2,1)S(1)}, u32[]{:S(2)}, u32[]{:S(2)}) %collective-permute-start.58) | collective-permute-done | bytes 524320 | tf_op jit(solution)/shard_map/ppermute | solution.py:424
  681.0 16.6 %collective-permute-done.55 = bf16[256,2176]{1,0:T(8,128)(2,1)} collective-permute-done((bf16[256,2176]{1,0:T(8,128)(2,1)S(1)}, bf16[256,2176]{1,0:T(8,128)(2,1)}, u32[]{:S(2)}, u32[]{:S(2)}) %collective-permute-start.55) | collective-permute-done | bytes 1114144 | tf_op jit(solution)/shard_map/ppermute | solution.py:427
  697.6 10.5 %add_convert_fusion.5 = bf16[256,2048]{1,0:T(8,128)(2,1)} fusion(bf16[512,2048]{1,0:T(8,128)(2,1)} %collective-permute-done.54, bf16[256,2176]{1,0:T(8,128)(2,1)S(1)} %get-tuple-element.369, bf16[2048,2176]{1,0:T(8,128)(2,1)} %copy-done.70), kind=kOutput, calls=%fused_computation.55 | convolution fusion | flops 2283274240 | bytes 12124160 | tf_op jit(solution)/shard_map/dot_general | solution.py:18
  712.7 8.8 %collective-permute-done.61 = bf16[256,2176]{1,0:T(8,128)(2,1)} collective-permute-done((bf16[256,2176]{1,0:T(8,128)(2,1)}, bf16[256,2176]{1,0:T(8,128)(2,1)}, u32[]{:S(2)}, u32[]{:S(2)}) %collective-permute-start.61) | collective-permute-done | bytes 1114144 | tf_op jit(solution)/shard_map/ppermute | solution.py:427
  732.9 6.7 convert_add_fusion
  750.4 4.5 collective-permute-done.67
  758.7 19.0 %collective-permute-done.71.refs_2_ = bf16[176,2048]{1,0:T(8,128)(2,1)S(1)} collective-permute-done((bf16[176,2048]{1,0:T(8,128)(2,1)S(1)}, bf16[176,2048]{1,0:T(8,128)(2,1)S(1)}, u32[]{:S(2)}, u32[]{:S(2)}) %collective-permute-start.71) | collective-permute-done | bytes 720928 | tf_op jit(solution)/shard_map/ppermute | solution.py:442
  782.5 4.8 shard_map.221
  789.0 10.7 %collective-permute-done.73 = bf16[256,2176]{1,0:T(8,128)(2,1)} collective-permute-done((bf16[256,2176]{1,0:T(8,128)(2,1)}, bf16[256,2176]{1,0:T(8,128)(2,1)}, u32[]{:S(2)}, u32[]{:S(2)}) %collective-permute-start.73) | collective-permute-done | bytes 1114144 | tf_op jit(solution)/shard_map/ppermute | solution.py:424
  811.6 10.2 %collective-permute-done.80.refs_2_ = bf16[256,1024]{1,0:T(8,128)(2,1)} collective-permute-done((bf16[256,1024]{1,0:T(8,128)(2,1)}, bf16[256,1024]{1,0:T(8,128)(2,1)}, u32[]{:S(2)}, u32[]{:S(2)}) %collective-permute-start.80) | collective-permute-done | bytes 524320 | tf_op jit(solution)/shard_map/ppermute | solution.py:442
  824.4 11.2 %shard_map.222 = f32[256,11008]{1,0:T(8,128)} custom-call(bf16[256,2816]{1,0:T(8,128)(2,1)} %copy-done.21, bf16[256,2816]{1,0:T(8,128)(2,1)} %collective-permute-done.77.refs_1_, bf16[256,2816]{1,0:T(8,128)(2,1)} %collective-permute-done.66.refs_2_, bf16[256,2816]{1,0:T(8,128)(2,1)} %collective-permute-done.78.refs_3_), custom_call_target="tpu_custom_call" | custom-call | tf_op jit(solution)/shard_map/pallas_call | solution.py:547
  839.5 4.7 collective-permute-done.86
  844.2 6.2 shard_map.223.refs_0_
  855.2 6.3 shard_map.224
  (478 shorter events, 221.6 us)
Async XLA Ops:
  6.3 29.9 %collective-permute-start.2 = (bf16[256,2176]{1,0:T(8,128)(2,1)}, bf16[256,2176]{1,0:T(8,128)(2,1)}, u32[]{:S(2)}, u32[]{:S(2)}) collective-permute-start(bf16[256,2176]{1,0:T(8,128)(2,1)} %shard_map.212.refs_4_), channel_id=1, source_target_pairs={{0,8},{4,12},{8,16},{12,20},{16,24},{20,28},{24,0},{28,4},{1,9},{5... | collective-permute-start | bytes 3342344 | tf_op jit(solution)/shard_map/ppermute | solution.py:424
  9.3 26.9 %collective-permute-start.1 = (bf16[256,2176]{1,0:T(8,128)(2,1)}, bf16[256,2176]{1,0:T(8,128)(2,1)S(1)}, u32[]{:S(2)}, u32[]{:S(2)}) collective-permute-start(bf16[256,2176]{1,0:T(8,128)(2,1)} %shard_map.212.refs_4_), channel_id=1, source_target_pairs={{0,4},{4,0},{8,12},{12,8},{16,20},{20,16},{24,28},{28,24},{1,5},{5... | collective-permute-start | bytes 3342344 | tf_op jit(solution)/shard_map/ppermute | solution.py:427
  16.3 20.0 %collective-permute-start = (bf16[256,2176]{1,0:T(8,128)(2,1)S(1)}, bf16[256,2176]{1,0:T(8,128)(2,1)S(1)}, u32[]{:S(2)}, u32[]{:S(2)}) collective-permute-start(bf16[256,2176]{1,0:T(8,128)(2,1)S(1)} %constant_dynamic-update-slice_fusion.refs_0_), channel_id=1, source_target_pairs={{0,1},{1,0},{2,3},{3,2},{4,5},{5,4},{6,7},{7,6},{8,9},{9,8},{10,11... | collective-permute-start | bytes 3342344 | tf_op jit(solution)/shard_map/ppermute | solution.py:439
  16.3 27.1 %collective-permute-start.3 = (bf16[256,2176]{1,0:T(8,128)(2,1)S(1)}, bf16[256,2176]{1,0:T(8,128)(2,1)}, u32[]{:S(2)}, u32[]{:S(2)}) collective-permute-start(bf16[256,2176]{1,0:T(8,128)(2,1)S(1)} %constant_dynamic-update-slice_fusion.refs_0_), channel_id=1, source_target_pairs={{0,2},{1,3},{2,0},{3,1},{4,6},{5,7},{6,4},{7,5},{8,10},{9,11},{10,... | collective-permute-start | bytes 3342344 | tf_op jit(solution)/shard_map/ppermute | solution.py:442
  43.4 29.0 %collective-permute-start.5 = (bf16[256,2176]{1,0:T(8,128)(2,1)}, bf16[256,2176]{1,0:T(8,128)(2,1)S(1)}, u32[]{:S(2)}, u32[]{:S(2)}) collective-permute-start(bf16[256,2176]{1,0:T(8,128)(2,1)} %collective-permute-done.2.refs_2_), channel_id=1, source_target_pairs={{0,8},{4,12},{8,16},{12,20},{16,24},{20,28},{24,0},{28,4},{1,9},{5... | collective-permute-start | bytes 3342344 | tf_op jit(solution)/shard_map/ppermute | solution.py:424
  48.2 35.4 %collective-permute-start.8 = (bf16[256,2176]{1,0:T(8,128)(2,1)}, bf16[256,2176]{1,0:T(8,128)(2,1)S(1)}, u32[]{:S(2)}, u32[]{:S(2)}) collective-permute-start(bf16[256,2176]{1,0:T(8,128)(2,1)} %collective-permute-done.2.refs_2_), channel_id=1, source_target_pairs={{0,4},{4,0},{8,12},{12,8},{16,20},{20,16},{24,28},{28,24},{1,5},{5... | collective-permute-start | bytes 3342344 | tf_op jit(solution)/shard_map/ppermute | solution.py:427
  72.4 29.4 %collective-permute-start.7 = (bf16[256,2176]{1,0:T(8,128)(2,1)S(1)}, bf16[256,2176]{1,0:T(8,128)(2,1)}, u32[]{:S(2)}, u32[]{:S(2)}) collective-permute-start(bf16[256,2176]{1,0:T(8,128)(2,1)S(1)} %collective-permute-done.5.refs_1_), channel_id=1, source_target_pairs={{0,8},{4,12},{8,16},{12,20},{16,24},{20,28},{24,0},{28,4},{1,9},{5... | collective-permute-start | bytes 3342344 | tf_op jit(solution)/shard_map/ppermute | solution.py:424
  72.4 35.0 %collective-permute-start.9 = (bf16[256,2176]{1,0:T(8,128)(2,1)S(1)}, bf16[256,2176]{1,0:T(8,128)(2,1)S(1)}, u32[]{:S(2)}, u32[]{:S(2)}) collective-permute-start(bf16[256,2176]{1,0:T(8,128)(2,1)S(1)} %collective-permute-done.5.refs_1_), channel_id=1, source_target_pairs={{0,4},{4,0},{8,12},{12,8},{16,20},{20,16},{24,28},{28,24},{1,5},{5... | collective-permute-start | bytes 3342344 | tf_op jit(solution)/shard_map/ppermute | solution.py:427
  72.9 38.8 %collective-permute-start.11 = (bf16[128,2048]{1,0:T(8,128)(2,1)S(1)}, bf16[128,2048]{1,0:T(8,128)(2,1)}, u32[]{:S(2)}, u32[]{:S(2)}) collective-permute-start(bf16[128,2048]{1,0:T(8,128)(2,1)S(1)} %broadcast_select_fusion.2), channel_id=1, source_target_pairs={{0,8},{4,12},{8,16},{12,20},{16,24},{20,28},{24,0},{28,4},{1,9},{5... | collective-permute-start | bytes 1572872 | tf_op jit(solution)/shard_map/ppermute | solution.py:424
  101.8 28.9 %collective-permute-start.10 = (bf16[256,2176]{1,0:T(8,128)(2,1)}, bf16[256,2176]{1,0:T(8,128)(2,1)}, u32[]{:S(2)}, u32[]{:S(2)}) collective-permute-start(bf16[256,2176]{1,0:T(8,128)(2,1)} %collective-permute-done.7.refs_3_), channel_id=1, source_target_pairs={{0,4},{4,0},{8,12},{12,8},{16,20},{20,16},{24,28},{28,24},{1,5},{5... | collective-permute-start | bytes 3342344 | tf_op jit(solution)/shard_map/ppermute | solution.py:427
  126.5 36.7 %collective-permute-start.13 = (bf16[128,2048]{1,0:T(8,128)(2,1)}, bf16[128,2048]{1,0:T(8,128)(2,1)S(1)}, u32[]{:S(2)}, u32[]{:S(2)}) collective-permute-start(bf16[128,2048]{1,0:T(8,128)(2,1)} %collective-permute-done.12), channel_id=1, source_target_pairs={{0,8},{4,12},{8,16},{12,20},{16,24},{20,28},{24,0},{28,4},{1,9},{5... | collective-permute-start | bytes 1572872 | tf_op jit(solution)/shard_map/ppermute | solution.py:424
  128.3 42.9 %collective-permute-start.15 = (bf16[256,2816]{1,0:T(8,128)(2,1)S(1)}, bf16[256,2816]{1,0:T(8,128)(2,1)S(1)}, u32[]{:S(2)}, u32[]{:S(2)}) collective-permute-start(bf16[256,2816]{1,0:T(8,128)(2,1)S(1)} %copy-done.5), channel_id=1, source_target_pairs={{0,8},{4,12},{8,16},{12,20},{16,24},{20,28},{24,0},{28,4},{1,9},{5... | collective-permute-start | bytes 4325384 | tf_op jit(solution)/shard_map/ppermute | solution.py:424
  130.7 40.5 %collective-permute-start.14 = (bf16[256,2816]{1,0:T(8,128)(2,1)S(1)}, bf16[256,2816]{1,0:T(8,128)(2,1)S(1)}, u32[]{:S(2)}, u32[]{:S(2)}) collective-permute-start(bf16[256,2816]{1,0:T(8,128)(2,1)S(1)} %copy-done.5), channel_id=1, source_target_pairs={{0,4},{4,0},{8,12},{12,8},{16,20},{20,16},{24,28},{28,24},{1,5},{5... | collective-permute-start | bytes 4325384 | tf_op jit(solution)/shard_map/ppermute | solution.py:427
  172.4 35.9 %collective-permute-start.19 = (bf16[256,2816]{1,0:T(8,128)(2,1)S(1)}, bf16[256,2816]{1,0:T(8,128)(2,1)}, u32[]{:S(2)}, u32[]{:S(2)}) collective-permute-start(bf16[256,2816]{1,0:T(8,128)(2,1)S(1)} %collective-permute-done.15.refs_2_.refs_10_), channel_id=1, source_target_pairs={{0,8},{4,12},{8,16},{12,20},{16,24},{20,28},{24,0},{28,4},{1,9},{5... | collective-permute-start | bytes 4325384 | tf_op jit(solution)/shard_map/ppermute | solution.py:424
  172.4 36.7 %collective-permute-start.18 = (bf16[256,2816]{1,0:T(8,128)(2,1)S(1)}, bf16[256,2816]{1,0:T(8,128)(2,1)S(1)}, u32[]{:S(2)}, u32[]{:S(2)}) collective-permute-start(bf16[256,2816]{1,0:T(8,128)(2,1)S(1)} %collective-permute-done.15.refs_2_.refs_10_), channel_id=1, source_target_pairs={{0,4},{4,0},{8,12},{12,8},{16,20},{20,16},{24,28},{28,24},{1,5},{5... | collective-permute-start | bytes 4325384 | tf_op jit(solution)/shard_map/ppermute | solution.py:427
  180.3 28.8 %collective-permute-start.17 = (bf16[256,2048]{1,0:T(8,128)(2,1)}, bf16[256,2048]{1,0:T(8,128)(2,1)}, u32[]{:S(2)}, u32[]{:S(2)}) collective-permute-start(bf16[256,2048]{1,0:T(8,128)(2,1)} %add_convert_fusion.8), channel_id=1, source_target_pairs={{0,2},{1,3},{2,0},{3,1},{4,6},{5,7},{6,4},{7,5},{8,10},{9,11},{10,... | collective-permute-start | bytes 3145736 | tf_op jit(solution)/shard_map/ppermute | solution.py:442
  208.3 35.5 %collective-permute-start.23 = (bf16[256,2816]{1,0:T(8,128)(2,1)}, bf16[256,2816]{1,0:T(8,128)(2,1)S(1)}, u32[]{:S(2)}, u32[]{:S(2)}) collective-permute-start(bf16[256,2816]{1,0:T(8,128)(2,1)} %collective-permute-done.19.refs_1_.refs_9_), channel_id=1, source_target_pairs={{0,8},{4,12},{8,16},{12,20},{16,24},{20,28},{24,0},{28,4},{1,9},{5... | collective-permute-start | bytes 4325384 | tf_op jit(solution)/shard_map/ppermute | solution.py:424
  208.5 35.2 %collective-permute-start.22 = (bf16[256,2816]{1,0:T(8,128)(2,1)}, bf16[256,2816]{1,0:T(8,128)(2,1)}, u32[]{:S(2)}, u32[]{:S(2)}) collective-permute-start(bf16[256,2816]{1,0:T(8,128)(2,1)} %collective-permute-done.19.refs_1_.refs_9_), channel_id=1, source_target_pairs={{0,4},{4,0},{8,12},{12,8},{16,20},{20,16},{24,28},{28,24},{1,5},{5... | collective-permute-start | bytes 4325384 | tf_op jit(solution)/shard_map/ppermute | solution.py:427
  214.6 29.2 %collective-permute-start.21 = (bf16[256,2048]{1,0:T(8,128)(2,1)S(1)}, bf16[256,2048]{1,0:T(8,128)(2,1)S(1)}, u32[]{:S(2)}, u32[]{:S(2)}) collective-permute-start(bf16[256,2048]{1,0:T(8,128)(2,1)S(1)} %constant_dynamic-update-slice_fusion.13), channel_id=1, source_target_pairs={{0,2},{1,3},{2,0},{3,1},{4,6},{5,7},{6,4},{7,5},{8,10},{9,11},{10,... | collective-permute-start | bytes 3145736 | tf_op jit(solution)/shard_map/ppermute | solution.py:442
  216.1 28.4 %collective-permute-start.20 = (bf16[256,2048]{1,0:T(8,128)(2,1)S(1)}, bf16[256,2048]{1,0:T(8,128)(2,1)S(1)}, u32[]{:S(2)}, u32[]{:S(2)}) collective-permute-start(bf16[256,2048]{1,0:T(8,128)(2,1)S(1)} %constant_dynamic-update-slice_fusion.13), channel_id=1, source_target_pairs={{0,1},{1,0},{2,3},{3,2},{4,5},{5,4},{6,7},{7,6},{8,9},{9,8},{10,11... | collective-permute-start | bytes 3145736 | tf_op jit(solution)/shard_map/ppermute | solution.py:439
  243.8 20.7 %collective-permute-start.26 = (bf16[176,2048]{1,0:T(8,128)(2,1)}, bf16[176,2048]{1,0:T(8,128)(2,1)}, u32[]{:S(2)}, u32[]{:S(2)}) collective-permute-start(bf16[176,2048]{1,0:T(8,128)(2,1)} %get-tuple-element.274), channel_id=1, source_target_pairs={{0,8},{4,12},{8,16},{12,20},{16,24},{20,28},{24,0},{28,4},{1,9},{5... | collective-permute-start | bytes 2162696 | tf_op jit(solution)/shard_map/ppermute | solution.py:424
  243.9 33.9 %collective-permute-start.25 = (bf16[256,2816]{1,0:T(8,128)(2,1)S(1)}, bf16[256,2816]{1,0:T(8,128)(2,1)S(1)}, u32[]{:S(2)}, u32[]{:S(2)}) collective-permute-start(bf16[256,2816]{1,0:T(8,128)(2,1)S(1)} %collective-permute-done.23.refs_3_.refs_11_), channel_id=1, source_target_pairs={{0,4},{4,0},{8,12},{12,8},{16,20},{20,16},{24,28},{28,24},{1,5},{5... | collective-permute-start | bytes 4325384 | tf_op jit(solution)/shard_map/ppermute | solution.py:427
  264.5 35.4 %collective-permute-start.27 = (bf16[176,2048]{1,0:T(8,128)(2,1)}, bf16[176,2048]{1,0:T(8,128)(2,1)}, u32[]{:S(2)}, u32[]{:S(2)}) collective-permute-start(bf16[176,2048]{1,0:T(8,128)(2,1)} %collective-permute-done.26), channel_id=1, source_target_pairs={{0,8},{4,12},{8,16},{12,20},{16,24},{20,28},{24,0},{28,4},{1,9},{5... | collective-permute-start | bytes 2162696 | tf_op jit(solution)/shard_map/ppermute | solution.py:424
  277.8 22.1 %collective-permute-start.30 = (bf16[176,2048]{1,0:T(8,128)(2,1)}, bf16[176,2048]{1,0:T(8,128)(2,1)}, u32[]{:S(2)}, u32[]{:S(2)}) collective-permute-start(bf16[176,2048]{1,0:T(8,128)(2,1)} %get-tuple-element.274), channel_id=1, source_target_pairs={{0,4},{4,0},{8,12},{12,8},{16,20},{20,16},{24,28},{28,24},{1,5},{5... | collective-permute-start | bytes 2162696 | tf_op jit(solution)/shard_map/ppermute | solution.py:427
  278.3 33.0 %collective-permute-start.29 = (bf16[176,2048]{1,0:T(8,128)(2,1)}, bf16[176,2048]{1,0:T(8,128)(2,1)}, u32[]{:S(2)}, u32[]{:S(2)}) collective-permute-start(bf16[176,2048]{1,0:T(8,128)(2,1)} %collective-permute-done.26), channel_id=1, source_target_pairs={{0,4},{4,0},{8,12},{12,8},{16,20},{20,16},{24,28},{28,24},{1,5},{5... | collective-permute-start | bytes 2162696 | tf_op jit(solution)/shard_map/ppermute | solution.py:427
  311.3 18.8 %collective-permute-start.28 = (bf16[176,2048]{1,0:T(8,128)(2,1)}, bf16[176,2048]{1,0:T(8,128)(2,1)S(1)}, u32[]{:S(2)}, u32[]{:S(2)}) collective-permute-start(bf16[176,2048]{1,0:T(8,128)(2,1)} %collective-permute-done.27), channel_id=1, source_target_pairs={{0,8},{4,12},{8,16},{12,20},{16,24},{20,28},{24,0},{28,4},{1,9},{5... | collective-permute-start | bytes 2162696 | tf_op jit(solution)/shard_map/ppermute | solution.py:424
  311.3 19.3 %collective-permute-start.31 = (bf16[176,2048]{1,0:T(8,128)(2,1)}, bf16[176,2048]{1,0:T(8,128)(2,1)S(1)}, u32[]{:S(2)}, u32[]{:S(2)}) collective-permute-start(bf16[176,2048]{1,0:T(8,128)(2,1)} %collective-permute-done.27), channel_id=1, source_target_pairs={{0,4},{4,0},{8,12},{12,8},{16,20},{20,16},{24,28},{28,24},{1,5},{5... | collective-permute-start | bytes 2162696 | tf_op jit(solution)/shard_map/ppermute | solution.py:427
  359.4 25.3 %collective-permute-start.34 = (bf16[256,2048]{1,0:T(8,128)(2,1)S(1)}, bf16[256,2048]{1,0:T(8,128)(2,1)S(1)}, u32[]{:S(2)}, u32[]{:S(2)}) collective-permute-start(bf16[256,2048]{1,0:T(8,128)(2,1)S(1)} %add_convert_fusion.7), channel_id=1, source_target_pairs={{0,2},{1,3},{2,0},{3,1},{4,6},{5,7},{6,4},{7,5},{8,10},{9,11},{10,... | collective-permute-start | bytes 3145736 | tf_op jit(solution)/shard_map/ppermute | solution.py:442
  389.7 24.5 %collective-permute-start.36 = (bf16[256,2048]{1,0:T(8,128)(2,1)S(1)}, bf16[256,2048]{1,0:T(8,128)(2,1)}, u32[]{:S(2)}, u32[]{:S(2)}) collective-permute-start(bf16[256,2048]{1,0:T(8,128)(2,1)S(1)} %get-tuple-element.294), channel_id=1, source_target_pairs={{0,2},{1,3},{2,0},{3,1},{4,6},{5,7},{6,4},{7,5},{8,10},{9,11},{10,... | collective-permute-start | bytes 3145736 | tf_op jit(solution)/shard_map/ppermute | solution.py:442
  391.2 23.0 %collective-permute-start.35 = (bf16[256,2048]{1,0:T(8,128)(2,1)S(1)}, bf16[256,2048]{1,0:T(8,128)(2,1)}, u32[]{:S(2)}, u32[]{:S(2)}) collective-permute-start(bf16[256,2048]{1,0:T(8,128)(2,1)S(1)} %get-tuple-element.294), channel_id=1, source_target_pairs={{0,1},{1,0},{2,3},{3,2},{4,5},{5,4},{6,7},{7,6},{8,9},{9,8},{10,11... | collective-permute-start | bytes 3145736 | tf_op jit(solution)/shard_map/ppermute | solution.py:439
  457.2 20.2 %collective-permute-start.39 = (bf16[512,2048]{1,0:T(8,128)(2,1)S(1)}, bf16[512,2048]{1,0:T(8,128)(2,1)S(1)}, u32[]{:S(2)}, u32[]{:S(2)}) collective-permute-start(bf16[512,2048]{1,0:T(8,128)(2,1)S(1)} %convolution_convert_fusion.10), channel_id=1, source_target_pairs={{0,1},{1,0},{2,3},{3,2},{4,5},{5,4},{6,7},{7,6},{8,9},{9,8},{10,11... | collective-permute-start | bytes 6291464 | tf_op jit(solution)/shard_map/ppermute | solution.py:439
  475.8 33.3 %collective-permute-start.42 = (bf16[352,2048]{1,0:T(8,128)(2,1)S(1)}, bf16[352,2048]{1,0:T(8,128)(2,1)}, u32[]{:S(2)}, u32[]{:S(2)}) collective-permute-start(bf16[352,2048]{1,0:T(8,128)(2,1)S(1)} %pad_maximum_fusion.4), channel_id=1, source_target_pairs={{0,4},{4,0},{8,12},{12,8},{16,20},{20,16},{24,28},{28,24},{1,5},{5... | collective-permute-start | bytes 4325384 | tf_op jit(solution)/shard_map/ppermute | solution.py:427
  486.6 24.8 %collective-permute-start.41 = (bf16[256,2048]{1,0:T(8,128)(2,1)}, bf16[256,2048]{1,0:T(8,128)(2,1)}, u32[]{:S(2)}, u32[]{:S(2)}) collective-permute-start(bf16[256,2048]{1,0:T(8,128)(2,1)} %add_convert_fusion.6), channel_id=1, source_target_pairs={{0,2},{1,3},{2,0},{3,1},{4,6},{5,7},{6,4},{7,5},{8,10},{9,11},{10,... | collective-permute-start | bytes 3145736 | tf_op jit(solution)/shard_map/ppermute | solution.py:442
  491.4 42.8 %collective-permute-start.46 = (bf16[176,2048]{1,0:T(8,128)(2,1)}, bf16[176,2048]{1,0:T(8,128)(2,1)}, u32[]{:S(2)}, u32[]{:S(2)}) collective-permute-start(bf16[176,2048]{1,0:T(8,128)(2,1)} %get-tuple-element.313), channel_id=1, source_target_pairs={{0,8},{4,12},{8,16},{12,20},{16,24},{20,28},{24,0},{28,4},{1,9},{5... | collective-permute-start | bytes 2162696 | tf_op jit(solution)/shard_map/ppermute | solution.py:424
  491.4 42.8 %collective-permute-start.47 = (bf16[176,2048]{1,0:T(8,128)(2,1)S(1)}, bf16[176,2048]{1,0:T(8,128)(2,1)}, u32[]{:S(2)}, u32[]{:S(2)}) collective-permute-start(bf16[176,2048]{1,0:T(8,128)(2,1)S(1)} %get-tuple-element.314), channel_id=1, source_target_pairs={{0,24},{4,28},{8,0},{12,4},{16,8},{20,12},{24,16},{28,20},{1,25},{... | collective-permute-start | bytes 2162696 | tf_op jit(solution)/shard_map/ppermute | solution.py:424
  509.1 32.6 %collective-permute-start.45 = (bf16[256,2816]{1,0:T(8,128)(2,1)}, bf16[256,2816]{1,0:T(8,128)(2,1)}, u32[]{:S(2)}, u32[]{:S(2)}) collective-permute-start(bf16[256,2816]{1,0:T(8,128)(2,1)} %convolution_convert_fusion.4), channel_id=1, source_target_pairs={{0,4},{4,0},{8,12},{12,8},{16,20},{20,16},{24,28},{28,24},{1,5},{5... | collective-permute-start | bytes 4325384 | tf_op jit(solution)/shard_map/ppermute | solution.py:427
  532.7 23.5 %collective-permute-start.44 = (bf16[256,2048]{1,0:T(8,128)(2,1)S(1)}, bf16[256,2048]{1,0:T(8,128)(2,1)S(1)}, u32[]{:S(2)}, u32[]{:S(2)}) collective-permute-start(bf16[256,2048]{1,0:T(8,128)(2,1)S(1)} %get-tuple-element.321.refs_0_), channel_id=1, source_target_pairs={{0,2},{1,3},{2,0},{3,1},{4,6},{5,7},{6,4},{7,5},{8,10},{9,11},{10,... | collective-permute-start | bytes 3145736 | tf_op jit(solution)/shard_map/ppermute | solution.py:442
  534.2 25.8 %collective-permute-start.43 = (bf16[256,2048]{1,0:T(8,128)(2,1)S(1)}, bf16[256,2048]{1,0:T(8,128)(2,1)}, u32[]{:S(2)}, u32[]{:S(2)}) collective-permute-start(bf16[256,2048]{1,0:T(8,128)(2,1)S(1)} %get-tuple-element.321.refs_0_), channel_id=1, source_target_pairs={{0,1},{1,0},{2,3},{3,2},{4,5},{5,4},{6,7},{7,6},{8,9},{9,8},{10,11... | collective-permute-start | bytes 3145736 | tf_op jit(solution)/shard_map/ppermute | solution.py:439
  544.4 31.8 %collective-permute-start.51 = (bf16[256,2816]{1,0:T(8,128)(2,1)}, bf16[256,2816]{1,0:T(8,128)(2,1)}, u32[]{:S(2)}, u32[]{:S(2)}) collective-permute-start(bf16[256,2816]{1,0:T(8,128)(2,1)} %convolution_convert_fusion.3), channel_id=1, source_target_pairs={{0,4},{4,0},{8,12},{12,8},{16,20},{20,16},{24,28},{28,24},{1,5},{5... | collective-permute-start | bytes 4325384 | tf_op jit(solution)/shard_map/ppermute | solution.py:427
  556.2 52.0 %collective-permute-start.49 = (bf16[256,2816]{1,0:T(8,128)(2,1)}, bf16[256,2816]{1,0:T(8,128)(2,1)}, u32[]{:S(2)}, u32[]{:S(2)}) collective-permute-start(bf16[256,2816]{1,0:T(8,128)(2,1)} %fusion), channel_id=1, source_target_pairs={{0,8},{4,12},{8,16},{12,20},{16,24},{20,28},{24,0},{28,4},{1,9},{5... | collective-permute-start | bytes 4325384 | tf_op jit(solution)/shard_map/ppermute | solution.py:424
  557.1 51.2 %collective-permute-start.50 = (bf16[176,2048]{1,0:T(8,128)(2,1)}, bf16[176,2048]{1,0:T(8,128)(2,1)}, u32[]{:S(2)}, u32[]{:S(2)}) collective-permute-start(bf16[176,2048]{1,0:T(8,128)(2,1)} %add_convert_fusion.10), channel_id=1, source_target_pairs={{0,8},{4,12},{8,16},{12,20},{16,24},{20,28},{24,0},{28,4},{1,9},{5... | collective-permute-start | bytes 2162696 | tf_op jit(solution)/shard_map/ppermute | solution.py:424
  576.2 62.9 %collective-permute-start.52 = (bf16[256,2816]{1,0:T(8,128)(2,1)}, bf16[256,2816]{1,0:T(8,128)(2,1)}, u32[]{:S(2)}, u32[]{:S(2)}) collective-permute-start(bf16[256,2816]{1,0:T(8,128)(2,1)} %convolution_convert_fusion.2), channel_id=1, source_target_pairs={{0,4},{4,0},{8,12},{12,8},{16,20},{20,16},{24,28},{28,24},{1,5},{5... | collective-permute-start | bytes 4325384 | tf_op jit(solution)/shard_map/ppermute | solution.py:427
  582.2 57.0 %collective-permute-start.53 = (bf16[256,2816]{1,0:T(8,128)(2,1)}, bf16[256,2816]{1,0:T(8,128)(2,1)}, u32[]{:S(2)}, u32[]{:S(2)}) collective-permute-start(bf16[256,2816]{1,0:T(8,128)(2,1)} %fusion.1), channel_id=1, source_target_pairs={{0,24},{4,28},{8,0},{12,4},{16,8},{20,12},{24,16},{28,20},{1,25},{... | collective-permute-start | bytes 4325384 | tf_op jit(solution)/shard_map/ppermute | solution.py:424
  634.1 24.6 %collective-permute-start.57 = (bf16[128,2048]{1,0:T(8,128)(2,1)S(1)}, bf16[128,2048]{1,0:T(8,128)(2,1)S(1)}, u32[]{:S(2)}, u32[]{:S(2)}) collective-permute-start(bf16[128,2048]{1,0:T(8,128)(2,1)S(1)} %get-tuple-element.468), channel_id=1, source_target_pairs={{0,8},{4,12},{8,16},{12,20},{16,24},{20,28},{24,0},{28,4},{1,9},{5... | collective-permute-start | bytes 1572872 | tf_op jit(solution)/shard_map/ppermute | solution.py:424
  639.1 34.5 %collective-permute-start.56 = (bf16[256,2816]{1,0:T(8,128)(2,1)S(1)}, bf16[256,2816]{1,0:T(8,128)(2,1)S(1)}, u32[]{:S(2)}, u32[]{:S(2)}) collective-permute-start(bf16[256,2816]{1,0:T(8,128)(2,1)S(1)} %copy-done.41), channel_id=1, source_target_pairs={{0,4},{4,0},{8,12},{12,8},{16,20},{20,16},{24,28},{28,24},{1,5},{5... | collective-permute-start | bytes 4325384 | tf_op jit(solution)/shard_map/ppermute | solution.py:427
  653.2 44.4 %collective-permute-start.54 = (bf16[512,2048]{1,0:T(8,128)(2,1)S(1)}, bf16[512,2048]{1,0:T(8,128)(2,1)}, u32[]{:S(2)}, u32[]{:S(2)}) collective-permute-start(bf16[512,2048]{1,0:T(8,128)(2,1)S(1)} %convolution_convert_fusion.13), channel_id=1, source_target_pairs={{0,1},{1,0},{2,3},{3,2},{4,5},{5,4},{6,7},{7,6},{8,9},{9,8},{10,11... | collective-permute-start | bytes 6291464 | tf_op jit(solution)/shard_map/ppermute | solution.py:439
  657.2 40.4 %collective-permute-start.55 = (bf16[256,2176]{1,0:T(8,128)(2,1)S(1)}, bf16[256,2176]{1,0:T(8,128)(2,1)}, u32[]{:S(2)}, u32[]{:S(2)}) collective-permute-start(bf16[256,2176]{1,0:T(8,128)(2,1)S(1)} %convolution_convert_fusion.8), channel_id=1, source_target_pairs={{0,4},{4,0},{8,12},{12,8},{16,20},{20,16},{24,28},{28,24},{1,5},{5... | collective-permute-start | bytes 3342344 | tf_op jit(solution)/shard_map/ppermute | solution.py:427
  669.0 40.5 %collective-permute-start.62 = (bf16[128,2048]{1,0:T(8,128)(2,1)S(1)}, bf16[128,2048]{1,0:T(8,128)(2,1)}, u32[]{:S(2)}, u32[]{:S(2)}) collective-permute-start(bf16[128,2048]{1,0:T(8,128)(2,1)S(1)} %add_convert_fusion.17), channel_id=1, source_target_pairs={{0,8},{4,12},{8,16},{12,20},{16,24},{20,28},{24,0},{28,4},{1,9},{5... | collective-permute-start | bytes 1572872 | tf_op jit(solution)/shard_map/ppermute | solution.py:424
  677.4 48.4 %collective-permute-start.60 = (bf16[256,2816]{1,0:T(8,128)(2,1)S(1)}, bf16[256,2816]{1,0:T(8,128)(2,1)S(1)}, u32[]{:S(2)}, u32[]{:S(2)}) collective-permute-start(bf16[256,2816]{1,0:T(8,128)(2,1)S(1)} %add_convert_fusion.1), channel_id=1, source_target_pairs={{0,8},{4,12},{8,16},{12,20},{16,24},{20,28},{24,0},{28,4},{1,9},{5... | collective-permute-start | bytes 4325384 | tf_op jit(solution)/shard_map/ppermute | solution.py:424
  680.3 41.1 %collective-permute-start.61 = (bf16[256,2176]{1,0:T(8,128)(2,1)}, bf16[256,2176]{1,0:T(8,128)(2,1)}, u32[]{:S(2)}, u32[]{:S(2)}) collective-permute-start(bf16[256,2176]{1,0:T(8,128)(2,1)} %convolution_convert_fusion.7), channel_id=1, source_target_pairs={{0,4},{4,0},{8,12},{12,8},{16,20},{20,16},{24,28},{28,24},{1,5},{5... | collective-permute-start | bytes 3342344 | tf_op jit(solution)/shard_map/ppermute | solution.py:427
  708.1 24.8 %collective-permute-start.59 = (bf16[256,2048]{1,0:T(8,128)(2,1)}, bf16[256,2048]{1,0:T(8,128)(2,1)}, u32[]{:S(2)}, u32[]{:S(2)}) collective-permute-start(bf16[256,2048]{1,0:T(8,128)(2,1)} %add_convert_fusion.5), channel_id=1, source_target_pairs={{0,2},{1,3},{2,0},{3,1},{4,6},{5,7},{6,4},{7,5},{8,10},{9,11},{10,... | collective-permute-start | bytes 3145736 | tf_op jit(solution)/shard_map/ppermute | solution.py:442
  712.0 35.1 %collective-permute-start.63 = (bf16[256,2176]{1,0:T(8,128)(2,1)}, bf16[256,2176]{1,0:T(8,128)(2,1)S(1)}, u32[]{:S(2)}, u32[]{:S(2)}) collective-permute-start(bf16[256,2176]{1,0:T(8,128)(2,1)} %convolution_convert_fusion.6), channel_id=1, source_target_pairs={{0,4},{4,0},{8,12},{12,8},{16,20},{20,16},{24,28},{28,24},{1,5},{5... | collective-permute-start | bytes 3342344 | tf_op jit(solution)/shard_map/ppermute | solution.py:427
  725.1 29.8 %collective-permute-start.67 = (bf16[256,2176]{1,0:T(8,128)(2,1)}, bf16[256,2176]{1,0:T(8,128)(2,1)}, u32[]{:S(2)}, u32[]{:S(2)}) collective-permute-start(bf16[256,2176]{1,0:T(8,128)(2,1)} %add_convert_fusion.4), channel_id=1, source_target_pairs={{0,8},{4,12},{8,16},{12,20},{16,24},{20,28},{24,0},{28,4},{1,9},{5... | collective-permute-start | bytes 3342344 | tf_op jit(solution)/shard_map/ppermute | solution.py:424
  729.5 48.3 %collective-permute-start.66 = (bf16[256,2816]{1,0:T(8,128)(2,1)S(1)}, bf16[256,2816]{1,0:T(8,128)(2,1)}, u32[]{:S(2)}, u32[]{:S(2)}) collective-permute-start(bf16[256,2816]{1,0:T(8,128)(2,1)S(1)} %add_convert_fusion.refs_0_), channel_id=1, source_target_pairs={{0,2},{1,3},{2,0},{3,1},{4,6},{5,7},{6,4},{7,5},{8,10},{9,11},{10,... | collective-permute-start | bytes 4325384 | tf_op jit(solution)/shard_map/ppermute | solution.py:442
  743.0 34.7 %collective-permute-start.71 = (bf16[176,2048]{1,0:T(8,128)(2,1)S(1)}, bf16[176,2048]{1,0:T(8,128)(2,1)S(1)}, u32[]{:S(2)}, u32[]{:S(2)}) collective-permute-start(bf16[176,2048]{1,0:T(8,128)(2,1)S(1)} %add_convert_fusion.9.refs_0_), channel_id=1, source_target_pairs={{0,2},{1,3},{2,0},{3,1},{4,6},{5,7},{6,4},{7,5},{8,10},{9,11},{10,... | collective-permute-start | bytes 2162696 | tf_op jit(solution)/shard_map/ppermute | solution.py:442
  744.6 42.8 %collective-permute-start.64 = (bf16[256,2176]{1,0:T(8,128)(2,1)}, bf16[256,2176]{1,0:T(8,128)(2,1)}, u32[]{:S(2)}, u32[]{:S(2)}) collective-permute-start(bf16[256,2176]{1,0:T(8,128)(2,1)} %convolution_convert_fusion.5), channel_id=1, source_target_pairs={{0,4},{4,0},{8,12},{12,8},{16,20},{20,16},{24,28},{28,24},{1,5},{5... | collective-permute-start | bytes 3342344 | tf_op jit(solution)/shard_map/ppermute | solution.py:427
  749.8 28.9 %collective-permute-start.69 = (bf16[256,2176]{1,0:T(8,128)(2,1)S(1)}, bf16[256,2176]{1,0:T(8,128)(2,1)S(1)}, u32[]{:S(2)}, u32[]{:S(2)}) collective-permute-start(bf16[256,2176]{1,0:T(8,128)(2,1)S(1)} %add_convert_fusion.3), channel_id=1, source_target_pairs={{0,24},{4,28},{8,0},{12,4},{16,8},{20,12},{24,16},{28,20},{1,25},{... | collective-permute-start | bytes 3342344 | tf_op jit(solution)/shard_map/ppermute | solution.py:424
  758.7 40.9 %collective-permute-start.73 = (bf16[256,2176]{1,0:T(8,128)(2,1)}, bf16[256,2176]{1,0:T(8,128)(2,1)}, u32[]{:S(2)}, u32[]{:S(2)}) collective-permute-start(bf16[256,2176]{1,0:T(8,128)(2,1)} %add_convert_fusion.2), channel_id=1, source_target_pairs={{0,8},{4,12},{8,16},{12,20},{16,24},{20,28},{24,0},{28,4},{1,9},{5... | collective-permute-start | bytes 3342344 | tf_op jit(solution)/shard_map/ppermute | solution.py:424
  781.5 30.0 %collective-permute-start.77 = (bf16[256,2816]{1,0:T(8,128)(2,1)S(1)}, bf16[256,2816]{1,0:T(8,128)(2,1)}, u32[]{:S(2)}, u32[]{:S(2)}) collective-permute-start(bf16[256,2816]{1,0:T(8,128)(2,1)S(1)} %add_convert_fusion.refs_0_), channel_id=1, source_target_pairs={{0,1},{1,0},{2,3},{3,2},{4,5},{5,4},{6,7},{7,6},{8,9},{9,8},{10,11... | collective-permute-start | bytes 4325384 | tf_op jit(solution)/shard_map/ppermute | solution.py:439
  787.3 18.7 %collective-permute-start.75 = (bf16[128,2048]{1,0:T(8,128)(2,1)S(1)}, bf16[128,2048]{1,0:T(8,128)(2,1)S(1)}, u32[]{:S(2)}, u32[]{:S(2)}) collective-permute-start(bf16[128,2048]{1,0:T(8,128)(2,1)S(1)} %add_convert_fusion.16), channel_id=1, source_target_pairs={{2,6},{3,7},{4,0},{5,1},{10,14},{11,15},{12,8},{13,9},{18,22},{19,... | collective-permute-start | bytes 1572872 | tf_op jit(solution)/shard_map/ppermute | solution.py:436
  809.6 26.0 %collective-permute-start.83 = (bf16[256,1152]{1,0:T(8,128)(2,1)}, bf16[256,1152]{1,0:T(8,128)(2,1)}, u32[]{:S(2)}, u32[]{:S(2)}) collective-permute-start(bf16[256,1152]{1,0:T(8,128)(2,1)} %add_convert_fusion.13.refs_1_), channel_id=1, source_target_pairs={{0,2},{1,3},{2,0},{3,1},{4,6},{5,7},{6,4},{7,5},{8,10},{9,11},{10,... | collective-permute-start | bytes 1769480 | tf_op jit(solution)/shard_map/ppermute | solution.py:442
  811.5 27.9 %collective-permute-start.79 = (bf16[256,1024]{1,0:T(8,128)(2,1)}, bf16[256,1024]{1,0:T(8,128)(2,1)}, u32[]{:S(2)}, u32[]{:S(2)}) collective-permute-start(bf16[256,1024]{1,0:T(8,128)(2,1)} %add_convert_fusion.15.refs_0_), channel_id=1, source_target_pairs={{0,1},{1,0},{2,3},{3,2},{4,5},{5,4},{6,7},{7,6},{8,9},{9,8},{10,11... | collective-permute-start | bytes 1572872 | tf_op jit(solution)/shard_map/ppermute | solution.py:439
  821.8 22.3 %collective-permute-start.81 = (bf16[256,1024]{1,0:T(8,128)(2,1)}, bf16[256,1024]{1,0:T(8,128)(2,1)}, u32[]{:S(2)}, u32[]{:S(2)}) collective-permute-start(bf16[256,1024]{1,0:T(8,128)(2,1)} %collective-permute-done.80.refs_2_), channel_id=1, source_target_pairs={{0,1},{1,0},{2,3},{3,2},{4,5},{5,4},{6,7},{7,6},{8,9},{9,8},{10,11... | collective-permute-start | bytes 1572872 | tf_op jit(solution)/shard_map/ppermute | solution.py:439
  822.9 38.5 %collective-permute-start.87 = (bf16[256,2048]{1,0:T(8,128)(2,1)}, bf16[256,2048]{1,0:T(8,128)(2,1)S(1)}, u32[]{:S(2)}, u32[]{:S(2)}) collective-permute-start(bf16[256,2048]{1,0:T(8,128)(2,1)} %pad_maximum_fusion.5), channel_id=1, source_target_pairs={{0,2},{1,3},{2,0},{3,1},{4,6},{5,7},{6,4},{7,5},{8,10},{9,11},{10,... | collective-permute-start | bytes 3145736 | tf_op jit(solution)/shard_map/ppermute | solution.py:442
  (120 other events, 1715.0 us)
